TPU v7x, 32 devices: a whole 2x2x4 slice. The times are simulated.
32 devices in a mesh: dp: 2 (over x), seq: 16 (over z, y, core).
Axes of the slice: x: 2, y: 2, z: 4, core: 2. Of those that a mesh axis runs over, the one named last changes fastest.
Arguments:
- queries: bfloat16 [2, 2048, 4096], P('dp', 'seq'), may hold values from -5 to 5
- rotated_key_rows: bfloat16 [2, 2048, 512], P('dp', 'seq'), may hold values from -5 to 5
- hidden_states: bfloat16 [2, 2048, 8192], P('dp', 'seq'), may hold values from -6 to 6
- block_order: int32 [32], replicated, may hold values from 0 to 31, each once
- first_weight: bfloat16 [8192, 512], replicated, may hold values from -0.0625 to 0.0625
- first_bias: float32 [512], replicated, may hold values from -3 to 3
- output_weight: bfloat16 [4, 512], replicated, may hold values from -0.25 to 0.25
- output_bias: float32 [4], replicated, may hold values from -1 to 1
Outputs:
- token_attention_mass: float32 [2, 4, 2048], P('dp', None, 'seq')
- loss_value: float32 [], replicated
- step_first: float32 [8192, 512], P('seq')
- output_weight_step: float32 [4, 512], replicated
- step_bias: float32 [512], replicated
- grad_bias: float32 [4], replicated
All inputs are finite; a program needn't handle non-finite values.
Results may differ from a plain program's by a relative error of at most 0.0023.
Values may be sent and summed in bfloat16 or wider, within the bound.
No kernel may reach another device: no remote copies, remote signals or barrier semaphores. Data moves between devices by JAX's collectives and lax.ppermute only.
A program may use at most 64 MiB of HBM per device.

v0:
```python
import math

import jax
import jax.numpy as jnp
from jax import lax
from jax.sharding import PartitionSpec as P

D = 8192
KEY_VALUE_HEADS = 4
HEAD_SIZE = 128
RETAIN_HIDDEN = 512
BLK = 64
QUERY_GROUP_SIZE = 8


def key_places(block_order, offset, amount):
    row_ids = offset + lax.iota(jnp.int32, amount)
    block_ids = row_ids // BLK
    block_table = lax.iota(jnp.int32, block_order.shape[0])
    anchor = jnp.sum(
        jnp.where(block_ids[:, None] == block_table[None, :], block_order[None, :], 0), axis=1
    )
    return anchor * BLK + row_ids % BLK


def raw_scores(head_queries, mass_portion):
    head_keys = mass_portion.reshape(mass_portion.shape[0], KEY_VALUE_HEADS, HEAD_SIZE)
    return jnp.einsum(
        "tkgd,nkd->kgtn", head_queries, head_keys, preferred_element_type=jnp.float32
    ) * HEAD_SIZE ** (-0.5)


def blockwise(mass_portion, offset, update, carried):
    rows_here = mass_portion.shape[0]
    inner = math.gcd(rows_here, 512)

    def visit_block(step_index, running):
        local_start = step_index * inner
        sub_rows = lax.dynamic_slice_in_dim(mass_portion, local_start, inner, 0)
        return update(running, sub_rows, offset + local_start)

    return lax.fori_loop(0, rows_here // inner, visit_block, carried)


def normalizer_step(running, mass_portion, key_start, head_queries, query_pos, block_order):
    highest, summed = running
    key_pos = key_places(block_order, key_start, mass_portion.shape[0])
    scores = raw_scores(head_queries, mass_portion)
    visible = query_pos[:, None] >= key_pos[None, :]
    masked = jnp.where(visible, scores, -1e30)
    raised = jnp.maximum(highest, jnp.max(masked, axis=-1))
    exponents = jnp.where(visible, jnp.exp(masked - raised[..., None]), 0.0)
    return (raised, summed * jnp.exp(highest - raised) + jnp.sum(exponents, axis=-1))


def mass_step(mass_portion, key_start, head_queries, query_pos, log_total, block_order):
    amount = mass_portion.shape[0]
    key_pos = key_places(block_order, key_start, amount)
    scores = raw_scores(head_queries, mass_portion)
    visible = query_pos[:, None] >= key_pos[None, :]
    masked = jnp.where(visible, scores, -1e30)
    weights = jnp.where(visible, jnp.exp(masked - log_total[..., None]), 0.0)
    return jnp.sum(weights, axis=(1, 2)) / QUERY_GROUP_SIZE


def normalized_scores(value_rows, square_sum, entries):
    return value_rows / jnp.sqrt(square_sum / entries + 1e-06)


def per_device(
    queries,
    rotated_key_rows,
    hidden_states,
    block_order,
    first_weight,
    first_bias,
    output_weight,
    output_bias,
):
    local_row_slice = queries.shape[1]
    total_length = local_row_slice * lax.axis_size("seq")
    head_queries = queries.reshape(local_row_slice, KEY_VALUE_HEADS, QUERY_GROUP_SIZE, HEAD_SIZE)
    local_key_rows = rotated_key_rows.reshape(local_row_slice, KEY_VALUE_HEADS * HEAD_SIZE)
    query_pos = key_places(block_order, lax.axis_index("seq") * local_row_slice, local_row_slice)
    start_state = (
        jnp.full((KEY_VALUE_HEADS, QUERY_GROUP_SIZE, local_row_slice), -1e30, jnp.float32),
        jnp.zeros((KEY_VALUE_HEADS, QUERY_GROUP_SIZE, local_row_slice), jnp.float32),
    )

    def norm_update(running, sub_rows, key_start):
        return normalizer_step(running, sub_rows, key_start, head_queries, query_pos, block_order)

    empty_mass = jnp.zeros((KEY_VALUE_HEADS, total_length), jnp.float32)
    keys_whole = lax.all_gather(local_key_rows, "seq", axis=0, tiled=True)
    highest, summed = blockwise(keys_whole, 0, norm_update, start_state)
    log_total = highest + jnp.log(summed)

    def add_kept(collected, sub_rows, key_start):
        term = mass_step(sub_rows, key_start, head_queries, query_pos, log_total, block_order)
        return lax.dynamic_update_slice_in_dim(collected, term, key_start, 1)

    column_mass = blockwise(keys_whole, 0, add_kept, empty_mass)
    key_attention_mass = lax.psum_scatter(column_mass, "seq", scatter_dimension=1, tiled=True)
    tokens_in = hidden_states.reshape(local_row_slice, hidden_states.shape[2])
    pre_act = jnp.dot(tokens_in, first_weight, preferred_element_type=jnp.float32) + first_bias
    hidden = jax.nn.silu(pre_act).astype(jnp.bfloat16)
    predicted_scores = (
        lax.dot_general(
            output_weight, hidden, (((1,), (1,)), ((), ())), preferred_element_type=jnp.float32
        )
        + output_bias[:, None]
    )
    score_residue = predicted_scores - jnp.log(1.0 + key_attention_mass)
    loss_part = 0.5 * jnp.sum(score_residue * score_residue) / total_length
    out_grad = score_residue / total_length
    bias_part = jnp.sum(out_grad, axis=1)
    second_part = jnp.dot(out_grad, hidden.astype(jnp.float32), precision=lax.Precision.HIGHEST)
    back_grad = jnp.dot(
        out_grad.T, output_weight.astype(jnp.float32), precision=lax.Precision.HIGHEST
    )
    gate_value = jax.nn.sigmoid(pre_act)
    slope_grad = back_grad * gate_value * (1.0 + pre_act * (1.0 - gate_value))
    first_bias_part = jnp.sum(slope_grad, axis=0)
    slope_half = slope_grad.astype(jnp.bfloat16)
    columns_all = lax.all_to_all(tokens_in, "seq", split_axis=1, concat_axis=0, tiled=True)
    slope_all = lax.all_gather(slope_half, "seq", axis=0, tiled=True)
    first_shard = lax.dot_general(
        columns_all, slope_all, (((0,), (0,)), ((), ())), preferred_element_type=jnp.float32
    )
    output_total, first_bias_total, bias_total, loss_total = lax.psum(
        (second_part, first_bias_part, bias_part, loss_part), ("dp", "seq")
    )
    first_grad = lax.psum(first_shard, "dp")
    first_square = lax.psum(jnp.sum(first_grad * first_grad), "seq")
    step_first = normalized_scores(first_grad, first_square, D * RETAIN_HIDDEN)
    output_weight_step = normalized_scores(
        output_total, jnp.sum(output_total * output_total), RETAIN_HIDDEN * KEY_VALUE_HEADS
    )
    step_bias = normalized_scores(
        first_bias_total, jnp.sum(first_bias_total * first_bias_total), RETAIN_HIDDEN
    )
    return (
        key_attention_mass.reshape(1, KEY_VALUE_HEADS, local_row_slice),
        loss_total,
        step_first,
        output_weight_step,
        step_bias,
        bias_total,
    )


def solution(mesh):
    in_specs = (
        P("dp", "seq", None),
        P("dp", "seq", None),
        P("dp", "seq", None),
        P(),
        P(),
        P(),
        P(),
        P(),
    )
    out_specs = (P("dp", None, "seq"), P(), P("seq", None), P(), P(), P())
    return jax.shard_map(
        per_device, mesh=mesh, in_specs=in_specs, out_specs=out_specs, check_vma=False
    )
```

profile of v0, /device:TPU:0, one launch (start us, length us, event | category | flops | bytes accessed | tf_op | source)
XLA Modules:
  0.0 330.7 jit_solution(4713822610207357693)
XLA Ops:
  7.2 1.7 copy.42
  9.0 4.1 %copy.46 = bf16[1,128,8192]{1,2,0:T(8,128)(2,1)} copy(bf16[1,128,8192]{2,1,0:T(8,128)(2,1)} %param.14) | data formatting | bytes 4194304 | tf_op args[2]
  13.1 7.4 %all-to-all-start = ((bf16[128,16,512]{0,2,1:T(8,128)(2,1)}), bf16[128,16,512]{0,2,1:T(8,128)(2,1)}, u32[]{:S(2)}, u32[]{:S(2)}) async-start(bf16[128,16,512]{0,2,1:T(8,128)(2,1)} %bitcast.8), calls=%async_computation | async-start | bytes 4194304 | tf_op jit(solution)/shard_map/all_to_all | solution.py:125
  20.6 0.7 copy.43
  21.3 0.7 copy.45
  22.1 58.7 %all-gather.6.cloned.1.call-done = bf16[1,2048,512]{1,2,0:T(8,128)(2,1)} async-done(((bf16[1,128,512]{1,2,0:T(8,128)(2,1)}), bf16[1,2048,512]{1,2,0:T(8,128)(2,1)}) %all-gather.6.cloned.1.call-update) | async-done | bytes 2097168 | tf_op jit(solution)/shard_map/all_gather | solution.py:94
  80.8 42.5 %while.34 = (s32[]{:T(128)}, f32[4,8,128]{2,1,0:T(8,128)S(1)}, f32[4,8,128]{2,1,0:T(8,128)S(1)}, s32[128]{0:T(128)S(1)}, s32[32]{0:T(128)S(1)}, /*index=5*/bf16[...) while((s32[]{:T(128)}, f32[4,8,128]{2,1,0:T(8,128)S(1)}, ...), condition=%wide.region_5.6_spmd.clone, body=%wide.region_1.5_spmd.clone.sunk | while | flops 553798144 | bytes 19821360 | solution.py:42
  80.8 1.1 constant_dynamic-slice_fusion.5
  82.0 0.1 broadcast_compare_fusion.5
  82.1 4.7 %fusion.58 = (f32[4,8,128]{2,1,0:T(8,128)S(1)}, f32[4,512,128,8]{2,1,3,0:T(8,128)}) fusion(pred[128,512]{0,1:T(8,128)(4,1)S(1)} %broadcast_compare_fusion.5, bf16[512,4,128,1]{0,2,3,1:T(8,128)(2,1)S(1)} %bitcast.76, bf16[128,4,8,128]{3,0,2,1:T(8,128)(2,1)S(1)} %get-tuple-element.638), kind=kOutput, calls=%fused_computation.23.clone.1 | convolution fusion | flops 543158272 | bytes 10043392 | tf_op jit(solution)/shard_map/while/body/eval_jaxpr/tkgd,nkd->kgtn/dot_general | solution.py:28
  86.8 4.5 %select_reduce_fusion.9 = f32[4,8,128]{2,1,0:T(8,128)S(1)} fusion(f32[4,512,128,8]{2,1,3,0:T(8,128)} %get-tuple-element.609, f32[4,8,128]{2,1,0:T(8,128)S(1)} %select_maximum_fusion.2, pred[128,512]{0,1:T(8,128)(4,1)S(1)} %broadcast_compare_fusion.5), kind=kLoop, calls=%fused_computation.22.clone.1 | loop fusion | flops 10481664 | bytes 8486912 | tf_op jit(solution)/shard_map/while/body/eval_jaxpr/reduce_sum | solution.py:53
  91.4 1.1 constant_dynamic-slice_fusion.5
  92.8 4.7 %fusion.58 = (f32[4,8,128]{2,1,0:T(8,128)S(1)}, f32[4,512,128,8]{2,1,3,0:T(8,128)}) fusion(pred[128,512]{0,1:T(8,128)(4,1)S(1)} %broadcast_compare_fusion.5, bf16[512,4,128,1]{0,2,3,1:T(8,128)(2,1)S(1)} %bitcast.76, bf16[128,4,8,128]{3,0,2,1:T(8,128)(2,1)S(1)} %get-tuple-element.638), kind=kOutput, calls=%fused_computation.23.clone.1 | convolution fusion | flops 543158272 | bytes 10043392 | tf_op jit(solution)/shard_map/while/body/eval_jaxpr/tkgd,nkd->kgtn/dot_general | solution.py:28
  97.4 4.5 %select_reduce_fusion.9 = f32[4,8,128]{2,1,0:T(8,128)S(1)} fusion(f32[4,512,128,8]{2,1,3,0:T(8,128)} %get-tuple-element.609, f32[4,8,128]{2,1,0:T(8,128)S(1)} %select_maximum_fusion.2, pred[128,512]{0,1:T(8,128)(4,1)S(1)} %broadcast_compare_fusion.5), kind=kLoop, calls=%fused_computation.22.clone.1 | loop fusion | flops 10481664 | bytes 8486912 | tf_op jit(solution)/shard_map/while/body/eval_jaxpr/reduce_sum | solution.py:53
  102.0 1.1 constant_dynamic-slice_fusion.5
  103.4 4.7 %fusion.58 = (f32[4,8,128]{2,1,0:T(8,128)S(1)}, f32[4,512,128,8]{2,1,3,0:T(8,128)}) fusion(pred[128,512]{0,1:T(8,128)(4,1)S(1)} %broadcast_compare_fusion.5, bf16[512,4,128,1]{0,2,3,1:T(8,128)(2,1)S(1)} %bitcast.76, bf16[128,4,8,128]{3,0,2,1:T(8,128)(2,1)S(1)} %get-tuple-element.638), kind=kOutput, calls=%fused_computation.23.clone.1 | convolution fusion | flops 543158272 | bytes 10043392 | tf_op jit(solution)/shard_map/while/body/eval_jaxpr/tkgd,nkd->kgtn/dot_general | solution.py:28
  108.1 4.5 %select_reduce_fusion.9 = f32[4,8,128]{2,1,0:T(8,128)S(1)} fusion(f32[4,512,128,8]{2,1,3,0:T(8,128)} %get-tuple-element.609, f32[4,8,128]{2,1,0:T(8,128)S(1)} %select_maximum_fusion.2, pred[128,512]{0,1:T(8,128)(4,1)S(1)} %broadcast_compare_fusion.5), kind=kLoop, calls=%fused_computation.22.clone.1 | loop fusion | flops 10481664 | bytes 8486912 | tf_op jit(solution)/shard_map/while/body/eval_jaxpr/reduce_sum | solution.py:53
  112.7 1.1 constant_dynamic-slice_fusion.5
  114.0 4.7 %fusion.58 = (f32[4,8,128]{2,1,0:T(8,128)S(1)}, f32[4,512,128,8]{2,1,3,0:T(8,128)}) fusion(pred[128,512]{0,1:T(8,128)(4,1)S(1)} %broadcast_compare_fusion.5, bf16[512,4,128,1]{0,2,3,1:T(8,128)(2,1)S(1)} %bitcast.76, bf16[128,4,8,128]{3,0,2,1:T(8,128)(2,1)S(1)} %get-tuple-element.638), kind=kOutput, calls=%fused_computation.23.clone.1 | convolution fusion | flops 543158272 | bytes 10043392 | tf_op jit(solution)/shard_map/while/body/eval_jaxpr/tkgd,nkd->kgtn/dot_general | solution.py:28
  118.7 4.5 %select_reduce_fusion.9 = f32[4,8,128]{2,1,0:T(8,128)S(1)} fusion(f32[4,512,128,8]{2,1,3,0:T(8,128)} %get-tuple-element.609, f32[4,8,128]{2,1,0:T(8,128)S(1)} %select_maximum_fusion.2, pred[128,512]{0,1:T(8,128)(4,1)S(1)} %broadcast_compare_fusion.5), kind=kLoop, calls=%fused_computation.22.clone.1 | loop fusion | flops 10481664 | bytes 8486912 | tf_op jit(solution)/shard_map/while/body/eval_jaxpr/reduce_sum | solution.py:53
  123.4 16.1 %while.33 = (s32[]{:T(128)}, f32[4,2048]{1,0:T(4,128)S(1)}, s32[128]{0:T(128)S(1)}, s32[32]{0:T(128)S(1)}, bf16[2048,512]{0,1:T(8,128)(2,1)}, /*index=5*/bf16[12...) while((s32[]{:T(128)}, f32[4,2048]{1,0:T(4,128)S(1)}, ...), condition=%wide.region_9.10_spmd, body=%wide.region_6.9_spmd.sunk | while | flops 547486208 | bytes 2806571 | solution.py:42
  123.4 1.2 constant_dynamic-slice_fusion.4
  124.8 2.6 fusion.54
  127.5 1.1 constant_dynamic-slice_fusion.4
  128.8 2.6 fusion.54
  131.5 1.1 constant_dynamic-slice_fusion.4
  132.8 2.6 fusion.54
  135.5 1.1 constant_dynamic-slice_fusion.4
  136.8 2.6 fusion.54
  139.5 1.3 copy.55
  140.9 4.9 %multiply_convert_fusion = (bf16[128,512]{1,0:T(8,128)(2,1)S(1)}, f32[128,512]{1,0:T(8,128)S(1)}) fusion(f32[512]{0:T(512)S(1)} %copy-done.4, bf16[8192,512]{1,0:T(8,128)(2,1)} %param.16, bf16[1,128,8192]{2,1,0:T(8,128)(2,1)S(1)} %copy-done.1), kind=kOutput, calls=%fused_computation.53 | convolution fusion | flops 1074135040 | bytes 10881024 | tf_op jit(solution)/shard_map/dot_general | solution.py:105
  145.8 49.9 %reduce-scatter.4.cloned.1.call-done = f32[128,4]{1,0:T(8,128)} async-done(((f32[2048,4]{1,0:T(8,128)}), f32[128,4]{1,0:T(8,128)}) %reduce-scatter.4.cloned.1.call-update) | async-done | bytes 2064
  195.7 0.9 copy.56
  196.6 0.8 multiply_reduce_fusion.4
  197.4 1.0 fusion.30
  198.5 2.9 copy.47
  201.3 37.7 %all-gather.4.cloned.1.call-done = bf16[2048,512]{1,0:T(8,128)(2,1)} async-done(((bf16[128,512]{1,0:T(8,128)(2,1)}), bf16[2048,512]{1,0:T(8,128)(2,1)}) %all-gather.4.cloned.1.call-update) | async-done | bytes 2097168 | tf_op jit(solution)/shard_map/all_gather | solution.py:126
  239.1 3.8 %convolution_bitcast_fusion = f32[512,512]{0,1:T(8,128)} fusion(bf16[2048,512]{1,0:T(8,128)(2,1)} %all-gather.4.cloned.1.call-done, bf16[2048,512]{1,0:T(8,128)(2,1)S(1)} %bitcast.81), kind=kOutput, calls=%fused_computation.44 | convolution fusion | flops 1073741824 | bytes 5242880 | tf_op jit(solution)/shard_map/dot_general | solution.py:127
  243.6 0.2 fusion.22
  243.7 38.8 %all-reduce = (f32[]{:T(128)}, f32[4,512]{1,0:T(4,128)S(1)}, f32[512]{0:T(512)S(1)}, f32[4]{0:T(128)}) all-reduce(f32[]{:T(128)S(6)} %div.89, f32[4,512]{1,0:T(4,128)S(1)} %fusion.22, f32[512]{0:T(512)S(1)} %get-tuple-element.515, f32[4]{0:T(128)S(1)} %get-tuple-element.478), channel_id=1, replica_groups=mesh['dp'=2,'seq'=16] {'dp','seq'}, use_global_device_ids=true, to_apply=%region_12.13 | all-reduce | flops 2565 | bytes 20520 | tf_op jit(solution)/shard_map/psum | solution.py:130
  282.5 0.6 multiply_reduce_fusion.1
  283.8 0.6 multiply_reduce_fusion.2
  285.1 0.6 broadcast_divide_fusion.1
  285.7 2.1 multiply_reduce_fusion
  287.8 0.6 broadcast_divide_fusion.2
  288.4 32.4 %psum.44 = f32[]{:T(128)} all-reduce(f32[]{:T(128)} %multiply_reduce_fusion), channel_id=1, replica_groups=mesh['dp'=2,'seq'=16] {'seq'}, use_global_device_ids=true, to_apply=%region_15.16 | all-reduce | flops 1 | bytes 8 | tf_op jit(solution)/shard_map/psum | solution.py:134
  321.6 1.3 broadcast_divide_fusion
  322.9 1.3 copy.48
  (78 shorter events, 2.3 us)
Async XLA Ops:
  7.2 189.5 %copy-start = (bf16[4,512]{1,0:T(4,128)(2,1)S(1)}, bf16[4,512]{1,0:T(4,128)(2,1)}, u32[]{:S(2)}) copy-start(bf16[4,512]{1,0:T(4,128)(2,1)} %param.18) | copy-start | bytes 12292
  7.2 13.4 %copy-start.2 = (bf16[1,128,4096]{2,1,0:T(8,128)(2,1)S(1)}, bf16[1,128,4096]{2,1,0:T(8,128)(2,1)}, u32[]{:S(2)}) copy-start(bf16[1,128,4096]{2,1,0:T(8,128)(2,1)} %param.12) | copy-start | bytes 3145732
  7.2 14.8 %copy-start.3 = (s32[32]{0:T(128)S(1)}, s32[32]{0:T(128)}, u32[]{:S(2)}) copy-start(s32[32]{0:T(128)} %param.15) | copy-start | bytes 388
  7.2 73.6 %all-gather.6.cloned.1.call-start = ((), (), s32[]{:S(2)}) async-start(), calls=%async_computation.4 | async-start | bytes 2228224 | tf_op jit(solution)/shard_map/all_gather | solution.py:94
  13.1 185.4 %all-to-all-start = ((bf16[128,16,512]{0,2,1:T(8,128)(2,1)}), bf16[128,16,512]{0,2,1:T(8,128)(2,1)}, u32[]{:S(2)}, u32[]{:S(2)}) async-start(bf16[128,16,512]{0,2,1:T(8,128)(2,1)} %bitcast.8), calls=%async_computation | async-start | bytes 4194304 | tf_op jit(solution)/shard_map/all_to_all | solution.py:125
  20.5 175.2 %reduce-scatter.4.cloned.1.call-start = ((), (), s32[]{:S(2)}) async-start(), calls=%async_computation.5 | async-start | bytes 1114112
  123.3 17.6 %copy-start.1 = (bf16[1,128,8192]{2,1,0:T(8,128)(2,1)S(1)}, bf16[1,128,8192]{2,1,0:T(8,128)(2,1)}, u32[]{:S(2)}) copy-start(bf16[1,128,8192]{2,1,0:T(8,128)(2,1)} %param.14) | copy-start | bytes 6291460
  123.3 17.6 %copy-start.4 = (f32[512]{0:T(512)S(1)}, f32[512]{0:T(512)}, u32[]{:S(2)}) copy-start(f32[512]{0:T(512)} %param.17) | copy-start | bytes 6148
  140.8 55.8 %copy-start.6 = (f32[4]{0:T(128)S(1)}, f32[4]{0:T(128)}, u32[]{:S(2)}) copy-start(f32[4]{0:T(128)} %param.19) | copy-start | bytes 52
  140.9 98.2 %all-gather.4.cloned.1.call-start = ((), (), s32[]{:S(2)}) async-start(), calls=%async_computation.2 | async-start | bytes 2228224 | tf_op jit(solution)/shard_map/all_gather | solution.py:126
  196.6 126.3 %copy-start.5 = (f32[4,128]{1,0:T(4,128)}, f32[4,128]{1,0:T(4,128)S(1)}, u32[]{:S(2)}) copy-start(f32[4,128]{1,0:T(4,128)S(1)} %copy.56) | copy-start | bytes 6148
  198.4 87.3 %all-reduce.3.cloned.1.call-start = ((), (), s32[]{:S(2)}) async-start(), calls=%async_computation.3 | async-start | bytes 2097152 | tf_op jit(solution)/shard_map/psum | solution.py:133
Sparse Core Ops, SparseCore 0:
  10.8 69.9 all-gather.5
  141.0 54.7 reduce-scatter.3
  198.7 40.3 all-gather.3
  243.1 39.8 all-reduce.2
where the time goes:
time: 332 us; the launch traced here: 331 us
  waiting for transfers between devices  146 us (44%)
  blocking collectives  71.2 us (21%)
  matrix products  39.8 us (12%)
  other arithmetic  26.1 us (8%)
  local copies, waits for them, and re-layouts  22.4 us (7%)
  between operations  16.7 us (5%)
  starting transfers between devices  7.6 us (2%)
    all_gather x1, waiting for transfers between devices, per_device(): keys_whole = lax.all_gather(local_key_rows, 'seq', axis=0, tiled=True)  58.7 us
    unnamed x5, waiting for transfers between devices  50 us
    psum x1, blocking collectives, per_device(): lax.psum((second_part, first_bias_part, bias_part, loss_part), ('dp', 'se...  38.8 us
    all_gather x1, waiting for transfers between devices, per_device(): slope_all = lax.all_gather(slope_half, 'seq', axis=0, tiled=True)  37.7 us
    psum x1, blocking collectives, per_device(): first_square = lax.psum(jnp.sum(first_grad * first_grad), 'seq')  32.4 us
    dot_general x8, matrix products, raw_scores(): jnp.einsum('tkgd,nkd->kgtn', head_queries, head_keys, preferred_element_t...  29.2 us
    reduce_sum x4, other arithmetic, normalizer_step(): jnp.sum(exponents, axis=-1)  18.2 us
    unnamed x20, local copies, waits for them, and re-layouts  10.1 us
  transfers between devices with their start and end apart: 5, of which 3 were waited for; matrix products, arithmetic and copies ran while one was open for 23% of the time, Pallas kernels for 0%

commit v1 on v0

v1 whole, which is shorter than its diff:
```python
import functools

import jax
import jax.numpy as jnp
from jax import lax
from jax.experimental import pallas as pl
from jax.experimental.pallas import tpu as pltpu
from jax.sharding import PartitionSpec as P

KEY_VALUE_HEADS = 4
HEAD_SIZE = 128
BLK = 64
QUERY_GROUP_SIZE = 8
LOG2_E = 1.4426950408889634
VMEM_LIMIT = 60 * 1024 * 1024
VMEM = pl.BlockSpec(memory_space=pltpu.VMEM)
SMEM = pl.BlockSpec(memory_space=pltpu.SMEM)


def swap(value, axis, mask):
    return lax.ppermute(value, axis, [(i, i ^ mask) for i in range(lax.axis_size(axis))])


def gather_xor(value, axis):
    amount = lax.axis_size(axis)
    top = amount // 4
    slots = {0: value}
    for step in (1, 2, 3):
        slots[step * top] = swap(value, axis, step * top)
    for mask in range(2, top, 2):
        for step in range(4):
            slots[step * top + mask] = swap(slots[step * top], axis, mask)
    for mask in range(0, amount, 2):
        slots[mask + 1] = swap(slots[mask], axis, 1)
    return [slots[k] for k in range(amount)]


def split3(value):
    high = value.astype(jnp.bfloat16)
    rest = value - high.astype(jnp.float32)
    middle = rest.astype(jnp.bfloat16)
    low = (rest - middle.astype(jnp.float32)).astype(jnp.bfloat16)
    return high, middle, low


def attention_kernel(slots, place_ref, order_ref, query_ref, *refs):
    key_refs, mass_ref = refs[:slots], refs[slots]
    keys, bias, scores, mixed = refs[slots + 1 :]
    rows = key_refs[0].shape[0]
    total = rows * slots
    pairs = query_ref.shape[0]
    lanes = query_ref.shape[1]
    per_head = pairs // KEY_VALUE_HEADS
    chunk = 256
    blocks = rows // BLK
    me = place_ref[0]
    scale = HEAD_SIZE ** (-0.5) * LOG2_E

    def pos_of(owner, index):
        at = jnp.zeros(index.shape, jnp.int32)
        for b in range(blocks):
            at = jnp.where(index // BLK == b, order_ref[owner * blocks + b], at)
        return at * BLK + index % BLK

    query_pos = pos_of(me, lax.broadcasted_iota(jnp.int32, (rows, rows), 1))
    key_index = lax.broadcasted_iota(jnp.int32, (rows, rows), 0)
    for k in range(slots):
        at = pl.ds(k * rows, rows)
        for head in range(KEY_VALUE_HEADS):
            keys[head, at, :] = key_refs[k][:, head * HEAD_SIZE : (head + 1) * HEAD_SIZE]
        bias[at, :] = jnp.where(pos_of(me ^ k, key_index) <= query_pos, 0.0, -1e30)

    def visit_head(head, carried):
        mixed[...] = jnp.zeros_like(mixed)

        def visit_pair(pair, also):
            query = query_ref[head * per_head + pair]
            top = jnp.full((8, lanes), -1e30, jnp.float32)
            for c in range(total // chunk):
                at = pl.ds(c * chunk, chunk)
                raw = lax.dot_general(
                    keys[head, at, :],
                    query,
                    (((1,), (1,)), ((), ())),
                    preferred_element_type=jnp.float32,
                )
                shade = bias[at, :]
                raw = raw + jnp.concatenate([shade] * (lanes // rows), axis=1)
                scores[at, :] = raw
                top = jnp.maximum(top, jnp.max(raw.reshape(chunk // 8, 8, lanes), axis=0))
            top = jnp.max(top, axis=0, keepdims=True)
            summed = jnp.zeros((8, lanes), jnp.float32)
            for c in range(total // chunk):
                at = pl.ds(c * chunk, chunk)
                weight = jnp.exp2((scores[at, :] - top) * scale)
                scores[at, :] = weight
                summed = summed + jnp.sum(weight.reshape(chunk // 8, 8, lanes), axis=0)
            share = (1.0 / QUERY_GROUP_SIZE) / jnp.sum(summed, axis=0, keepdims=True)
            for c in range(total // chunk):
                at = pl.ds(c * chunk, chunk)
                part = scores[at, :] * share
                gathered = mixed[at, :]
                for j in range(lanes // rows):
                    gathered = gathered + part[:, j * rows : (j + 1) * rows]
                mixed[at, :] = gathered
            return also

        lax.fori_loop(0, per_head, visit_pair, 0)
        for k in range(slots):
            tile = jnp.transpose(mixed[pl.ds(k * rows, rows), :])
            mass_ref[me ^ k, pl.ds(head, 1), :] = jnp.sum(tile, axis=0, keepdims=True)
        return carried

    lax.fori_loop(0, KEY_VALUE_HEADS, visit_head, 0)


def attention_mass(place, block_order, queries, key_slots):
    slots = len(key_slots)
    rows = queries.shape[0]
    heads = queries.shape[1] // HEAD_SIZE
    total = rows * slots
    fold = 2
    arranged = jnp.transpose(queries.reshape(rows, heads, HEAD_SIZE), (1, 0, 2))
    arranged = arranged.reshape(heads // fold, fold * rows, HEAD_SIZE)
    return pl.pallas_call(
        functools.partial(attention_kernel, slots),
        out_shape=jax.ShapeDtypeStruct((slots, KEY_VALUE_HEADS, rows), jnp.float32),
        in_specs=[SMEM, SMEM, VMEM] + [VMEM] * slots,
        out_specs=VMEM,
        scratch_shapes=[
            pltpu.VMEM((KEY_VALUE_HEADS, total, HEAD_SIZE), jnp.bfloat16),
            pltpu.VMEM((total, rows), jnp.float32),
            pltpu.VMEM((total, fold * rows), jnp.float32),
            pltpu.VMEM((total, rows), jnp.float32),
        ],
        compiler_params=pltpu.CompilerParams(vmem_limit_bytes=VMEM_LIMIT),
        cost_estimate=pl.CostEstimate(
            flops=2 * rows * total * heads * HEAD_SIZE,
            bytes_accessed=2 * rows * heads * HEAD_SIZE,
            transcendentals=rows * total * heads,
        ),
    )(place, block_order, arranged, *key_slots)


def gradient_kernel(slots, dp, place_ref, message_ref, columns_ref, output_ref, hidden_ref, *refs):
    slope_refs = refs[:slots]
    grad_ref, mass_ref, small_ref = refs[slots : slots + 3]
    out_grad, slope, wide, grad = refs[slots + 3 :]
    me, part = place_ref[0], place_ref[1]
    rows = hidden_ref.shape[0]
    total = rows * slots
    units = hidden_ref.shape[1]
    mass = jnp.sum(message_ref[:, :slots], axis=0)
    out_grad[...] = mass
    mass_ref[...] = out_grad[me]
    residue = message_ref[:, slots] - jnp.log(1.0 + mass)
    out_grad[...] = residue / total
    loss_sum = jnp.sum(residue * residue) * (0.5 / total)
    grad_bias = jnp.sum(jnp.sum(out_grad[...], axis=0), axis=1, keepdims=True)
    output_rows = output_ref[...]
    output_three = jnp.concatenate([output_rows] * 3, axis=0)
    first_bias = jnp.zeros((8, units), jnp.float32)
    for k in range(slots):
        owner = me ^ k
        scaled = out_grad[owner] * message_ref[owner, slots + 1]
        back = lax.dot_general(
            jnp.concatenate(split3(scaled), axis=0),
            output_three,
            (((0,), (0,)), ((), ())),
            preferred_element_type=jnp.float32,
        )
        fall = back * slope_refs[k][...].astype(jnp.float32)
        first_bias = first_bias + jnp.sum(fall.reshape(rows // 8, 8, units), axis=0)
        slope[pl.ds(pl.multiple_of(owner * rows, rows), rows), :] = fall.astype(jnp.bfloat16)
        wide[:, k * rows : (k + 1) * rows] = columns_ref[k]
    grad[...] = jnp.dot(wide[...], slope[...], preferred_element_type=jnp.float32)
    share = grad.shape[0] // dp
    for k in range(dp):
        grad_ref[k] = grad[pl.ds(pl.multiple_of((part ^ k) * share, share), share), :]
    second = lax.dot_general(
        jnp.concatenate(split3(out_grad[me]), axis=0),
        hidden_ref[...],
        (((1,), (0,)), ((), ())),
        preferred_element_type=jnp.float32,
    )
    heads = KEY_VALUE_HEADS
    second = second[:heads] + second[heads : 2 * heads] + second[2 * heads :]
    small_ref[pl.ds(0, heads), :] = second
    small_ref[pl.ds(heads, 1), :] = jnp.sum(first_bias, axis=0, keepdims=True)
    small_ref[pl.ds(heads + 1, 1), :] = jnp.full((1, units), loss_sum, jnp.float32)
    small_ref[pl.ds(heads + 2, heads), :] = jnp.broadcast_to(grad_bias, (heads, units))
    small_ref[pl.ds(2 * heads + 2, 6), :] = jnp.zeros((6, units), jnp.float32)


def gradient(place, message, columns, output_weight, hidden, slope_slots, dp):
    slots = len(slope_slots)
    rows, units = hidden.shape
    depth = columns.shape[1]
    return pl.pallas_call(
        functools.partial(gradient_kernel, slots, dp),
        out_shape=(
            jax.ShapeDtypeStruct((dp, depth // dp, units), jnp.float32),
            jax.ShapeDtypeStruct((KEY_VALUE_HEADS, rows), jnp.float32),
            jax.ShapeDtypeStruct((16, units), jnp.float32),
        ),
        in_specs=[SMEM] + [VMEM] * (4 + slots),
        out_specs=(VMEM, VMEM, VMEM),
        scratch_shapes=[
            pltpu.VMEM((slots, KEY_VALUE_HEADS, rows), jnp.float32),
            pltpu.VMEM((slots * rows, units), jnp.bfloat16),
            pltpu.VMEM((depth, slots * rows), jnp.bfloat16),
            pltpu.VMEM((depth, units), jnp.float32),
        ],
        compiler_params=pltpu.CompilerParams(vmem_limit_bytes=VMEM_LIMIT),
    )(place, message, columns, output_weight, hidden, *slope_slots)


def square_kernel(parts, small_ref, *refs):
    part_refs, total_ref, send_ref = refs[:parts], refs[parts], refs[parts + 1]
    total = part_refs[0][...]
    for part_ref in part_refs[1:]:
        total = total + part_ref[...]
    total_ref[...] = total
    units = total.shape[1]
    square = jnp.sum(jnp.sum(total * total, axis=0, keepdims=True), axis=1, keepdims=True)
    row = KEY_VALUE_HEADS * 2 + 2
    send_ref[...] = small_ref[...]
    send_ref[pl.ds(row, 1), :] = jnp.broadcast_to(square, (1, units))


def squares(small, parts):
    return pl.pallas_call(
        functools.partial(square_kernel, len(parts)),
        out_shape=(
            jax.ShapeDtypeStruct(parts[0].shape, jnp.float32),
            jax.ShapeDtypeStruct(small.shape, jnp.float32),
        ),
        in_specs=[VMEM] * (1 + len(parts)),
        out_specs=(VMEM, VMEM),
        compiler_params=pltpu.CompilerParams(vmem_limit_bytes=VMEM_LIMIT),
    )(small, *parts)


def scale_kernel(slots, dp, entries, place_ref, message_ref, *refs):
    part_refs = refs[:dp]
    step_ref, second_ref, first_bias_ref, bias_ref, loss_ref = refs[dp:]
    part = place_ref[1]
    heads = KEY_VALUE_HEADS
    total = jnp.sum(message_ref[...], axis=0)
    once = message_ref[0]
    for d in range(1, dp):
        once = once + message_ref[d * slots]
    square = total[2 * heads + 2 : 2 * heads + 3, :1]
    inverse = 1.0 / jnp.sqrt(square / entries + 1e-06)
    share = part_refs[0].shape[0]
    for k in range(dp):
        at = pl.ds(pl.multiple_of((part ^ k) * share, share), share)
        step_ref[at, :] = part_refs[k][...] * inverse
    second = total[:heads]
    spread = jnp.sum(jnp.sum(second * second, axis=0, keepdims=True), axis=1, keepdims=True)
    second_ref[...] = second / jnp.sqrt(spread / second.size + 1e-06)
    first_bias = once[heads : heads + 1]
    spread = jnp.sum(first_bias * first_bias, axis=1, keepdims=True)
    first_bias_ref[...] = first_bias / jnp.sqrt(spread / first_bias.size + 1e-06)
    loss_ref[...] = once[heads + 1 : heads + 2, :128]
    bias_ref[...] = once[heads + 2 : 2 * heads + 2, :128]


def scaled(place, message, parts, slots, entries):
    dp = len(parts)
    share, units = parts[0].shape
    return pl.pallas_call(
        functools.partial(scale_kernel, slots, dp, entries),
        out_shape=(
            jax.ShapeDtypeStruct((dp * share, units), jnp.float32),
            jax.ShapeDtypeStruct((KEY_VALUE_HEADS, units), jnp.float32),
            jax.ShapeDtypeStruct((1, units), jnp.float32),
            jax.ShapeDtypeStruct((KEY_VALUE_HEADS, 128), jnp.float32),
            jax.ShapeDtypeStruct((1, 128), jnp.float32),
        ),
        in_specs=[SMEM] + [VMEM] * (1 + dp),
        out_specs=(VMEM,) * 5,
        compiler_params=pltpu.CompilerParams(vmem_limit_bytes=VMEM_LIMIT),
    )(place, message, *parts)


def send_all(value, axes, amount):
    copies = jnp.broadcast_to(value[None], (amount,) + value.shape)
    return lax.all_to_all(copies, axes, 0, 0, tiled=True)


def per_device(
    queries,
    rotated_key_rows,
    hidden_states,
    block_order,
    first_weight,
    first_bias,
    output_weight,
    output_bias,
):
    seq, dp = lax.axis_size("seq"), lax.axis_size("dp")
    rows, model = hidden_states.shape[1:]
    units = first_weight.shape[1]
    place = jnp.stack([lax.axis_index("seq"), lax.axis_index("dp")]).astype(jnp.int32)
    tokens = hidden_states.reshape(rows, model)

    key_slots = gather_xor(rotated_key_rows.reshape(rows, -1), "seq")
    columns = lax.all_to_all(
        jnp.transpose(tokens).reshape(seq, model // seq, rows), "seq", 0, 0, tiled=True
    )

    pre_act = jnp.dot(tokens, first_weight, preferred_element_type=jnp.float32) + first_bias
    gate = jax.nn.sigmoid(pre_act)
    hidden = (pre_act * gate).astype(jnp.bfloat16)
    predicted = (
        lax.dot_general(
            output_weight, hidden, (((1,), (1,)), ((), ())), preferred_element_type=jnp.float32
        )
        + output_bias[:, None]
    )
    fall = gate * (1.0 + pre_act * (1.0 - gate))
    reach = jnp.maximum(jnp.max(jnp.abs(fall), axis=1), 1e-30)
    fall_slots = gather_xor((fall / reach[:, None]).astype(jnp.float16), "seq")

    mass = attention_mass(place, block_order, queries.reshape(rows, -1), key_slots)
    reach_rows = jnp.broadcast_to(reach[None, None, :], (1,) + predicted.shape)
    message = jnp.concatenate([mass, predicted[None], reach_rows], axis=0)
    message = send_all(message, "seq", seq)

    slope_slots = [fall_slot.astype(jnp.float32) for fall_slot in fall_slots]
    grads, own_mass, small = gradient(
        place, message, columns, output_weight, hidden, slope_slots, dp
    )
    parts = [grads[0]] + [swap(grads[k], "dp", k) for k in range(1, dp)]
    total, small = squares(small, parts)
    totals = [total] + [swap(total, "dp", k) for k in range(1, dp)]
    message = send_all(small, ("dp", "seq"), dp * seq)
    step_first, second, bias_step, bias, loss = scaled(
        place, message, totals, seq, model * units
    )
    return (
        own_mass.reshape(1, KEY_VALUE_HEADS, rows),
        loss[0, 0],
        step_first,
        second,
        bias_step.reshape(units),
        bias[:, 0],
    )


def solution(mesh):
    tokens = P("dp", "seq", None)
    return jax.shard_map(
        per_device,
        mesh=mesh,
        in_specs=(tokens, tokens, tokens, P(), P(), P(), P(), P()),
        out_specs=(P("dp", None, "seq"), P(), P("seq", None), P(), P(), P()),
        check_vma=False,
    )
```

time: 332 us -> 219 us (0.66)
  blocking collectives: 71.2 us -> 0 us
  matrix products: 39.8 us -> 5.57 us
  waiting for transfers between devices: 146 us -> 113 us
  Pallas kernels: 0 us -> 31.7 us
  starting transfers between devices: 7.6 us -> 38.4 us
  between operations: 16.7 us -> 0.95 us
  other arithmetic: 26.1 us -> 13.3 us
  local copies, waits for them, and re-layouts: 22.4 us -> 15.7 us
    ppermute x0 -> x32, waiting for transfers between devices: none -> 97.1 us  [swap(): lax.ppermute(value, axis, [(i, i ^ mask) for i in range(lax.axis_size(axi...]
    all_gather x2 -> x0, waiting for transfers between devices: 96.4 us -> none  [the longest x1 58.7 us: per_device(): keys_whole = lax.all_gather(local_key_rows, 'seq', axis=0, tiled=True)]
    psum x2 -> x0, blocking collectives: 71.2 us -> none  [the longest x1 38.8 us: per_device(): lax.psum((second_part, first_bias_part, bias_part, loss_part), ('dp', 'se...]
    unnamed x5 -> x0, waiting for transfers between devices: 50 us -> none
    dot_general x12 -> x1, matrix products: 39.1 us -> 5.47 us  [per_device(): jnp.dot(tokens, first_weight, preferred_element_type=jnp.float32)]
    pallas_call x0 -> x4, Pallas kernels: none -> 31.7 us  [the longest x1 20.8 us: attention_mass(): pl.pallas_call(functools.partial(attention_kernel, slots), out_shape=jax....]
    ppermute x0 -> x32, starting transfers between devices: none -> 25.2 us  [swap(): lax.ppermute(value, axis, [(i, i ^ mask) for i in range(lax.axis_size(axi...]
    reduce_sum x16 -> x0, other arithmetic: 22.3 us -> none  [the longest x4 18.2 us: normalizer_step(): jnp.sum(exponents, axis=-1)]
  transfers between devices with their start and end apart: 5 -> 35, of which waited for: 3 -> 13; matrix products, arithmetic and copies ran while one was open for 23% -> 10% of each run, Pallas kernels for 0% -> 0%
where the time goes in v1:
time: 219 us
  waiting for transfers between devices  113 us (52%)
  starting transfers between devices  38.4 us (18%)
  Pallas kernels  31.7 us (14%)
  local copies, waits for them, and re-layouts  15.7 us (7%)
  other arithmetic  13.3 us (6%)
  matrix products  5.57 us (3%)
    ppermute x32, waiting for transfers between devices, swap(): lax.ppermute(value, axis, [(i, i ^ mask) for i in range(lax.axis_size(axi...  97.1 us
    ppermute x32, starting transfers between devices, swap(): lax.ppermute(value, axis, [(i, i ^ mask) for i in range(lax.axis_size(axi...  25.2 us
    pallas_call x1, Pallas kernels, attention_mass(): pl.pallas_call(functools.partial(attention_kernel, slots), out_shape=jax....  20.8 us
    all_to_all x2, waiting for transfers between devices, send_all(): return lax.all_to_all(copies, axes, 0, 0, tiled=True)  15.8 us
    convert_element_type x16, other arithmetic, per_device(): slope_slots = [fall_slot.astype(jnp.float32) for fall_slot in fall_slots]  11.9 us
    all_to_all x2, starting transfers between devices, send_all(): return lax.all_to_all(copies, axes, 0, 0, tiled=True)  8.72 us
    pallas_call x1, Pallas kernels, gradient(): pl.pallas_call(functools.partial(gradient_kernel, slots, dp), out_shape=(...  6.16 us
    unnamed x53, local copies, waits for them, and re-layouts  5.66 us
  transfers between devices with their start and end apart: 35, of which 13 were waited for; matrix products, arithmetic and copies ran while one was open for 10% of the time, Pallas kernels for 0%

profile of v1, /device:TPU:0, one launch (start us, length us, event | category | flops | bytes accessed | tf_op | source)
XLA Modules:
  0.0 218.5 jit_solution(2606338788585668198)
XLA Ops:
  1.1 2.6 %collective-permute-start.1 = (bf16[128,512]{1,0:T(8,128)(2,1)}, bf16[128,512]{1,0:T(8,128)(2,1)S(1)}, u32[]{:S(2)}, u32[]{:S(2)}) collective-permute-start(bf16[128,512]{1,0:T(8,128)(2,1)} %bitcast.40), channel_id=1, source_target_pairs={{0,2},{1,3},{2,0},{3,1},{4,6},{5,7},{6,4},{7,5},{8,10},{9,11},{10,... | collective-permute-start | bytes 393224 | tf_op jit(solution)/shard_map/ppermute | solution.py:21
  3.7 1.6 collective-permute-start.3
  5.3 2.6 %collective-permute-start.7 = (bf16[128,512]{1,0:T(8,128)(2,1)}, bf16[128,512]{1,0:T(8,128)(2,1)S(1)}, u32[]{:S(2)}, u32[]{:S(2)}) collective-permute-start(bf16[128,512]{1,0:T(8,128)(2,1)} %bitcast.42), channel_id=1, source_target_pairs={{0,8},{1,9},{2,10},{3,11},{4,12},{5,13},{6,14},{7,15},{8,0},{9,1},... | collective-permute-start | bytes 393224 | tf_op jit(solution)/shard_map/ppermute | solution.py:21
  8.1 5.5 %abs_reduce_fusion = (f32[128]{0:T(128)S(1)}, f32[128,512]{1,0:T(8,128)S(1)}) fusion(f32[512]{0:T(512)} %param.13, bf16[8192,512]{1,0:T(8,128)(2,1)} %param.12, bf16[1,128,8192]{2,1,0:T(8,128)(2,1)} %param.10), kind=kOutput, calls=%fused_computation.8 | convolution fusion | flops 1074397056 | bytes 10750464 | tf_op jit(solution)/shard_map/dot_general | solution.py:313
  14.3 4.1 %collective-permute-done.7.refs_8_ = bf16[128,512]{1,0:T(8,128)(2,1)S(1)} collective-permute-done((bf16[128,512]{1,0:T(8,128)(2,1)}, bf16[128,512]{1,0:T(8,128)(2,1)S(1)}, u32[]{:S(2)}, u32[]{:S(2)}) %collective-permute-start.7) | collective-permute-done | bytes 131104 | tf_op jit(solution)/shard_map/ppermute | solution.py:21
  18.9 1.5 collective-permute-start.13
  20.5 0.8 fusion.6
  21.9 1.9 collective-permute-done.9.refs_10_
  23.9 1.4 collective-permute-done.13.refs_14_
  26.1 1.4 copy.16
  29.2 20.8 %shard_map.127 = f32[16,4,128]{2,1,0:T(4,128)} custom-call(s32[2]{0:T(128)} %pad_add_fusion.place_ref, s32[32]{0:T(128)} %order_ref.1, bf16[16,256,128]{2,1,0:T(8,128)(2,1)} %bitcast.38, bf16[128,512]{1,0:T(8,128)(2,1)} %bitcast.44, bf16[128,512]{1,0:T(8,128)(2,1)} %copy-done.10, bf16[128,512]{1,0:T(8,128)(2,1)} %copy-done.11, bf16[128,512]{1,0:T(8,128)(2,1)} %copy-done.17, ...), custom_call_target="tpu_custom_call" | custom-call | flops 2147483648 | bytes 1048576 | tf_op jit(solution)/shard_map/pallas_call | solution.py:125
  50.0 0.8 pad_maximum_fusion
  50.8 0.9 broadcast_in_dim.10
  51.7 5.1 %all-to-all-start = ((f32[16,18,4,128]{3,2,1,0:T(4,128)}), f32[16,18,4,128]{3,2,1,0:T(4,128)S(1)}, u32[]{:S(2)}, u32[]{:S(2)}) async-start(f32[16,18,4,128]{3,2,1,0:T(4,128)} %broadcast_in_dim.10), calls=%async_computation | async-start | bytes 1179648 | tf_op jit(solution)/shard_map/all_to_all | solution.py:289
  56.8 2.5 %copy.17 = bf16[8192,128]{1,0:T(8,128)(2,1)} copy(bf16[8192,128]{0,1:T(8,128)(2,1)S(1)} %bitcast.34) | data formatting | bytes 4194304 | tf_op jit(solution)/shard_map/transpose | solution.py:310
  59.3 13.1 %all-to-all-done.message_ref = f32[16,18,4,128]{3,2,1,0:T(4,128)S(1)} async-done(((f32[16,18,4,128]{3,2,1,0:T(4,128)}), f32[16,18,4,128]{3,2,1,0:T(4,128)S(1)}, u32[]{:S(2)}, u32[]{:S(2)}) %all-to-all-start) | async-done | bytes 589856 | tf_op jit(solution)/shard_map/all_to_all | solution.py:289
  72.3 0.8 copy-done.3
  73.1 4.4 %all-to-all-start.1 = ((bf16[16,512,128]{2,1,0:T(8,128)(2,1)}), bf16[16,512,128]{2,1,0:T(8,128)(2,1)S(1)}, u32[]{:S(2)}, u32[]{:S(2)}) async-start(bf16[16,512,128]{2,1,0:T(8,128)(2,1)} %bitcast.35), calls=%async_computation.1 | async-start | bytes 4194304 | tf_op jit(solution)/shard_map/all_to_all | solution.py:309
  77.6 1.9 collective-permute-start.16
  79.5 1.5 collective-permute-start.18
  81.0 2.4 %collective-permute-start.22 = (f16[128,512]{1,0:T(8,128)(2,1)S(1)}, f16[128,512]{1,0:T(8,128)(2,1)S(1)}, u32[]{:S(2)}, u32[]{:S(2)}) collective-permute-start(f16[128,512]{1,0:T(8,128)(2,1)S(1)} %get-tuple-element.27), channel_id=1, source_target_pairs={{0,8},{1,9},{2,10},{3,11},{4,12},{5,13},{6,14},{7,15},{8,0},{9,1},... | collective-permute-start | bytes 393224 | tf_op jit(solution)/shard_map/ppermute | solution.py:21
  83.9 11.9 %collective-permute-done.16 = f16[128,512]{1,0:T(8,128)(2,1)S(1)} collective-permute-done((f16[128,512]{1,0:T(8,128)(2,1)S(1)}, f16[128,512]{1,0:T(8,128)(2,1)S(1)}, u32[]{:S(2)}, u32[]{:S(2)}) %collective-permute-start.16) | collective-permute-done | bytes 131104 | tf_op jit(solution)/shard_map/ppermute | solution.py:21
  95.8 19.7 %collective-permute-done.18 = f16[128,512]{1,0:T(8,128)(2,1)S(1)} collective-permute-done((f16[128,512]{1,0:T(8,128)(2,1)S(1)}, f16[128,512]{1,0:T(8,128)(2,1)S(1)}, u32[]{:S(2)}, u32[]{:S(2)}) %collective-permute-start.18) | collective-permute-done | bytes 131104 | tf_op jit(solution)/shard_map/ppermute | solution.py:21
  115.5 2.2 %collective-permute-start.20 = (f16[128,512]{1,0:T(8,128)(2,1)S(1)}, f16[128,512]{1,0:T(8,128)(2,1)S(1)}, u32[]{:S(2)}, u32[]{:S(2)}) collective-permute-start(f16[128,512]{1,0:T(8,128)(2,1)S(1)} %collective-permute-done.18), channel_id=1, source_target_pairs={{0,2},{1,3},{2,0},{3,1},{4,6},{5,7},{6,4},{7,5},{8,10},{9,11},{10,... | collective-permute-start | bytes 393224 | tf_op jit(solution)/shard_map/ppermute | solution.py:21
  117.7 17.8 %collective-permute-done.22 = f16[128,512]{1,0:T(8,128)(2,1)S(1)} collective-permute-done((f16[128,512]{1,0:T(8,128)(2,1)S(1)}, f16[128,512]{1,0:T(8,128)(2,1)S(1)}, u32[]{:S(2)}, u32[]{:S(2)}) %collective-permute-start.22) | collective-permute-done | bytes 131104 | tf_op jit(solution)/shard_map/ppermute | solution.py:21
  135.5 1.6 collective-permute-start.24
  138.2 3.4 %collective-permute-done.24 = f16[128,512]{1,0:T(8,128)(2,1)S(1)} collective-permute-done((f16[128,512]{1,0:T(8,128)(2,1)S(1)}, f16[128,512]{1,0:T(8,128)(2,1)S(1)}, u32[]{:S(2)}, u32[]{:S(2)}) %collective-permute-start.24) | collective-permute-done | bytes 131104 | tf_op jit(solution)/shard_map/ppermute | solution.py:21
  141.5 1.4 collective-permute-done.28
  143.6 0.7 convert_element_type.60.refs_4_
  148.8 0.8 convert_element_type.59.refs_3_
  149.5 0.8 convert_element_type.61.refs_5_
  151.0 0.7 convert_element_type.69.refs_13_
  152.5 0.7 convert_element_type.67.refs_11_
  154.0 1.3 copy-done.1
  155.3 6.2 %shard_map.128 = (f32[2,256,512]{2,1,0:T(8,128)}, f32[4,128]{1,0:T(4,128)}, f32[16,512]{1,0:T(8,128)}) custom-call(s32[2]{0:T(128)} %pad_add_fusion.place_ref, f32[16,18,4,128]{3,2,1,0:T(4,128)} %copy-done.3, bf16[16,512,128]{2,1,0:T(8,128)(2,1)} %copy-done.1, bf16[4,512]{1,0:T(4,128)(2,1)} %output_ref.1, bf16[128,512]{1,0:T(8,128)(2,1)} %copy-done.8, ...), custom_call_target="tpu_custom_call" | custom-call | tf_op jit(solution)/shard_map/pallas_call | solution.py:199
  161.5 2.1 slice_bitcast_fusion
  163.6 1.5 collective-permute-start.30
  165.1 12.8 %collective-permute-done.30.refs_1_ = f32[256,512]{1,0:T(8,128)S(1)} collective-permute-done((f32[256,512]{1,0:T(8,128)S(1)}, f32[256,512]{1,0:T(8,128)S(1)}, u32[]{:S(2)}, u32[]{:S(2)}) %collective-permute-start.30) | collective-permute-done | bytes 524320 | tf_op jit(solution)/shard_map/ppermute | solution.py:21
  177.9 0.8 copy-done.7
  178.7 2.1 shard_map.129
  180.8 1.9 broadcast_in_dim.11
  182.7 3.6 %all-to-all-start.2 = ((f32[32,16,512]{2,1,0:T(8,128)}), f32[32,16,512]{2,1,0:T(8,128)S(1)}, u32[]{:S(2)}, u32[]{:S(2)}) async-start(f32[32,16,512]{2,1,0:T(8,128)} %broadcast_in_dim.11), calls=%async_computation.2 | async-start | bytes 2097152 | tf_op jit(solution)/shard_map/all_to_all | solution.py:289
  186.4 1.8 collective-permute-start.31
  188.2 22.6 %collective-permute-done.31.refs_1_ = f32[256,512]{1,0:T(8,128)S(1)} collective-permute-done((f32[256,512]{1,0:T(8,128)S(1)}, f32[256,512]{1,0:T(8,128)S(1)}, u32[]{:S(2)}, u32[]{:S(2)}) %collective-permute-start.31) | collective-permute-done | bytes 524320 | tf_op jit(solution)/shard_map/ppermute | solution.py:21
  210.8 2.8 %all-to-all-done.2.message_ref = f32[32,16,512]{2,1,0:T(8,128)S(1)} async-done(((f32[32,16,512]{2,1,0:T(8,128)}), f32[32,16,512]{2,1,0:T(8,128)S(1)}, u32[]{:S(2)}, u32[]{:S(2)}) %all-to-all-start.2) | async-done | bytes 1048608 | tf_op jit(solution)/shard_map/all_to_all | solution.py:289
  213.5 1.0 copy-done.2
  214.6 2.7 %shard_map.130 = (f32[512,512]{1,0:T(8,128)}, f32[4,512]{1,0:T(4,128)}, f32[1,512]{1,0:T(1,128)}, f32[4,128]{1,0:T(4,128)}, f32[1,128]{1,0:T(1,128)}) custom-call(s32[2]{0:T(128)} %pad_add_fusion.place_ref, f32[32,16,512]{2,1,0:T(8,128)} %copy-done.2, f32[256,512]{1,0:T(8,128)} %get-tuple-element.20.refs_0_, f32[256,512]{1,0:T(8,128)} %copy-done.6), custom_call_target="tpu_custom_call" | custom-call | tf_op jit(solution)/shard_map/pallas_call | solution.py:272
  217.2 1.3 slice_reduce_fusion
  (107 shorter events, 13.9 us)
Async XLA Ops:
  0.6 13.1 %collective-permute-start = (bf16[128,512]{1,0:T(8,128)(2,1)}, bf16[128,512]{1,0:T(8,128)(2,1)S(1)}, u32[]{:S(2)}, u32[]{:S(2)}) collective-permute-start(bf16[128,512]{1,0:T(8,128)(2,1)} %bitcast.39), channel_id=1, source_target_pairs={{0,1},{1,0},{2,3},{3,2},{4,5},{5,4},{6,7},{7,6},{8,9},{9,8},{10,11... | collective-permute-start | bytes 393224 | tf_op jit(solution)/shard_map/ppermute | solution.py:21
  1.1 13.0 %collective-permute-start.1 = (bf16[128,512]{1,0:T(8,128)(2,1)}, bf16[128,512]{1,0:T(8,128)(2,1)S(1)}, u32[]{:S(2)}, u32[]{:S(2)}) collective-permute-start(bf16[128,512]{1,0:T(8,128)(2,1)} %bitcast.40), channel_id=1, source_target_pairs={{0,2},{1,3},{2,0},{3,1},{4,6},{5,7},{6,4},{7,5},{8,10},{9,11},{10,... | collective-permute-start | bytes 393224 | tf_op jit(solution)/shard_map/ppermute | solution.py:21
  3.7 9.9 %collective-permute-start.3 = (bf16[128,512]{1,0:T(8,128)(2,1)}, bf16[128,512]{1,0:T(8,128)(2,1)S(1)}, u32[]{:S(2)}, u32[]{:S(2)}) collective-permute-start(bf16[128,512]{1,0:T(8,128)(2,1)} %bitcast.41), channel_id=1, source_target_pairs={{0,4},{1,5},{2,6},{3,7},{4,0},{5,1},{6,2},{7,3},{8,12},{9,13},{10,... | collective-permute-start | bytes 393224 | tf_op jit(solution)/shard_map/ppermute | solution.py:21
  5.3 13.1 %collective-permute-start.7 = (bf16[128,512]{1,0:T(8,128)(2,1)}, bf16[128,512]{1,0:T(8,128)(2,1)S(1)}, u32[]{:S(2)}, u32[]{:S(2)}) collective-permute-start(bf16[128,512]{1,0:T(8,128)(2,1)} %bitcast.42), channel_id=1, source_target_pairs={{0,8},{1,9},{2,10},{3,11},{4,12},{5,13},{6,14},{7,15},{8,0},{9,1},... | collective-permute-start | bytes 393224 | tf_op jit(solution)/shard_map/ppermute | solution.py:21
  7.9 11.0 %collective-permute-start.11 = (bf16[128,512]{1,0:T(8,128)(2,1)}, bf16[128,512]{1,0:T(8,128)(2,1)S(1)}, u32[]{:S(2)}, u32[]{:S(2)}) collective-permute-start(bf16[128,512]{1,0:T(8,128)(2,1)} %bitcast.43), channel_id=1, source_target_pairs={{0,12},{1,13},{2,14},{3,15},{4,8},{5,9},{6,10},{7,11},{8,4},{9,5},... | collective-permute-start | bytes 393224 | tf_op jit(solution)/shard_map/ppermute | solution.py:21
  8.1 17.7 %copy-start.4 = (bf16[1,128,4096]{2,1,0:T(8,128)(2,1)S(1)}, bf16[1,128,4096]{2,1,0:T(8,128)(2,1)}, u32[]{:S(2)}) copy-start(bf16[1,128,4096]{2,1,0:T(8,128)(2,1)} %param.8) | copy-start | bytes 3145732
  13.6 13.9 %copy-start.12 = (bf16[128,512]{1,0:T(8,128)(2,1)}, bf16[128,512]{1,0:T(8,128)(2,1)S(1)}, u32[]{:S(2)}) copy-start(bf16[128,512]{1,0:T(8,128)(2,1)S(1)} %collective-permute-done.3.refs_4_) | copy-start | bytes 393220
  13.6 7.7 %collective-permute-start.4 = (bf16[128,512]{1,0:T(8,128)(2,1)S(1)}, bf16[128,512]{1,0:T(8,128)(2,1)S(1)}, u32[]{:S(2)}, u32[]{:S(2)}) collective-permute-start(bf16[128,512]{1,0:T(8,128)(2,1)S(1)} %collective-permute-done.3.refs_4_), channel_id=1, source_target_pairs={{0,1},{1,0},{2,3},{3,2},{4,5},{5,4},{6,7},{7,6},{8,9},{9,8},{10,11... | collective-permute-start | bytes 393224 | tf_op jit(solution)/shard_map/ppermute | solution.py:21
  13.7 13.8 %copy-start.10 = (bf16[128,512]{1,0:T(8,128)(2,1)}, bf16[128,512]{1,0:T(8,128)(2,1)S(1)}, u32[]{:S(2)}) copy-start(bf16[128,512]{1,0:T(8,128)(2,1)S(1)} %collective-permute-done.refs_1_) | copy-start | bytes 393220
  13.7 8.1 %collective-permute-start.5 = (bf16[128,512]{1,0:T(8,128)(2,1)S(1)}, bf16[128,512]{1,0:T(8,128)(2,1)S(1)}, u32[]{:S(2)}, u32[]{:S(2)}) collective-permute-start(bf16[128,512]{1,0:T(8,128)(2,1)S(1)} %collective-permute-done.3.refs_4_), channel_id=1, source_target_pairs={{0,2},{1,3},{2,0},{3,1},{4,6},{5,7},{6,4},{7,5},{8,10},{9,11},{10,... | collective-permute-start | bytes 393224 | tf_op jit(solution)/shard_map/ppermute | solution.py:21
  14.1 13.4 %copy-start.11 = (bf16[128,512]{1,0:T(8,128)(2,1)}, bf16[128,512]{1,0:T(8,128)(2,1)S(1)}, u32[]{:S(2)}) copy-start(bf16[128,512]{1,0:T(8,128)(2,1)S(1)} %collective-permute-done.1.refs_2_) | copy-start | bytes 393220
  14.1 7.2 %collective-permute-start.2 = (bf16[128,512]{1,0:T(8,128)(2,1)S(1)}, bf16[128,512]{1,0:T(8,128)(2,1)S(1)}, u32[]{:S(2)}, u32[]{:S(2)}) collective-permute-start(bf16[128,512]{1,0:T(8,128)(2,1)S(1)} %collective-permute-done.1.refs_2_), channel_id=1, source_target_pairs={{0,1},{1,0},{2,3},{3,2},{4,5},{5,4},{6,7},{7,6},{8,9},{9,8},{10,11... | collective-permute-start | bytes 393224 | tf_op jit(solution)/shard_map/ppermute | solution.py:21
  18.4 9.1 %copy-start.13 = (bf16[128,512]{1,0:T(8,128)(2,1)}, bf16[128,512]{1,0:T(8,128)(2,1)S(1)}, u32[]{:S(2)}) copy-start(bf16[128,512]{1,0:T(8,128)(2,1)S(1)} %collective-permute-done.7.refs_8_) | copy-start | bytes 393220
  18.4 5.4 %collective-permute-start.9 = (bf16[128,512]{1,0:T(8,128)(2,1)S(1)}, bf16[128,512]{1,0:T(8,128)(2,1)S(1)}, u32[]{:S(2)}, u32[]{:S(2)}) collective-permute-start(bf16[128,512]{1,0:T(8,128)(2,1)S(1)} %collective-permute-done.7.refs_8_), channel_id=1, source_target_pairs={{0,2},{1,3},{2,0},{3,1},{4,6},{5,7},{6,4},{7,5},{8,10},{9,11},{10,... | collective-permute-start | bytes 393224 | tf_op jit(solution)/shard_map/ppermute | solution.py:21
  18.9 8.6 %copy-start.14 = (bf16[128,512]{1,0:T(8,128)(2,1)}, bf16[128,512]{1,0:T(8,128)(2,1)S(1)}, u32[]{:S(2)}) copy-start(bf16[128,512]{1,0:T(8,128)(2,1)S(1)} %collective-permute-done.11.refs_12_) | copy-start | bytes 393220
  18.9 6.3 %collective-permute-start.13 = (bf16[128,512]{1,0:T(8,128)(2,1)S(1)}, bf16[128,512]{1,0:T(8,128)(2,1)S(1)}, u32[]{:S(2)}, u32[]{:S(2)}) collective-permute-start(bf16[128,512]{1,0:T(8,128)(2,1)S(1)} %collective-permute-done.11.refs_12_), channel_id=1, source_target_pairs={{0,2},{1,3},{2,0},{3,1},{4,6},{5,7},{6,4},{7,5},{8,10},{9,11},{10,... | collective-permute-start | bytes 393224 | tf_op jit(solution)/shard_map/ppermute | solution.py:21
  21.3 6.3 %copy-start.8 = (bf16[128,512]{1,0:T(8,128)(2,1)}, bf16[128,512]{1,0:T(8,128)(2,1)S(1)}, u32[]{:S(2)}) copy-start(bf16[128,512]{1,0:T(8,128)(2,1)S(1)} %get-tuple-element.30.hidden_ref) | copy-start | bytes 393220
  21.3 6.2 %copy-start.17 = (bf16[128,512]{1,0:T(8,128)(2,1)}, bf16[128,512]{1,0:T(8,128)(2,1)S(1)}, u32[]{:S(2)}) copy-start(bf16[128,512]{1,0:T(8,128)(2,1)S(1)} %collective-permute-done.2.refs_3_) | copy-start | bytes 393220
  21.3 6.4 %collective-permute-start.8 = (bf16[128,512]{1,0:T(8,128)(2,1)S(1)}, bf16[128,512]{1,0:T(8,128)(2,1)S(1)}, u32[]{:S(2)}, u32[]{:S(2)}) collective-permute-start(bf16[128,512]{1,0:T(8,128)(2,1)S(1)} %collective-permute-done.7.refs_8_), channel_id=1, source_target_pairs={{0,1},{1,0},{2,3},{3,2},{4,5},{5,4},{6,7},{7,6},{8,9},{9,8},{10,11... | collective-permute-start | bytes 393224 | tf_op jit(solution)/shard_map/ppermute | solution.py:21
  21.3 6.2 %copy-start.15 = (bf16[128,512]{1,0:T(8,128)(2,1)}, bf16[128,512]{1,0:T(8,128)(2,1)S(1)}, u32[]{:S(2)}) copy-start(bf16[128,512]{1,0:T(8,128)(2,1)S(1)} %collective-permute-done.4.refs_5_) | copy-start | bytes 393220
  21.3 6.4 %collective-permute-start.12 = (bf16[128,512]{1,0:T(8,128)(2,1)S(1)}, bf16[128,512]{1,0:T(8,128)(2,1)S(1)}, u32[]{:S(2)}, u32[]{:S(2)}) collective-permute-start(bf16[128,512]{1,0:T(8,128)(2,1)S(1)} %collective-permute-done.11.refs_12_), channel_id=1, source_target_pairs={{0,1},{1,0},{2,3},{3,2},{4,5},{5,4},{6,7},{7,6},{8,9},{9,8},{10,11... | collective-permute-start | bytes 393224 | tf_op jit(solution)/shard_map/ppermute | solution.py:21
  21.8 5.7 %copy-start.16 = (bf16[128,512]{1,0:T(8,128)(2,1)}, bf16[128,512]{1,0:T(8,128)(2,1)S(1)}, u32[]{:S(2)}) copy-start(bf16[128,512]{1,0:T(8,128)(2,1)S(1)} %collective-permute-done.5.refs_6_) | copy-start | bytes 393220
  21.8 6.0 %collective-permute-start.6 = (bf16[128,512]{1,0:T(8,128)(2,1)S(1)}, bf16[128,512]{1,0:T(8,128)(2,1)S(1)}, u32[]{:S(2)}, u32[]{:S(2)}) collective-permute-start(bf16[128,512]{1,0:T(8,128)(2,1)S(1)} %collective-permute-done.5.refs_6_), channel_id=1, source_target_pairs={{0,1},{1,0},{2,3},{3,2},{4,5},{5,4},{6,7},{7,6},{8,9},{9,8},{10,11... | collective-permute-start | bytes 393224 | tf_op jit(solution)/shard_map/ppermute | solution.py:21
  23.9 3.7 %copy-start.18 = (bf16[128,512]{1,0:T(8,128)(2,1)}, bf16[128,512]{1,0:T(8,128)(2,1)S(1)}, u32[]{:S(2)}) copy-start(bf16[128,512]{1,0:T(8,128)(2,1)S(1)} %collective-permute-done.9.refs_10_) | copy-start | bytes 393220
  23.9 4.0 %collective-permute-start.10 = (bf16[128,512]{1,0:T(8,128)(2,1)S(1)}, bf16[128,512]{1,0:T(8,128)(2,1)S(1)}, u32[]{:S(2)}, u32[]{:S(2)}) collective-permute-start(bf16[128,512]{1,0:T(8,128)(2,1)S(1)} %collective-permute-done.9.refs_10_), channel_id=1, source_target_pairs={{0,1},{1,0},{2,3},{3,2},{4,5},{5,4},{6,7},{7,6},{8,9},{9,8},{10,11... | collective-permute-start | bytes 393224 | tf_op jit(solution)/shard_map/ppermute | solution.py:21
  25.3 2.6 %collective-permute-start.14 = (bf16[128,512]{1,0:T(8,128)(2,1)S(1)}, bf16[128,512]{1,0:T(8,128)(2,1)S(1)}, u32[]{:S(2)}, u32[]{:S(2)}) collective-permute-start(bf16[128,512]{1,0:T(8,128)(2,1)S(1)} %collective-permute-done.13.refs_14_), channel_id=1, source_target_pairs={{0,1},{1,0},{2,3},{3,2},{4,5},{5,4},{6,7},{7,6},{8,9},{9,8},{10,11... | collective-permute-start | bytes 393224 | tf_op jit(solution)/shard_map/ppermute | solution.py:21
  29.2 27.6 %copy-start = (bf16[1,128,8192]{2,1,0:T(8,128)(2,1)S(1)}, bf16[1,128,8192]{2,1,0:T(8,128)(2,1)}, u32[]{:S(2)}) copy-start(bf16[1,128,8192]{2,1,0:T(8,128)(2,1)} %param.10) | copy-start | bytes 6291460
  51.7 20.7 %all-to-all-start = ((f32[16,18,4,128]{3,2,1,0:T(4,128)}), f32[16,18,4,128]{3,2,1,0:T(4,128)S(1)}, u32[]{:S(2)}, u32[]{:S(2)}) async-start(f32[16,18,4,128]{3,2,1,0:T(4,128)} %broadcast_in_dim.10), calls=%async_computation | async-start | bytes 1179648 | tf_op jit(solution)/shard_map/all_to_all | solution.py:289
  73.1 80.8 %all-to-all-start.1 = ((bf16[16,512,128]{2,1,0:T(8,128)(2,1)}), bf16[16,512,128]{2,1,0:T(8,128)(2,1)S(1)}, u32[]{:S(2)}, u32[]{:S(2)}) async-start(bf16[16,512,128]{2,1,0:T(8,128)(2,1)} %bitcast.35), calls=%async_computation.1 | async-start | bytes 4194304 | tf_op jit(solution)/shard_map/all_to_all | solution.py:309
  77.6 18.2 %collective-permute-start.16 = (f16[128,512]{1,0:T(8,128)(2,1)S(1)}, f16[128,512]{1,0:T(8,128)(2,1)S(1)}, u32[]{:S(2)}, u32[]{:S(2)}) collective-permute-start(f16[128,512]{1,0:T(8,128)(2,1)S(1)} %get-tuple-element.27), channel_id=1, source_target_pairs={{0,2},{1,3},{2,0},{3,1},{4,6},{5,7},{6,4},{7,5},{8,10},{9,11},{10,... | collective-permute-start | bytes 393224 | tf_op jit(solution)/shard_map/ppermute | solution.py:21
  79.5 36.0 %collective-permute-start.18 = (f16[128,512]{1,0:T(8,128)(2,1)S(1)}, f16[128,512]{1,0:T(8,128)(2,1)S(1)}, u32[]{:S(2)}, u32[]{:S(2)}) collective-permute-start(f16[128,512]{1,0:T(8,128)(2,1)S(1)} %get-tuple-element.27), channel_id=1, source_target_pairs={{0,4},{1,5},{2,6},{3,7},{4,0},{5,1},{6,2},{7,3},{8,12},{9,13},{10,... | collective-permute-start | bytes 393224 | tf_op jit(solution)/shard_map/ppermute | solution.py:21
  81.0 34.5 %collective-permute-start.15 = (f16[128,512]{1,0:T(8,128)(2,1)S(1)}, f16[128,512]{1,0:T(8,128)(2,1)S(1)}, u32[]{:S(2)}, u32[]{:S(2)}) collective-permute-start(f16[128,512]{1,0:T(8,128)(2,1)S(1)} %get-tuple-element.27), channel_id=1, source_target_pairs={{0,1},{1,0},{2,3},{3,2},{4,5},{5,4},{6,7},{7,6},{8,9},{9,8},{10,11... | collective-permute-start | bytes 393224 | tf_op jit(solution)/shard_map/ppermute | solution.py:21
  81.0 54.6 %collective-permute-start.22 = (f16[128,512]{1,0:T(8,128)(2,1)S(1)}, f16[128,512]{1,0:T(8,128)(2,1)S(1)}, u32[]{:S(2)}, u32[]{:S(2)}) collective-permute-start(f16[128,512]{1,0:T(8,128)(2,1)S(1)} %get-tuple-element.27), channel_id=1, source_target_pairs={{0,8},{1,9},{2,10},{3,11},{4,12},{5,13},{6,14},{7,15},{8,0},{9,1},... | collective-permute-start | bytes 393224 | tf_op jit(solution)/shard_map/ppermute | solution.py:21
  83.3 53.8 %collective-permute-start.26 = (f16[128,512]{1,0:T(8,128)(2,1)S(1)}, f16[128,512]{1,0:T(8,128)(2,1)S(1)}, u32[]{:S(2)}, u32[]{:S(2)}) collective-permute-start(f16[128,512]{1,0:T(8,128)(2,1)S(1)} %get-tuple-element.27), channel_id=1, source_target_pairs={{0,12},{1,13},{2,14},{3,15},{4,8},{5,9},{6,10},{7,11},{8,4},{9,5},... | collective-permute-start | bytes 393224 | tf_op jit(solution)/shard_map/ppermute | solution.py:21
  95.8 41.8 %collective-permute-start.17 = (f16[128,512]{1,0:T(8,128)(2,1)S(1)}, f16[128,512]{1,0:T(8,128)(2,1)S(1)}, u32[]{:S(2)}, u32[]{:S(2)}) collective-permute-start(f16[128,512]{1,0:T(8,128)(2,1)S(1)} %collective-permute-done.16), channel_id=1, source_target_pairs={{0,1},{1,0},{2,3},{3,2},{4,5},{5,4},{6,7},{7,6},{8,9},{9,8},{10,11... | collective-permute-start | bytes 393224 | tf_op jit(solution)/shard_map/ppermute | solution.py:21
  115.5 22.1 %collective-permute-start.19 = (f16[128,512]{1,0:T(8,128)(2,1)S(1)}, f16[128,512]{1,0:T(8,128)(2,1)S(1)}, u32[]{:S(2)}, u32[]{:S(2)}) collective-permute-start(f16[128,512]{1,0:T(8,128)(2,1)S(1)} %collective-permute-done.18), channel_id=1, source_target_pairs={{0,1},{1,0},{2,3},{3,2},{4,5},{5,4},{6,7},{7,6},{8,9},{9,8},{10,11... | collective-permute-start | bytes 393224 | tf_op jit(solution)/shard_map/ppermute | solution.py:21
  115.5 22.6 %collective-permute-start.20 = (f16[128,512]{1,0:T(8,128)(2,1)S(1)}, f16[128,512]{1,0:T(8,128)(2,1)S(1)}, u32[]{:S(2)}, u32[]{:S(2)}) collective-permute-start(f16[128,512]{1,0:T(8,128)(2,1)S(1)} %collective-permute-done.18), channel_id=1, source_target_pairs={{0,2},{1,3},{2,0},{3,1},{4,6},{5,7},{6,4},{7,5},{8,10},{9,11},{10,... | collective-permute-start | bytes 393224 | tf_op jit(solution)/shard_map/ppermute | solution.py:21
  135.5 6.0 %collective-permute-start.24 = (f16[128,512]{1,0:T(8,128)(2,1)S(1)}, f16[128,512]{1,0:T(8,128)(2,1)S(1)}, u32[]{:S(2)}, u32[]{:S(2)}) collective-permute-start(f16[128,512]{1,0:T(8,128)(2,1)S(1)} %collective-permute-done.22), channel_id=1, source_target_pairs={{0,2},{1,3},{2,0},{3,1},{4,6},{5,7},{6,4},{7,5},{8,10},{9,11},{10,... | collective-permute-start | bytes 393224 | tf_op jit(solution)/shard_map/ppermute | solution.py:21
  137.1 5.8 %collective-permute-start.28 = (f16[128,512]{1,0:T(8,128)(2,1)S(1)}, f16[128,512]{1,0:T(8,128)(2,1)S(1)}, u32[]{:S(2)}, u32[]{:S(2)}) collective-permute-start(f16[128,512]{1,0:T(8,128)(2,1)S(1)} %collective-permute-done.26), channel_id=1, source_target_pairs={{0,2},{1,3},{2,0},{3,1},{4,6},{5,7},{6,4},{7,5},{8,10},{9,11},{10,... | collective-permute-start | bytes 393224 | tf_op jit(solution)/shard_map/ppermute | solution.py:21
  137.6 12.7 %collective-permute-start.23 = (f16[128,512]{1,0:T(8,128)(2,1)S(1)}, f16[128,512]{1,0:T(8,128)(2,1)S(1)}, u32[]{:S(2)}, u32[]{:S(2)}) collective-permute-start(f16[128,512]{1,0:T(8,128)(2,1)S(1)} %collective-permute-done.22), channel_id=1, source_target_pairs={{0,1},{1,0},{2,3},{3,2},{4,5},{5,4},{6,7},{7,6},{8,9},{9,8},{10,11... | collective-permute-start | bytes 393224 | tf_op jit(solution)/shard_map/ppermute | solution.py:21
  137.6 13.4 %collective-permute-start.27 = (f16[128,512]{1,0:T(8,128)(2,1)S(1)}, f16[128,512]{1,0:T(8,128)(2,1)S(1)}, u32[]{:S(2)}, u32[]{:S(2)}) collective-permute-start(f16[128,512]{1,0:T(8,128)(2,1)S(1)} %collective-permute-done.26), channel_id=1, source_target_pairs={{0,1},{1,0},{2,3},{3,2},{4,5},{5,4},{6,7},{7,6},{8,9},{9,8},{10,11... | collective-permute-start | bytes 393224 | tf_op jit(solution)/shard_map/ppermute | solution.py:21
  138.1 13.7 %collective-permute-start.21 = (f16[128,512]{1,0:T(8,128)(2,1)S(1)}, f16[128,512]{1,0:T(8,128)(2,1)S(1)}, u32[]{:S(2)}, u32[]{:S(2)}) collective-permute-start(f16[128,512]{1,0:T(8,128)(2,1)S(1)} %collective-permute-done.20), channel_id=1, source_target_pairs={{0,1},{1,0},{2,3},{3,2},{4,5},{5,4},{6,7},{7,6},{8,9},{9,8},{10,11... | collective-permute-start | bytes 393224 | tf_op jit(solution)/shard_map/ppermute | solution.py:21
  141.5 11.0 %collective-permute-start.25 = (f16[128,512]{1,0:T(8,128)(2,1)S(1)}, f16[128,512]{1,0:T(8,128)(2,1)S(1)}, u32[]{:S(2)}, u32[]{:S(2)}) collective-permute-start(f16[128,512]{1,0:T(8,128)(2,1)S(1)} %collective-permute-done.24), channel_id=1, source_target_pairs={{0,1},{1,0},{2,3},{3,2},{4,5},{5,4},{6,7},{7,6},{8,9},{9,8},{10,11... | collective-permute-start | bytes 393224 | tf_op jit(solution)/shard_map/ppermute | solution.py:21
  142.9 10.3 %collective-permute-start.29 = (f16[128,512]{1,0:T(8,128)(2,1)S(1)}, f16[128,512]{1,0:T(8,128)(2,1)S(1)}, u32[]{:S(2)}, u32[]{:S(2)}) collective-permute-start(f16[128,512]{1,0:T(8,128)(2,1)S(1)} %collective-permute-done.28), channel_id=1, source_target_pairs={{0,1},{1,0},{2,3},{3,2},{4,5},{5,4},{6,7},{7,6},{8,9},{9,8},{10,11... | collective-permute-start | bytes 393224 | tf_op jit(solution)/shard_map/ppermute | solution.py:21
  163.6 14.3 %collective-permute-start.30 = (f32[256,512]{1,0:T(8,128)S(1)}, f32[256,512]{1,0:T(8,128)S(1)}, u32[]{:S(2)}, u32[]{:S(2)}) collective-permute-start(f32[256,512]{1,0:T(8,128)S(1)} %get-tuple-element.28), channel_id=1, source_target_pairs={{0,16},{16,0},{1,17},{17,1},{2,18},{18,2},{3,19},{19,3},{4,20},{20... | collective-permute-start | bytes 1572872 | tf_op jit(solution)/shard_map/ppermute | solution.py:21
  180.8 5.5 %copy-start.5 = (f32[256,512]{1,0:T(8,128)S(1)}, f32[256,512]{1,0:T(8,128)}, u32[]{:S(2)}) copy-start(f32[256,512]{1,0:T(8,128)} %get-tuple-element.20.refs_0_) | copy-start | bytes 1572868
  182.7 30.8 %all-to-all-start.2 = ((f32[32,16,512]{2,1,0:T(8,128)}), f32[32,16,512]{2,1,0:T(8,128)S(1)}, u32[]{:S(2)}, u32[]{:S(2)}) async-start(f32[32,16,512]{2,1,0:T(8,128)} %broadcast_in_dim.11), calls=%async_computation.2 | async-start | bytes 2097152 | tf_op jit(solution)/shard_map/all_to_all | solution.py:289
  186.4 24.4 %collective-permute-start.31 = (f32[256,512]{1,0:T(8,128)S(1)}, f32[256,512]{1,0:T(8,128)S(1)}, u32[]{:S(2)}, u32[]{:S(2)}) collective-permute-start(f32[256,512]{1,0:T(8,128)S(1)} %copy-done.5), channel_id=1, source_target_pairs={{0,16},{16,0},{1,17},{17,1},{2,18},{18,2},{3,19},{19,3},{4,20},{20... | collective-permute-start | bytes 1572872 | tf_op jit(solution)/shard_map/ppermute | solution.py:21
  (13 other events, 17.5 us)

commit v2 on v1

--- a/solution.py
+++ b/solution.py
@@ -21,18 +21,23 @@
     return lax.ppermute(value, axis, [(i, i ^ mask) for i in range(lax.axis_size(axis))])
 
 
-def gather_xor(value, axis):
-    amount = lax.axis_size(axis)
-    top = amount // 4
-    slots = {0: value}
-    for step in (1, 2, 3):
-        slots[step * top] = swap(value, axis, step * top)
+def gather_far(value, axis):
+    top = lax.axis_size(axis) // 4
+    return [value] + [swap(value, axis, step * top) for step in (1, 2, 3)]
+
+
+def gather_even(far, axis):
+    top = lax.axis_size(axis) // 4
+    slots = {step * top: far[step] for step in range(4)}
     for mask in range(2, top, 2):
         for step in range(4):
             slots[step * top + mask] = swap(slots[step * top], axis, mask)
-    for mask in range(0, amount, 2):
-        slots[mask + 1] = swap(slots[mask], axis, 1)
-    return [slots[k] for k in range(amount)]
+    return [slots[k] for k in range(0, 4 * top, 2)]
+
+
+def gather_xor(far, axis):
+    pairs = [(slot, swap(slot, axis, 1)) for slot in gather_even(far, axis)]
+    return [slot for pair in pairs for slot in pair]
 
 
 def split3(value):
@@ -44,8 +49,8 @@
 
 
 def attention_kernel(slots, place_ref, order_ref, query_ref, *refs):
-    key_refs, mass_ref = refs[:slots], refs[slots]
-    keys, bias, scores, mixed = refs[slots + 1 :]
+    key_refs, predicted_ref, reach_ref, mass_ref = refs[:slots], *refs[slots : slots + 3]
+    keys, bias, scores, mixed = refs[slots + 3 :]
     rows = key_refs[0].shape[0]
     total = rows * slots
     pairs = query_ref.shape[0]
@@ -62,6 +67,12 @@
             at = jnp.where(index // BLK == b, order_ref[owner * blocks + b], at)
         return at * BLK + index % BLK
 
+    mass_ref[...] = jnp.zeros_like(mass_ref)
+    mass_ref[me, KEY_VALUE_HEADS:, :] = predicted_ref[...]
+    beside = mass_ref.shape[0] - slots
+    spot = lax.broadcasted_iota(jnp.int32, (beside, 8, rows), 0) * 8
+    spot = spot + lax.broadcasted_iota(jnp.int32, (beside, 8, rows), 1)
+    mass_ref[slots:] = jnp.where(spot == me, reach_ref[...][None], 0.0)
     query_pos = pos_of(me, lax.broadcasted_iota(jnp.int32, (rows, rows), 1))
     key_index = lax.broadcasted_iota(jnp.int32, (rows, rows), 0)
     for k in range(slots):
@@ -114,7 +125,7 @@
     lax.fori_loop(0, KEY_VALUE_HEADS, visit_head, 0)
 
 
-def attention_mass(place, block_order, queries, key_slots):
+def attention_mass(place, block_order, queries, key_slots, predicted, reach):
     slots = len(key_slots)
     rows = queries.shape[0]
     heads = queries.shape[1] // HEAD_SIZE
@@ -124,8 +135,8 @@
     arranged = arranged.reshape(heads // fold, fold * rows, HEAD_SIZE)
     return pl.pallas_call(
         functools.partial(attention_kernel, slots),
-        out_shape=jax.ShapeDtypeStruct((slots, KEY_VALUE_HEADS, rows), jnp.float32),
-        in_specs=[SMEM, SMEM, VMEM] + [VMEM] * slots,
+        out_shape=jax.ShapeDtypeStruct((slots + slots // 8, 8, rows), jnp.float32),
+        in_specs=[SMEM, SMEM, VMEM] + [VMEM] * (slots + 2),
         out_specs=VMEM,
         scratch_shapes=[
             pltpu.VMEM((KEY_VALUE_HEADS, total, HEAD_SIZE), jnp.bfloat16),
@@ -139,21 +150,26 @@
             bytes_accessed=2 * rows * heads * HEAD_SIZE,
             transcendentals=rows * total * heads,
         ),
-    )(place, block_order, arranged, *key_slots)
-
-
-def gradient_kernel(slots, dp, place_ref, message_ref, columns_ref, output_ref, hidden_ref, *refs):
-    slope_refs = refs[:slots]
-    grad_ref, mass_ref, small_ref = refs[slots : slots + 3]
-    out_grad, slope, wide, grad = refs[slots + 3 :]
+    )(place, block_order, arranged, *key_slots, predicted, reach)
+
+
+def gradient_kernel(slots, dp, place_ref, columns_ref, output_ref, hidden_ref, *refs):
+    message_refs, fall_refs = refs[:4], refs[4:6]
+    grad_ref, mass_ref, small_ref = refs[6:9]
+    out_grad, slope, wide, grad, reaches = refs[9:]
     me, part = place_ref[0], place_ref[1]
     rows = hidden_ref.shape[0]
     total = rows * slots
     units = hidden_ref.shape[1]
-    mass = jnp.sum(message_ref[:, :slots], axis=0)
+    message = (message_refs[0][...] + message_refs[1][...]) + (
+        message_refs[2][...] + message_refs[3][...]
+    )
+    for k in range(slots):
+        reaches[k] = message[slots + k // 8, k % 8 : k % 8 + 1, :]
+    mass = message[:slots, :KEY_VALUE_HEADS]
     out_grad[...] = mass
     mass_ref[...] = out_grad[me]
-    residue = message_ref[:, slots] - jnp.log(1.0 + mass)
+    residue = message[:slots, KEY_VALUE_HEADS:] - jnp.log(1.0 + mass)
     out_grad[...] = residue / total
     loss_sum = jnp.sum(residue * residue) * (0.5 / total)
     grad_bias = jnp.sum(jnp.sum(out_grad[...], axis=0), axis=1, keepdims=True)
@@ -162,14 +178,14 @@
     first_bias = jnp.zeros((8, units), jnp.float32)
     for k in range(slots):
         owner = me ^ k
-        scaled = out_grad[owner] * message_ref[owner, slots + 1]
+        scaled = out_grad[owner] * reaches[owner]
         back = lax.dot_general(
             jnp.concatenate(split3(scaled), axis=0),
             output_three,
             (((0,), (0,)), ((), ())),
             preferred_element_type=jnp.float32,
         )
-        fall = back * slope_refs[k][...].astype(jnp.float32)
+        fall = back * fall_refs[k % 2][k // 2]
         first_bias = first_bias + jnp.sum(fall.reshape(rows // 8, 8, units), axis=0)
         slope[pl.ds(pl.multiple_of(owner * rows, rows), rows), :] = fall.astype(jnp.bfloat16)
         wide[:, k * rows : (k + 1) * rows] = columns_ref[k]
@@ -192,8 +208,8 @@
     small_ref[pl.ds(2 * heads + 2, 6), :] = jnp.zeros((6, units), jnp.float32)
 
 
-def gradient(place, message, columns, output_weight, hidden, slope_slots, dp):
-    slots = len(slope_slots)
+def gradient(place, messages, columns, output_weight, hidden, falls, dp):
+    slots = 2 * falls[0].shape[0]
     rows, units = hidden.shape
     depth = columns.shape[1]
     return pl.pallas_call(
@@ -203,16 +219,17 @@
             jax.ShapeDtypeStruct((KEY_VALUE_HEADS, rows), jnp.float32),
             jax.ShapeDtypeStruct((16, units), jnp.float32),
         ),
-        in_specs=[SMEM] + [VMEM] * (4 + slots),
+        in_specs=[SMEM] + [VMEM] * 9,
         out_specs=(VMEM, VMEM, VMEM),
         scratch_shapes=[
             pltpu.VMEM((slots, KEY_VALUE_HEADS, rows), jnp.float32),
             pltpu.VMEM((slots * rows, units), jnp.bfloat16),
             pltpu.VMEM((depth, slots * rows), jnp.bfloat16),
             pltpu.VMEM((depth, units), jnp.float32),
+            pltpu.VMEM((slots, 1, rows), jnp.float32),
         ],
         compiler_params=pltpu.CompilerParams(vmem_limit_bytes=VMEM_LIMIT),
-    )(place, message, columns, output_weight, hidden, *slope_slots)
+    )(place, columns, output_weight, hidden, *messages, *falls)
 
 
 def square_kernel(parts, small_ref, *refs):
@@ -305,7 +322,7 @@
     place = jnp.stack([lax.axis_index("seq"), lax.axis_index("dp")]).astype(jnp.int32)
     tokens = hidden_states.reshape(rows, model)
 
-    key_slots = gather_xor(rotated_key_rows.reshape(rows, -1), "seq")
+    key_slots = gather_xor(gather_far(rotated_key_rows.reshape(rows, -1), "seq"), "seq")
     columns = lax.all_to_all(
         jnp.transpose(tokens).reshape(seq, model // seq, rows), "seq", 0, 0, tiled=True
     )
@@ -321,16 +338,22 @@
     )
     fall = gate * (1.0 + pre_act * (1.0 - gate))
     reach = jnp.maximum(jnp.max(jnp.abs(fall), axis=1), 1e-30)
-    fall_slots = gather_xor((fall / reach[:, None]).astype(jnp.float16), "seq")
-
-    mass = attention_mass(place, block_order, queries.reshape(rows, -1), key_slots)
-    reach_rows = jnp.broadcast_to(reach[None, None, :], (1,) + predicted.shape)
-    message = jnp.concatenate([mass, predicted[None], reach_rows], axis=0)
-    message = send_all(message, "seq", seq)
-
-    slope_slots = [fall_slot.astype(jnp.float32) for fall_slot in fall_slots]
+    fall_far = gather_far((fall / reach[:, None]).astype(jnp.float16), "seq")
+
+    message = attention_mass(
+        place, block_order, queries.reshape(rows, -1), key_slots, predicted, reach[None]
+    )
+    message, *fall_far = lax.optimization_barrier((message, *fall_far))
+    falls = jnp.stack(gather_even(fall_far, "seq"))
+    falls = [falls.astype(jnp.float32), swap(falls, "seq", 1).astype(jnp.float32)]
+    mask = 1
+    while mask < seq // 4:
+        message = message + swap(message, "seq", mask)
+        mask *= 2
+    messages = gather_far(message, "seq")
+
     grads, own_mass, small = gradient(
-        place, message, columns, output_weight, hidden, slope_slots, dp
+        place, messages, columns, output_weight, hidden, falls, dp
     )
     parts = [grads[0]] + [swap(grads[k], "dp", k) for k in range(1, dp)]
     total, small = squares(small, parts)

time: 219 us -> 169 us (0.77)
  waiting for transfers between devices: 113 us -> 68.9 us
  other arithmetic: 13.3 us -> 4.59 us
  starting transfers between devices: 38.4 us -> 42.7 us
    ppermute x32 -> x30, waiting for transfers between devices: 97.1 us -> 66.1 us  [swap(): lax.ppermute(value, axis, [(i, i ^ mask) for i in range(lax.axis_size(axi...]
    all_to_all x2 -> x1, waiting for transfers between devices: 15.8 us -> 2.76 us  [send_all(): return lax.all_to_all(copies, axes, 0, 0, tiled=True)]
    convert_element_type x16 -> x3, other arithmetic: 11.9 us -> 3.45 us  [the longest x1 1.66 us: per_device(): swap(falls, 'seq', 1).astype(jnp.float32)]
    ppermute x32 -> x30, starting transfers between devices: 25.2 us -> 32 us  [swap(): lax.ppermute(value, axis, [(i, i ^ mask) for i in range(lax.axis_size(axi...]
    all_to_all x2 -> x1, starting transfers between devices: 8.72 us -> 5.46 us  [send_all(): return lax.all_to_all(copies, axes, 0, 0, tiled=True)]
    unnamed x53 -> x64, local copies, waits for them, and re-layouts: 5.66 us -> 3.66 us
  transfers between devices with their start and end apart: 35 -> 32, of which waited for: 13 -> 14; matrix products, arithmetic and copies ran while one was open for 10% -> 10% of each run, Pallas kernels for 0% -> 12%
where the time goes in v2:
time: 169 us
  waiting for transfers between devices  68.9 us (41%)
  starting transfers between devices  42.7 us (25%)
  Pallas kernels  31.7 us (19%)
  local copies, waits for them, and re-layouts  14.4 us (9%)
  matrix products  5.6 us (3%)
  other arithmetic  4.59 us (3%)
    ppermute x30, waiting for transfers between devices, swap(): lax.ppermute(value, axis, [(i, i ^ mask) for i in range(lax.axis_size(axi...  66.1 us
    ppermute x30, starting transfers between devices, swap(): lax.ppermute(value, axis, [(i, i ^ mask) for i in range(lax.axis_size(axi...  32 us
    pallas_call x1, Pallas kernels, attention_mass(): pl.pallas_call(functools.partial(attention_kernel, slots), out_shape=jax....  20.8 us
    pallas_call x1, Pallas kernels, gradient(): pl.pallas_call(functools.partial(gradient_kernel, slots, dp), out_shape=(...  6.16 us
    all_to_all x1, starting transfers between devices, send_all(): return lax.all_to_all(copies, axes, 0, 0, tiled=True)  5.46 us
    all_to_all x1, starting transfers between devices, per_device(): lax.all_to_all(jnp.transpose(tokens).reshape(seq, model // seq, rows), 's...  5.17 us
    dot_general x1, matrix products, per_device(): jnp.dot(tokens, first_weight, preferred_element_type=jnp.float32)  4.88 us
    transpose x1, local copies, waits for them, and re-layouts, per_device(): jnp.transpose(tokens).reshape(seq, model // seq, rows)  4.08 us
  transfers between devices with their start and end apart: 32, of which 14 were waited for; matrix products, arithmetic and copies ran while one was open for 10% of the time, Pallas kernels for 12%

profile of v2, /device:TPU:0, one launch (start us, length us, event | category | flops | bytes accessed | tf_op | source)
XLA Modules:
  0.0 168.9 jit_solution(11613837575950779687)
XLA Ops:
  1.1 2.6 %collective-permute-start.1 = (bf16[128,512]{1,0:T(8,128)(2,1)}, bf16[128,512]{1,0:T(8,128)(2,1)S(1)}, u32[]{:S(2)}, u32[]{:S(2)}) collective-permute-start(bf16[128,512]{1,0:T(8,128)(2,1)} %bitcast.56), channel_id=1, source_target_pairs={{0,2},{1,3},{2,0},{3,1},{4,6},{5,7},{6,4},{7,5},{8,10},{9,11},{10,... | collective-permute-start | bytes 393224 | tf_op jit(solution)/shard_map/ppermute | solution.py:21
  3.7 1.6 collective-permute-start.3
  5.3 2.6 %collective-permute-start.7 = (bf16[128,512]{1,0:T(8,128)(2,1)}, bf16[128,512]{1,0:T(8,128)(2,1)}, u32[]{:S(2)}, u32[]{:S(2)}) collective-permute-start(bf16[128,512]{1,0:T(8,128)(2,1)} %bitcast.58), channel_id=1, source_target_pairs={{0,8},{1,9},{2,10},{3,11},{4,12},{5,13},{6,14},{7,15},{8,0},{9,1},... | collective-permute-start | bytes 393224 | tf_op jit(solution)/shard_map/ppermute | solution.py:21
  8.1 4.1 %copy.16 = bf16[8192,128]{1,0:T(8,128)(2,1)} copy(bf16[8192,128]{0,1:T(8,128)(2,1)} %bitcast.50) | data formatting | bytes 4194304 | tf_op jit(solution)/shard_map/transpose | solution.py:327
  12.2 5.2 %all-to-all-start = ((bf16[16,512,128]{2,1,0:T(8,128)(2,1)}), bf16[16,512,128]{2,1,0:T(8,128)(2,1)}, u32[]{:S(2)}, u32[]{:S(2)}) async-start(bf16[16,512,128]{2,1,0:T(8,128)(2,1)} %bitcast.51), calls=%async_computation | async-start | bytes 4194304 | tf_op jit(solution)/shard_map/all_to_all | solution.py:326
  17.4 4.9 %abs_reduce_fusion = (f32[128]{0:T(128)S(1)}, f32[128,512]{1,0:T(8,128)S(1)}) fusion(f32[512]{0:T(512)S(1)} %copy-done.13, bf16[8192,512]{1,0:T(8,128)(2,1)} %param.12, bf16[1,128,8192]{2,1,0:T(8,128)(2,1)S(1)} %copy-done), kind=kOutput, calls=%fused_computation.8 | convolution fusion | flops 1074397056 | bytes 10750464 | tf_op jit(solution)/shard_map/dot_general | solution.py:330
  23.2 1.7 collective-permute-start.5
  25.3 1.7 collective-permute-start.13
  27.8 8.3 %collective-permute-done.5.refs_6_ = bf16[128,512]{1,0:T(8,128)(2,1)S(1)} collective-permute-done((bf16[128,512]{1,0:T(8,128)(2,1)S(1)}, bf16[128,512]{1,0:T(8,128)(2,1)S(1)}, u32[]{:S(2)}, u32[]{:S(2)}) %collective-permute-start.5) | collective-permute-done | bytes 131104 | tf_op jit(solution)/shard_map/ppermute | solution.py:21
  36.0 6.6 %collective-permute-done.9.refs_10_ = bf16[128,512]{1,0:T(8,128)(2,1)S(1)} collective-permute-done((bf16[128,512]{1,0:T(8,128)(2,1)}, bf16[128,512]{1,0:T(8,128)(2,1)S(1)}, u32[]{:S(2)}, u32[]{:S(2)}) %collective-permute-start.9) | collective-permute-done | bytes 131104 | tf_op jit(solution)/shard_map/ppermute | solution.py:21
  42.6 3.1 %collective-permute-done.13.refs_14_ = bf16[128,512]{1,0:T(8,128)(2,1)S(1)} collective-permute-done((bf16[128,512]{1,0:T(8,128)(2,1)}, bf16[128,512]{1,0:T(8,128)(2,1)S(1)}, u32[]{:S(2)}, u32[]{:S(2)}) %collective-permute-start.13) | collective-permute-done | bytes 131104 | tf_op jit(solution)/shard_map/ppermute | solution.py:21
  45.8 0.7 fusion.5.refs_16_
  46.8 1.4 copy.17
  48.2 0.6 pad_add_fusion.place_ref
  48.8 3.8 %collective-permute-start.16 = (f16[128,512]{1,0:T(8,128)(2,1)S(1)}, f16[128,512]{1,0:T(8,128)(2,1)S(1)}, u32[]{:S(2)}, u32[]{:S(2)}) collective-permute-start(f16[128,512]{1,0:T(8,128)(2,1)S(1)} %get-tuple-element.22), channel_id=1, source_target_pairs={{0,8},{1,9},{2,10},{3,11},{4,12},{5,13},{6,14},{7,15},{8,0},{9,1},... | collective-permute-start | bytes 393224 | tf_op jit(solution)/shard_map/ppermute | solution.py:21
  52.6 0.6 collective-permute-start.17
  53.3 0.6 copy-done.25
  53.9 20.8 %shard_map.127 = f32[18,8,128]{2,1,0:T(8,128)} custom-call(s32[2]{0:T(128)} %pad_add_fusion.place_ref, s32[32]{0:T(128)} %order_ref.1, bf16[16,256,128]{2,1,0:T(8,128)(2,1)} %bitcast.54, bf16[128,512]{1,0:T(8,128)(2,1)} %bitcast.60, bf16[128,512]{1,0:T(8,128)(2,1)} %copy-done.14, bf16[128,512]{1,0:T(8,128)(2,1)} %copy-done.15, bf16[128,512]{1,0:T(8,128)(2,1)} %copy-done.19, ...), custom_call_target="tpu_custom_call" | custom-call | flops 2147483648 | bytes 1048576 | tf_op jit(solution)/shard_map/pallas_call | solution.py:136
  74.7 0.6 collective-permute-done.16
  75.3 1.6 collective-permute-start.23
  77.3 1.6 collective-permute-start.25
  79.4 2.4 %collective-permute-done.23 = f16[128,512]{1,0:T(8,128)(2,1)S(1)} collective-permute-done((f16[128,512]{1,0:T(8,128)(2,1)S(1)}, f16[128,512]{1,0:T(8,128)(2,1)S(1)}, u32[]{:S(2)}, u32[]{:S(2)}) %collective-permute-start.23) | collective-permute-done | bytes 131104 | tf_op jit(solution)/shard_map/ppermute | solution.py:21
  81.8 2.7 %collective-permute-done.24 = f16[128,512]{1,0:T(8,128)(2,1)S(1)} collective-permute-done((f16[128,512]{1,0:T(8,128)(2,1)S(1)}, f16[128,512]{1,0:T(8,128)(2,1)S(1)}, u32[]{:S(2)}, u32[]{:S(2)}) %collective-permute-start.24) | collective-permute-done | bytes 131104 | tf_op jit(solution)/shard_map/ppermute | solution.py:21
  84.6 2.3 %collective-permute-done.25 = f16[128,512]{1,0:T(8,128)(2,1)S(1)} collective-permute-done((f16[128,512]{1,0:T(8,128)(2,1)S(1)}, f16[128,512]{1,0:T(8,128)(2,1)S(1)}, u32[]{:S(2)}, u32[]{:S(2)}) %collective-permute-start.25) | collective-permute-done | bytes 131104 | tf_op jit(solution)/shard_map/ppermute | solution.py:21
  87.0 1.3 collective-permute-done.26
  88.9 2.3 %collective-permute-done.18 = f32[18,8,128]{2,1,0:T(8,128)S(1)} collective-permute-done((f32[18,8,128]{2,1,0:T(8,128)S(1)}, f32[18,8,128]{2,1,0:T(8,128)S(1)}, u32[]{:S(2)}, u32[]{:S(2)}) %collective-permute-start.18) | collective-permute-done | bytes 73760 | tf_op jit(solution)/shard_map/ppermute | solution.py:21
  91.2 1.7 collective-permute-start.19
  92.8 2.8 %collective-permute-done.19 = f32[18,8,128]{2,1,0:T(8,128)S(1)} collective-permute-done((f32[18,8,128]{2,1,0:T(8,128)S(1)}, f32[18,8,128]{2,1,0:T(8,128)S(1)}, u32[]{:S(2)}, u32[]{:S(2)}) %collective-permute-start.19) | collective-permute-done | bytes 73760 | tf_op jit(solution)/shard_map/ppermute | solution.py:21
  95.6 3.4 %collective-permute-start.20 = (f32[18,8,128]{2,1,0:T(8,128)S(1)}, f32[18,8,128]{2,1,0:T(8,128)S(1)}, u32[]{:S(2)}, u32[]{:S(2)}) collective-permute-start(f32[18,8,128]{2,1,0:T(8,128)S(1)} %add.38.refs_0_), channel_id=1, source_target_pairs={{0,4},{1,5},{2,6},{3,7},{4,0},{5,1},{6,2},{7,3},{8,12},{9,13},{10,... | collective-permute-start | bytes 221192 | tf_op jit(solution)/shard_map/ppermute | solution.py:21
  99.5 2.0 %collective-permute-start.22 = (f32[18,8,128]{2,1,0:T(8,128)S(1)}, f32[18,8,128]{2,1,0:T(8,128)S(1)}, u32[]{:S(2)}, u32[]{:S(2)}) collective-permute-start(f32[18,8,128]{2,1,0:T(8,128)S(1)} %add.38.refs_0_), channel_id=1, source_target_pairs={{0,12},{1,13},{2,14},{3,15},{4,8},{5,9},{6,10},{7,11},{8,4},{9,5},... | collective-permute-start | bytes 221192 | tf_op jit(solution)/shard_map/ppermute | solution.py:21
  101.5 1.6 convert_element_type.14.refs_4_
  103.1 1.7 convert_element_type.15.refs_5_
  104.8 1.8 %collective-permute-done.21.refs_2_ = f32[18,8,128]{2,1,0:T(8,128)S(1)} collective-permute-done((f32[18,8,128]{2,1,0:T(8,128)S(1)}, f32[18,8,128]{2,1,0:T(8,128)S(1)}, u32[]{:S(2)}, u32[]{:S(2)}) %collective-permute-start.21) | collective-permute-done | bytes 73760 | tf_op jit(solution)/shard_map/ppermute | solution.py:21
  106.6 0.6 copy-done.10
  107.2 6.2 %shard_map.128 = (f32[2,256,512]{2,1,0:T(8,128)}, f32[4,128]{1,0:T(4,128)}, f32[16,512]{1,0:T(8,128)}) custom-call(s32[2]{0:T(128)} %pad_add_fusion.place_ref, bf16[16,512,128]{2,1,0:T(8,128)(2,1)} %all-to-all-done.columns_ref, bf16[4,512]{1,0:T(4,128)(2,1)} %output_ref.1, bf16[128,512]{1,0:T(8,128)(2,1)} %copy-done.5, f32[18,8,128]{2,1,0:T(8,128)} %copy-done.7, ...), custom_call_target="tpu_custom_call" | custom-call | tf_op jit(solution)/shard_map/pallas_call | solution.py:215
  113.4 2.1 %slice_bitcast_fusion = (f32[256,512]{1,0:T(8,128)S(1)}, f32[256,512]{1,0:T(8,128)}) fusion(f32[2,256,512]{2,1,0:T(8,128)} %get-tuple-element.28), kind=kLoop, calls=%fused_computation.5 | loop fusion | bytes 2097152 | tf_op jit(solution)/shard_map/squeeze | solution.py:358
  115.5 1.5 collective-permute-start.28
  117.0 9.4 %collective-permute-done.28.refs_1_ = f32[256,512]{1,0:T(8,128)S(1)} collective-permute-done((f32[256,512]{1,0:T(8,128)S(1)}, f32[256,512]{1,0:T(8,128)S(1)}, u32[]{:S(2)}, u32[]{:S(2)}) %collective-permute-start.28) | collective-permute-done | bytes 524320 | tf_op jit(solution)/shard_map/ppermute | solution.py:21
  126.4 0.8 copy-done.6
  127.2 2.1 %shard_map.129 = (f32[256,512]{1,0:T(8,128)}, f32[16,512]{1,0:T(8,128)}) custom-call(f32[16,512]{1,0:T(8,128)} %get-tuple-element.27.small_ref, f32[256,512]{1,0:T(8,128)} %get-tuple-element.37.refs_0_, f32[256,512]{1,0:T(8,128)} %copy-done.6), custom_call_target="tpu_custom_call" | custom-call | tf_op jit(solution)/shard_map/pallas_call | solution.py:249
  129.3 1.9 %broadcast_in_dim.2 = f32[32,16,512]{2,1,0:T(8,128)} broadcast(f32[16,512]{1,0:T(8,128)} %get-tuple-element.29), dimensions={1,2} | broadcast | bytes 1081344 | tf_op jit(solution)/shard_map/broadcast_in_dim | solution.py:305
  131.2 5.5 %all-to-all-start.1 = ((f32[32,16,512]{2,1,0:T(8,128)}), f32[32,16,512]{2,1,0:T(8,128)S(1)}, u32[]{:S(2)}, u32[]{:S(2)}) async-start(f32[32,16,512]{2,1,0:T(8,128)} %broadcast_in_dim.2), calls=%async_computation.1 | async-start | bytes 2097152 | tf_op jit(solution)/shard_map/all_to_all | solution.py:306
  136.7 1.8 %collective-permute-start.29 = (f32[256,512]{1,0:T(8,128)S(1)}, f32[256,512]{1,0:T(8,128)S(1)}, u32[]{:S(2)}, u32[]{:S(2)}) collective-permute-start(f32[256,512]{1,0:T(8,128)S(1)} %copy-done.3), channel_id=1, source_target_pairs={{0,16},{16,0},{1,17},{17,1},{2,18},{18,2},{3,19},{19,3},{4,20},{20... | collective-permute-start | bytes 1572872 | tf_op jit(solution)/shard_map/ppermute | solution.py:21
  138.5 22.6 %collective-permute-done.29.refs_1_ = f32[256,512]{1,0:T(8,128)S(1)} collective-permute-done((f32[256,512]{1,0:T(8,128)S(1)}, f32[256,512]{1,0:T(8,128)S(1)}, u32[]{:S(2)}, u32[]{:S(2)}) %collective-permute-start.29) | collective-permute-done | bytes 524320 | tf_op jit(solution)/shard_map/ppermute | solution.py:21
  161.1 2.8 %all-to-all-done.1.message_ref = f32[32,16,512]{2,1,0:T(8,128)S(1)} async-done(((f32[32,16,512]{2,1,0:T(8,128)}), f32[32,16,512]{2,1,0:T(8,128)S(1)}, u32[]{:S(2)}, u32[]{:S(2)}) %all-to-all-start.1) | async-done | bytes 1048608 | tf_op jit(solution)/shard_map/all_to_all | solution.py:306
  163.9 1.0 copy-done.1
  164.9 2.7 %shard_map.130 = (f32[512,512]{1,0:T(8,128)}, f32[4,512]{1,0:T(4,128)}, f32[1,512]{1,0:T(1,128)}, f32[4,128]{1,0:T(4,128)}, f32[1,128]{1,0:T(1,128)}) custom-call(s32[2]{0:T(128)} %pad_add_fusion.place_ref, f32[32,16,512]{2,1,0:T(8,128)} %copy-done.1, f32[256,512]{1,0:T(8,128)} %get-tuple-element.30.refs_0_, f32[256,512]{1,0:T(8,128)} %copy-done.4), custom_call_target="tpu_custom_call" | custom-call | tf_op jit(solution)/shard_map/pallas_call | solution.py:289
  167.6 1.3 slice_reduce_fusion
  (99 shorter events, 5.4 us)
Async XLA Ops:
  0.6 22.6 %collective-permute-start = (bf16[128,512]{1,0:T(8,128)(2,1)}, bf16[128,512]{1,0:T(8,128)(2,1)S(1)}, u32[]{:S(2)}, u32[]{:S(2)}) collective-permute-start(bf16[128,512]{1,0:T(8,128)(2,1)} %bitcast.55), channel_id=1, source_target_pairs={{0,1},{1,0},{2,3},{3,2},{4,5},{5,4},{6,7},{7,6},{8,9},{9,8},{10,11... | collective-permute-start | bytes 393224 | tf_op jit(solution)/shard_map/ppermute | solution.py:21
  1.1 23.8 %collective-permute-start.1 = (bf16[128,512]{1,0:T(8,128)(2,1)}, bf16[128,512]{1,0:T(8,128)(2,1)S(1)}, u32[]{:S(2)}, u32[]{:S(2)}) collective-permute-start(bf16[128,512]{1,0:T(8,128)(2,1)} %bitcast.56), channel_id=1, source_target_pairs={{0,2},{1,3},{2,0},{3,1},{4,6},{5,7},{6,4},{7,5},{8,10},{9,11},{10,... | collective-permute-start | bytes 393224 | tf_op jit(solution)/shard_map/ppermute | solution.py:21
  3.7 19.1 %collective-permute-start.3 = (bf16[128,512]{1,0:T(8,128)(2,1)}, bf16[128,512]{1,0:T(8,128)(2,1)S(1)}, u32[]{:S(2)}, u32[]{:S(2)}) collective-permute-start(bf16[128,512]{1,0:T(8,128)(2,1)} %bitcast.57), channel_id=1, source_target_pairs={{0,4},{1,5},{2,6},{3,7},{4,0},{5,1},{6,2},{7,3},{8,12},{9,13},{10,... | collective-permute-start | bytes 393224 | tf_op jit(solution)/shard_map/ppermute | solution.py:21
  5.3 19.7 %collective-permute-start.7 = (bf16[128,512]{1,0:T(8,128)(2,1)}, bf16[128,512]{1,0:T(8,128)(2,1)}, u32[]{:S(2)}, u32[]{:S(2)}) collective-permute-start(bf16[128,512]{1,0:T(8,128)(2,1)} %bitcast.58), channel_id=1, source_target_pairs={{0,8},{1,9},{2,10},{3,11},{4,12},{5,13},{6,14},{7,15},{8,0},{9,1},... | collective-permute-start | bytes 393224 | tf_op jit(solution)/shard_map/ppermute | solution.py:21
  7.9 17.4 %collective-permute-start.11 = (bf16[128,512]{1,0:T(8,128)(2,1)}, bf16[128,512]{1,0:T(8,128)(2,1)}, u32[]{:S(2)}, u32[]{:S(2)}) collective-permute-start(bf16[128,512]{1,0:T(8,128)(2,1)} %bitcast.59), channel_id=1, source_target_pairs={{0,12},{1,13},{2,14},{3,15},{4,8},{5,9},{6,10},{7,11},{8,4},{9,5},... | collective-permute-start | bytes 393224 | tf_op jit(solution)/shard_map/ppermute | solution.py:21
  12.2 5.2 %copy-start = (bf16[1,128,8192]{2,1,0:T(8,128)(2,1)S(1)}, bf16[1,128,8192]{2,1,0:T(8,128)(2,1)}, u32[]{:S(2)}) copy-start(bf16[1,128,8192]{2,1,0:T(8,128)(2,1)} %param.10) | copy-start | bytes 6291460
  12.2 5.2 %copy-start.13 = (f32[512]{0:T(512)S(1)}, f32[512]{0:T(512)}, u32[]{:S(2)}) copy-start(f32[512]{0:T(512)} %param.13) | copy-start | bytes 6148
  12.2 94.4 %all-to-all-start = ((bf16[16,512,128]{2,1,0:T(8,128)(2,1)}), bf16[16,512,128]{2,1,0:T(8,128)(2,1)}, u32[]{:S(2)}, u32[]{:S(2)}) async-start(bf16[16,512,128]{2,1,0:T(8,128)(2,1)} %bitcast.51), calls=%async_computation | async-start | bytes 4194304 | tf_op jit(solution)/shard_map/all_to_all | solution.py:326
  17.4 28.3 %copy-start.12 = (bf16[4,512]{1,0:T(4,128)(2,1)S(1)}, bf16[4,512]{1,0:T(4,128)(2,1)}, u32[]{:S(2)}) copy-start(bf16[4,512]{1,0:T(4,128)(2,1)} %output_ref.1) | copy-start | bytes 12292
  17.4 28.3 %copy-start.27 = (f32[4]{0:T(128)S(1)}, f32[4]{0:T(128)}, u32[]{:S(2)}) copy-start(f32[4]{0:T(128)} %param.15) | copy-start | bytes 52
  17.4 29.1 %copy-start.2 = (bf16[1,128,4096]{2,1,0:T(8,128)(2,1)S(1)}, bf16[1,128,4096]{2,1,0:T(8,128)(2,1)}, u32[]{:S(2)}) copy-start(bf16[1,128,4096]{2,1,0:T(8,128)(2,1)} %param.8) | copy-start | bytes 3145732
  22.9 25.3 %copy-start.16 = (bf16[128,512]{1,0:T(8,128)(2,1)}, bf16[128,512]{1,0:T(8,128)(2,1)S(1)}, u32[]{:S(2)}) copy-start(bf16[128,512]{1,0:T(8,128)(2,1)S(1)} %collective-permute-done.3.refs_4_) | copy-start | bytes 393220
  22.9 4.4 %collective-permute-start.4 = (bf16[128,512]{1,0:T(8,128)(2,1)S(1)}, bf16[128,512]{1,0:T(8,128)(2,1)S(1)}, u32[]{:S(2)}, u32[]{:S(2)}) collective-permute-start(bf16[128,512]{1,0:T(8,128)(2,1)S(1)} %collective-permute-done.3.refs_4_), channel_id=1, source_target_pairs={{0,1},{1,0},{2,3},{3,2},{4,5},{5,4},{6,7},{7,6},{8,9},{9,8},{10,11... | collective-permute-start | bytes 393224 | tf_op jit(solution)/shard_map/ppermute | solution.py:21
  23.2 24.9 %copy-start.14 = (bf16[128,512]{1,0:T(8,128)(2,1)}, bf16[128,512]{1,0:T(8,128)(2,1)S(1)}, u32[]{:S(2)}) copy-start(bf16[128,512]{1,0:T(8,128)(2,1)S(1)} %collective-permute-done.refs_1_) | copy-start | bytes 393220
  23.2 12.8 %collective-permute-start.5 = (bf16[128,512]{1,0:T(8,128)(2,1)S(1)}, bf16[128,512]{1,0:T(8,128)(2,1)S(1)}, u32[]{:S(2)}, u32[]{:S(2)}) collective-permute-start(bf16[128,512]{1,0:T(8,128)(2,1)S(1)} %collective-permute-done.3.refs_4_), channel_id=1, source_target_pairs={{0,2},{1,3},{2,0},{3,1},{4,6},{5,7},{6,4},{7,5},{8,10},{9,11},{10,... | collective-permute-start | bytes 393224 | tf_op jit(solution)/shard_map/ppermute | solution.py:21
  24.9 23.2 %copy-start.15 = (bf16[128,512]{1,0:T(8,128)(2,1)}, bf16[128,512]{1,0:T(8,128)(2,1)S(1)}, u32[]{:S(2)}) copy-start(bf16[128,512]{1,0:T(8,128)(2,1)S(1)} %collective-permute-done.1.refs_2_) | copy-start | bytes 393220
  24.9 2.3 %collective-permute-start.2 = (bf16[128,512]{1,0:T(8,128)(2,1)S(1)}, bf16[128,512]{1,0:T(8,128)(2,1)S(1)}, u32[]{:S(2)}, u32[]{:S(2)}) collective-permute-start(bf16[128,512]{1,0:T(8,128)(2,1)S(1)} %collective-permute-done.1.refs_2_), channel_id=1, source_target_pairs={{0,1},{1,0},{2,3},{3,2},{4,5},{5,4},{6,7},{7,6},{8,9},{9,8},{10,11... | collective-permute-start | bytes 393224 | tf_op jit(solution)/shard_map/ppermute | solution.py:21
  25.0 17.6 %collective-permute-start.9 = (bf16[128,512]{1,0:T(8,128)(2,1)}, bf16[128,512]{1,0:T(8,128)(2,1)S(1)}, u32[]{:S(2)}, u32[]{:S(2)}) collective-permute-start(bf16[128,512]{1,0:T(8,128)(2,1)} %collective-permute-done.7.refs_8_), channel_id=1, source_target_pairs={{0,2},{1,3},{2,0},{3,1},{4,6},{5,7},{6,4},{7,5},{8,10},{9,11},{10,... | collective-permute-start | bytes 393224 | tf_op jit(solution)/shard_map/ppermute | solution.py:21
  25.3 20.4 %collective-permute-start.13 = (bf16[128,512]{1,0:T(8,128)(2,1)}, bf16[128,512]{1,0:T(8,128)(2,1)S(1)}, u32[]{:S(2)}, u32[]{:S(2)}) collective-permute-start(bf16[128,512]{1,0:T(8,128)(2,1)} %collective-permute-done.11.refs_12_), channel_id=1, source_target_pairs={{0,2},{1,3},{2,0},{3,1},{4,6},{5,7},{6,4},{7,5},{8,10},{9,11},{10,... | collective-permute-start | bytes 393224 | tf_op jit(solution)/shard_map/ppermute | solution.py:21
  27.2 21.0 %copy-start.5 = (bf16[128,512]{1,0:T(8,128)(2,1)}, bf16[128,512]{1,0:T(8,128)(2,1)S(1)}, u32[]{:S(2)}) copy-start(bf16[128,512]{1,0:T(8,128)(2,1)S(1)} %get-tuple-element.39.hidden_ref) | copy-start | bytes 393220
  27.2 21.0 %copy-start.19 = (bf16[128,512]{1,0:T(8,128)(2,1)}, bf16[128,512]{1,0:T(8,128)(2,1)S(1)}, u32[]{:S(2)}) copy-start(bf16[128,512]{1,0:T(8,128)(2,1)S(1)} %collective-permute-done.2.refs_3_) | copy-start | bytes 393220
  27.2 21.6 %collective-permute-start.8 = (bf16[128,512]{1,0:T(8,128)(2,1)}, bf16[128,512]{1,0:T(8,128)(2,1)S(1)}, u32[]{:S(2)}, u32[]{:S(2)}) collective-permute-start(bf16[128,512]{1,0:T(8,128)(2,1)} %collective-permute-done.7.refs_8_), channel_id=1, source_target_pairs={{0,1},{1,0},{2,3},{3,2},{4,5},{5,4},{6,7},{7,6},{8,9},{9,8},{10,11... | collective-permute-start | bytes 393224 | tf_op jit(solution)/shard_map/ppermute | solution.py:21
  27.3 20.9 %copy-start.17 = (bf16[128,512]{1,0:T(8,128)(2,1)}, bf16[128,512]{1,0:T(8,128)(2,1)S(1)}, u32[]{:S(2)}) copy-start(bf16[128,512]{1,0:T(8,128)(2,1)S(1)} %collective-permute-done.4.refs_5_) | copy-start | bytes 393220
  27.3 21.5 %collective-permute-start.12 = (bf16[128,512]{1,0:T(8,128)(2,1)}, bf16[128,512]{1,0:T(8,128)(2,1)S(1)}, u32[]{:S(2)}, u32[]{:S(2)}) collective-permute-start(bf16[128,512]{1,0:T(8,128)(2,1)} %collective-permute-done.11.refs_12_), channel_id=1, source_target_pairs={{0,1},{1,0},{2,3},{3,2},{4,5},{5,4},{6,7},{7,6},{8,9},{9,8},{10,11... | collective-permute-start | bytes 393224 | tf_op jit(solution)/shard_map/ppermute | solution.py:21
  36.0 12.1 %copy-start.18 = (bf16[128,512]{1,0:T(8,128)(2,1)}, bf16[128,512]{1,0:T(8,128)(2,1)S(1)}, u32[]{:S(2)}) copy-start(bf16[128,512]{1,0:T(8,128)(2,1)S(1)} %collective-permute-done.5.refs_6_) | copy-start | bytes 393220
  36.0 16.6 %collective-permute-start.6 = (bf16[128,512]{1,0:T(8,128)(2,1)S(1)}, bf16[128,512]{1,0:T(8,128)(2,1)S(1)}, u32[]{:S(2)}, u32[]{:S(2)}) collective-permute-start(bf16[128,512]{1,0:T(8,128)(2,1)S(1)} %collective-permute-done.5.refs_6_), channel_id=1, source_target_pairs={{0,1},{1,0},{2,3},{3,2},{4,5},{5,4},{6,7},{7,6},{8,9},{9,8},{10,11... | collective-permute-start | bytes 393224 | tf_op jit(solution)/shard_map/ppermute | solution.py:21
  42.6 5.6 %copy-start.20 = (bf16[128,512]{1,0:T(8,128)(2,1)}, bf16[128,512]{1,0:T(8,128)(2,1)S(1)}, u32[]{:S(2)}) copy-start(bf16[128,512]{1,0:T(8,128)(2,1)S(1)} %collective-permute-done.9.refs_10_) | copy-start | bytes 393220
  42.6 10.6 %collective-permute-start.10 = (bf16[128,512]{1,0:T(8,128)(2,1)S(1)}, bf16[128,512]{1,0:T(8,128)(2,1)S(1)}, u32[]{:S(2)}, u32[]{:S(2)}) collective-permute-start(bf16[128,512]{1,0:T(8,128)(2,1)S(1)} %collective-permute-done.9.refs_10_), channel_id=1, source_target_pairs={{0,1},{1,0},{2,3},{3,2},{4,5},{5,4},{6,7},{7,6},{8,9},{9,8},{10,11... | collective-permute-start | bytes 393224 | tf_op jit(solution)/shard_map/ppermute | solution.py:21
  45.8 7.5 %collective-permute-start.14 = (bf16[128,512]{1,0:T(8,128)(2,1)S(1)}, bf16[128,512]{1,0:T(8,128)(2,1)S(1)}, u32[]{:S(2)}, u32[]{:S(2)}) collective-permute-start(bf16[128,512]{1,0:T(8,128)(2,1)S(1)} %collective-permute-done.13.refs_14_), channel_id=1, source_target_pairs={{0,1},{1,0},{2,3},{3,2},{4,5},{5,4},{6,7},{7,6},{8,9},{9,8},{10,11... | collective-permute-start | bytes 393224 | tf_op jit(solution)/shard_map/ppermute | solution.py:21
  48.8 25.9 %collective-permute-start.15 = (f16[128,512]{1,0:T(8,128)(2,1)S(1)}, f16[128,512]{1,0:T(8,128)(2,1)S(1)}, u32[]{:S(2)}, u32[]{:S(2)}) collective-permute-start(f16[128,512]{1,0:T(8,128)(2,1)S(1)} %get-tuple-element.22), channel_id=1, source_target_pairs={{0,4},{1,5},{2,6},{3,7},{4,0},{5,1},{6,2},{7,3},{8,12},{9,13},{10,... | collective-permute-start | bytes 393224 | tf_op jit(solution)/shard_map/ppermute | solution.py:21
  48.8 26.5 %collective-permute-start.16 = (f16[128,512]{1,0:T(8,128)(2,1)S(1)}, f16[128,512]{1,0:T(8,128)(2,1)S(1)}, u32[]{:S(2)}, u32[]{:S(2)}) collective-permute-start(f16[128,512]{1,0:T(8,128)(2,1)S(1)} %get-tuple-element.22), channel_id=1, source_target_pairs={{0,8},{1,9},{2,10},{3,11},{4,12},{5,13},{6,14},{7,15},{8,0},{9,1},... | collective-permute-start | bytes 393224 | tf_op jit(solution)/shard_map/ppermute | solution.py:21
  52.6 22.7 %collective-permute-start.17 = (f16[128,512]{1,0:T(8,128)(2,1)S(1)}, f16[128,512]{1,0:T(8,128)(2,1)S(1)}, u32[]{:S(2)}, u32[]{:S(2)}) collective-permute-start(f16[128,512]{1,0:T(8,128)(2,1)S(1)} %get-tuple-element.22), channel_id=1, source_target_pairs={{0,12},{1,13},{2,14},{3,15},{4,8},{5,9},{6,10},{7,11},{8,4},{9,5},... | collective-permute-start | bytes 393224 | tf_op jit(solution)/shard_map/ppermute | solution.py:21
  74.7 13.7 %copy-start.8 = (f32[18,8,128]{2,1,0:T(8,128)S(1)}, f32[18,8,128]{2,1,0:T(8,128)}, u32[]{:S(2)}) copy-start(f32[18,8,128]{2,1,0:T(8,128)} %shard_map.127) | copy-start | bytes 221188
  75.3 6.4 %collective-permute-start.23 = (f16[128,512]{1,0:T(8,128)(2,1)S(1)}, f16[128,512]{1,0:T(8,128)(2,1)S(1)}, u32[]{:S(2)}, u32[]{:S(2)}) collective-permute-start(f16[128,512]{1,0:T(8,128)(2,1)S(1)} %get-tuple-element.22), channel_id=1, source_target_pairs={{0,2},{1,3},{2,0},{3,1},{4,6},{5,7},{6,4},{7,5},{8,10},{9,11},{10,... | collective-permute-start | bytes 393224 | tf_op jit(solution)/shard_map/ppermute | solution.py:21
  76.9 7.6 %collective-permute-start.24 = (f16[128,512]{1,0:T(8,128)(2,1)S(1)}, f16[128,512]{1,0:T(8,128)(2,1)S(1)}, u32[]{:S(2)}, u32[]{:S(2)}) collective-permute-start(f16[128,512]{1,0:T(8,128)(2,1)S(1)} %collective-permute-done.15), channel_id=1, source_target_pairs={{0,2},{1,3},{2,0},{3,1},{4,6},{5,7},{6,4},{7,5},{8,10},{9,11},{10,... | collective-permute-start | bytes 393224 | tf_op jit(solution)/shard_map/ppermute | solution.py:21
  77.3 9.6 %collective-permute-start.25 = (f16[128,512]{1,0:T(8,128)(2,1)S(1)}, f16[128,512]{1,0:T(8,128)(2,1)S(1)}, u32[]{:S(2)}, u32[]{:S(2)}) collective-permute-start(f16[128,512]{1,0:T(8,128)(2,1)S(1)} %collective-permute-done.16), channel_id=1, source_target_pairs={{0,2},{1,3},{2,0},{3,1},{4,6},{5,7},{6,4},{7,5},{8,10},{9,11},{10,... | collective-permute-start | bytes 393224 | tf_op jit(solution)/shard_map/ppermute | solution.py:21
  78.9 9.4 %collective-permute-start.26 = (f16[128,512]{1,0:T(8,128)(2,1)S(1)}, f16[128,512]{1,0:T(8,128)(2,1)S(1)}, u32[]{:S(2)}, u32[]{:S(2)}) collective-permute-start(f16[128,512]{1,0:T(8,128)(2,1)S(1)} %collective-permute-done.17), channel_id=1, source_target_pairs={{0,2},{1,3},{2,0},{3,1},{4,6},{5,7},{6,4},{7,5},{8,10},{9,11},{10,... | collective-permute-start | bytes 393224 | tf_op jit(solution)/shard_map/ppermute | solution.py:21
  88.3 14.8 %collective-permute-start.27 = (f16[8,128,512]{2,1,0:T(8,128)(2,1)S(1)}, f16[8,128,512]{2,1,0:T(8,128)(2,1)S(1)}, u32[]{:S(2)}, u32[]{:S(2)}) collective-permute-start(f16[8,128,512]{2,1,0:T(8,128)(2,1)S(1)} %bitcast_dynamic-update-slice_fusion), channel_id=1, source_target_pairs={{0,1},{1,0},{2,3},{3,2},{4,5},{5,4},{6,7},{7,6},{8,9},{9,8},{10,11... | collective-permute-start | bytes 3145736 | tf_op jit(solution)/shard_map/ppermute | solution.py:21
  88.4 2.7 %collective-permute-start.18 = (f32[18,8,128]{2,1,0:T(8,128)S(1)}, f32[18,8,128]{2,1,0:T(8,128)S(1)}, u32[]{:S(2)}, u32[]{:S(2)}) collective-permute-start(f32[18,8,128]{2,1,0:T(8,128)S(1)} %copy-done.8), channel_id=1, source_target_pairs={{0,1},{1,0},{2,3},{3,2},{4,5},{5,4},{6,7},{7,6},{8,9},{9,8},{10,11... | collective-permute-start | bytes 221192 | tf_op jit(solution)/shard_map/ppermute | solution.py:21
  91.2 4.4 %collective-permute-start.19 = (f32[18,8,128]{2,1,0:T(8,128)S(1)}, f32[18,8,128]{2,1,0:T(8,128)S(1)}, u32[]{:S(2)}, u32[]{:S(2)}) collective-permute-start(f32[18,8,128]{2,1,0:T(8,128)S(1)} %add.37), channel_id=1, source_target_pairs={{0,2},{1,3},{2,0},{3,1},{4,6},{5,7},{6,4},{7,5},{8,10},{9,11},{10,... | collective-permute-start | bytes 221192 | tf_op jit(solution)/shard_map/ppermute | solution.py:21
  95.6 9.2 %copy-start.7 = (f32[18,8,128]{2,1,0:T(8,128)}, f32[18,8,128]{2,1,0:T(8,128)S(1)}, u32[]{:S(2)}) copy-start(f32[18,8,128]{2,1,0:T(8,128)S(1)} %add.38.refs_0_) | copy-start | bytes 221188
  95.6 9.2 %collective-permute-start.20 = (f32[18,8,128]{2,1,0:T(8,128)S(1)}, f32[18,8,128]{2,1,0:T(8,128)S(1)}, u32[]{:S(2)}, u32[]{:S(2)}) collective-permute-start(f32[18,8,128]{2,1,0:T(8,128)S(1)} %add.38.refs_0_), channel_id=1, source_target_pairs={{0,4},{1,5},{2,6},{3,7},{4,0},{5,1},{6,2},{7,3},{8,12},{9,13},{10,... | collective-permute-start | bytes 221192 | tf_op jit(solution)/shard_map/ppermute | solution.py:21
  99.1 7.5 %collective-permute-start.21 = (f32[18,8,128]{2,1,0:T(8,128)S(1)}, f32[18,8,128]{2,1,0:T(8,128)S(1)}, u32[]{:S(2)}, u32[]{:S(2)}) collective-permute-start(f32[18,8,128]{2,1,0:T(8,128)S(1)} %add.38.refs_0_), channel_id=1, source_target_pairs={{0,8},{1,9},{2,10},{3,11},{4,12},{5,13},{6,14},{7,15},{8,0},{9,1},... | collective-permute-start | bytes 221192 | tf_op jit(solution)/shard_map/ppermute | solution.py:21
  99.5 7.1 %collective-permute-start.22 = (f32[18,8,128]{2,1,0:T(8,128)S(1)}, f32[18,8,128]{2,1,0:T(8,128)S(1)}, u32[]{:S(2)}, u32[]{:S(2)}) collective-permute-start(f32[18,8,128]{2,1,0:T(8,128)S(1)} %add.38.refs_0_), channel_id=1, source_target_pairs={{0,12},{1,13},{2,14},{3,15},{4,8},{5,9},{6,10},{7,11},{8,4},{9,5},... | collective-permute-start | bytes 221192 | tf_op jit(solution)/shard_map/ppermute | solution.py:21
  115.5 10.9 %collective-permute-start.28 = (f32[256,512]{1,0:T(8,128)S(1)}, f32[256,512]{1,0:T(8,128)S(1)}, u32[]{:S(2)}, u32[]{:S(2)}) collective-permute-start(f32[256,512]{1,0:T(8,128)S(1)} %get-tuple-element.36), channel_id=1, source_target_pairs={{0,16},{16,0},{1,17},{17,1},{2,18},{18,2},{3,19},{19,3},{4,20},{20... | collective-permute-start | bytes 1572872 | tf_op jit(solution)/shard_map/ppermute | solution.py:21
  129.3 7.4 %copy-start.3 = (f32[256,512]{1,0:T(8,128)S(1)}, f32[256,512]{1,0:T(8,128)}, u32[]{:S(2)}) copy-start(f32[256,512]{1,0:T(8,128)} %get-tuple-element.30.refs_0_) | copy-start | bytes 1572868
  131.2 32.7 %all-to-all-start.1 = ((f32[32,16,512]{2,1,0:T(8,128)}), f32[32,16,512]{2,1,0:T(8,128)S(1)}, u32[]{:S(2)}, u32[]{:S(2)}) async-start(f32[32,16,512]{2,1,0:T(8,128)} %broadcast_in_dim.2), calls=%async_computation.1 | async-start | bytes 2097152 | tf_op jit(solution)/shard_map/all_to_all | solution.py:306
  136.7 24.4 %collective-permute-start.29 = (f32[256,512]{1,0:T(8,128)S(1)}, f32[256,512]{1,0:T(8,128)S(1)}, u32[]{:S(2)}, u32[]{:S(2)}) collective-permute-start(f32[256,512]{1,0:T(8,128)S(1)} %copy-done.3), channel_id=1, source_target_pairs={{0,16},{16,0},{1,17},{17,1},{2,18},{18,2},{3,19},{19,3},{4,20},{20... | collective-permute-start | bytes 1572872 | tf_op jit(solution)/shard_map/ppermute | solution.py:21
  (12 other events, 21.0 us)

commit v3 on v2

v3 whole, which is shorter than its diff:
```python
import functools

import jax
import jax.numpy as jnp
from jax import lax
from jax.experimental import pallas as pl
from jax.experimental.pallas import tpu as pltpu
from jax.sharding import PartitionSpec as P

KEY_VALUE_HEADS = 4
HEAD_SIZE = 128
BLK = 64
QUERY_GROUP_SIZE = 8
LOG2_E = 1.4426950408889634
VMEM_LIMIT = 60 * 1024 * 1024
VMEM = pl.BlockSpec(memory_space=pltpu.VMEM)
SMEM = pl.BlockSpec(memory_space=pltpu.SMEM)


def swap(value, axis, mask):
    return lax.ppermute(value, axis, [(i, i ^ mask) for i in range(lax.axis_size(axis))])


def gather_far(value, axis):
    top = lax.axis_size(axis) // 4
    return [value] + [swap(value, axis, step * top) for step in (1, 2, 3)]


def gather_even(far, axis):
    top = lax.axis_size(axis) // 4
    slots = {step * top: far[step] for step in range(4)}
    for mask in range(2, top, 2):
        for step in range(4):
            slots[step * top + mask] = swap(slots[step * top], axis, mask)
    return [slots[k] for k in range(0, 4 * top, 2)]


def gather_odd(even, axis):
    pairs = [(slot, swap(slot, axis, 1)) for slot in even]
    return [slot for pair in pairs for slot in pair]


def double(stacked, axis, mask):
    return jnp.concatenate([stacked, swap(stacked, axis, mask)], axis=0)


def near_order(amount):
    order = [(0, 0)]
    mask = amount // 4
    while mask > 1:
        order = order + [(0, at ^ mask) for _, at in order]
        mask //= 2
    return order + [(1, at) for _, at in order]


def pack(ref, value):
    rows = value.shape[0]
    reach = jnp.max(jnp.max(jnp.abs(value), axis=0, keepdims=True), axis=1, keepdims=True)
    power = jnp.ceil(jnp.log2(jnp.maximum(reach, 1e-30)))
    ref[:rows, :] = value * jnp.exp2(-power)
    ref[rows:, :] = jnp.broadcast_to(power, (ref.shape[0] - rows, value.shape[1]))


def unpack(ref):
    rows = ref.shape[0] - 16
    return ref[:rows, :] * jnp.exp2(ref[rows : rows + 1, :])


def halved(value):
    value = lax.reduce_precision(value, exponent_bits=5, mantissa_bits=10)
    return value, value.astype(jnp.float16)


def split3(value):
    high = value.astype(jnp.bfloat16)
    rest = value - high.astype(jnp.float32)
    middle = rest.astype(jnp.bfloat16)
    low = (rest - middle.astype(jnp.float32)).astype(jnp.bfloat16)
    return high, middle, low


def prepare_kernel(
    chunks,
    tokens_ref,
    weight_ref,
    bias_ref,
    output_ref,
    output_bias_ref,
    turned_ref,
    hidden_ref,
    fall_ref,
    predicted_ref,
    reach_ref,
    tokens,
    weight,
    turned,
    copied,
):
    rows = tokens.shape[1]
    block = tokens.shape[2]
    held = turned.shape[1]
    half = chunks // 2

    def copy_in(c):
        at = pl.ds(c * block, block)
        return (
            pltpu.make_async_copy(tokens_ref.at[:, at], tokens.at[c], copied.at[0, c]),
            pltpu.make_async_copy(weight_ref.at[at], weight.at[c], copied.at[1, c]),
        )

    def copy_out(c):
        at = turned_ref.at[pl.ds(c % half * held, held), c // half]
        return pltpu.make_async_copy(turned.at[c], at, copied.at[2, c])

    for c in range(chunks):
        for copy in copy_in(c):
            copy.start()
    pre_act = jnp.broadcast_to(bias_ref[...], hidden_ref.shape)
    for c in range(chunks):
        for copy in copy_in(c):
            copy.wait()
        part = tokens[c]
        turned[c] = jnp.transpose(part).reshape(turned.shape[1:])
        copy_out(c).start()
        pre_act = pre_act + jnp.dot(part, weight[c], preferred_element_type=jnp.float32)
    gate = jax.nn.sigmoid(pre_act)
    hidden = (pre_act * gate).astype(jnp.bfloat16)
    hidden_ref[...] = hidden
    predicted = lax.dot_general(
        output_ref[...], hidden, (((1,), (1,)), ((), ())), preferred_element_type=jnp.float32
    )
    for head in range(predicted.shape[0]):
        predicted_ref[head : head + 1, :] = predicted[head : head + 1] + output_bias_ref[head]
    fall = gate * (1.0 + pre_act * (1.0 - gate))
    reach = jnp.maximum(jnp.max(jnp.abs(fall), axis=1, keepdims=True), 1e-30)
    fall_ref[...] = fall / reach
    reach_ref[...] = jnp.transpose(jnp.broadcast_to(reach, (rows, rows)))[:1]
    for c in range(chunks):
        copy_out(c).wait()


def prepare(tokens, first_weight, first_bias, output_weight, output_bias, slots):
    rows, model = tokens.shape
    units = first_weight.shape[1]
    share = model // slots // 2
    block = max(share, min(1024, model // 2))
    chunks = model // block
    heads = output_weight.shape[0]
    anywhere = pl.BlockSpec(memory_space=pl.ANY)
    return pl.pallas_call(
        functools.partial(prepare_kernel, chunks),
        out_shape=(
            jax.ShapeDtypeStruct((slots, 2, share, rows), jnp.bfloat16),
            jax.ShapeDtypeStruct((rows, units), jnp.bfloat16),
            jax.ShapeDtypeStruct((rows, units), jnp.float32),
            jax.ShapeDtypeStruct((heads, rows), jnp.float32),
            jax.ShapeDtypeStruct((1, rows), jnp.float32),
        ),
        in_specs=[anywhere, anywhere, VMEM, VMEM, SMEM],
        out_specs=(anywhere, VMEM, VMEM, VMEM, VMEM),
        scratch_shapes=[
            pltpu.VMEM((chunks, rows, block), jnp.bfloat16),
            pltpu.VMEM((chunks, block, units), jnp.bfloat16),
            pltpu.VMEM((chunks, block // share, share, rows), jnp.bfloat16),
            pltpu.SemaphoreType.DMA((3, chunks)),
        ],
        compiler_params=pltpu.CompilerParams(vmem_limit_bytes=VMEM_LIMIT),
        cost_estimate=pl.CostEstimate(
            flops=2 * rows * model * units,
            bytes_accessed=2 * model * (units + 2 * rows),
            transcendentals=rows * units,
        ),
    )(tokens, first_weight, first_bias[None], output_weight, output_bias)


def attention_kernel(slots, heads, order_ref, query_ref, *refs):
    key_refs, mass_ref = refs[:slots], refs[-5]
    keys, bias, scores, mixed = refs[-4:]
    beside_refs = refs[slots:-5]
    rows = key_refs[0].shape[0]
    total = rows * slots
    lanes = scores.shape[1]
    fold = lanes // rows
    first, count = heads
    chunk = 256
    blocks = rows // BLK
    me = lax.axis_index("seq")
    scale = HEAD_SIZE ** (-0.5) * LOG2_E

    def pos_of(owner, index):
        at = jnp.zeros(index.shape, jnp.int32)
        for b in range(blocks):
            at = jnp.where(index // BLK == b, order_ref[owner * blocks + b], at)
        return at * BLK + index % BLK

    if beside_refs:
        early_ref, predicted_ref, reach_ref = beside_refs
        mass_ref[...] = jnp.zeros_like(mass_ref)
        mass_ref[:slots, :first, :] = early_ref[...]
        mass_ref[me, KEY_VALUE_HEADS:, :] = predicted_ref[...]
        beside = mass_ref.shape[0] - slots
        spot = lax.broadcasted_iota(jnp.int32, (beside, 8, rows), 0) * 8
        spot = spot + lax.broadcasted_iota(jnp.int32, (beside, 8, rows), 1)
        mass_ref[slots:] = jnp.where(spot == me, reach_ref[...][None], 0.0)
    query_pos = pos_of(me, lax.broadcasted_iota(jnp.int32, (rows, rows), 1))
    key_index = lax.broadcasted_iota(jnp.int32, (rows, rows), 0)
    for k in range(slots):
        at = pl.ds(k * rows, rows)
        for head in range(count):
            columns = slice((first + head) * HEAD_SIZE, (first + head + 1) * HEAD_SIZE)
            keys[head, at, :] = key_refs[k][:, columns]
        bias[at, :] = jnp.where(pos_of(me ^ k, key_index) <= query_pos, 0.0, -1e30)

    def visit_head(head, carried):
        mixed[...] = jnp.zeros_like(mixed)

        def visit_pair(pair, also):
            start = (first + head) * QUERY_GROUP_SIZE + pair * fold
            query = jnp.concatenate(
                [
                    query_ref[:, pl.ds(pl.multiple_of((start + j) * HEAD_SIZE, HEAD_SIZE), HEAD_SIZE)]
                    for j in range(fold)
                ],
                axis=0,
            )
            top = jnp.full((8, lanes), -1e30, jnp.float32)
            for c in range(total // chunk):
                at = pl.ds(c * chunk, chunk)
                raw = lax.dot_general(
                    keys[head, at, :],
                    query,
                    (((1,), (1,)), ((), ())),
                    preferred_element_type=jnp.float32,
                )
                shade = bias[at, :]
                raw = raw + jnp.concatenate([shade] * (lanes // rows), axis=1)
                scores[at, :] = raw
                top = jnp.maximum(top, jnp.max(raw.reshape(chunk // 8, 8, lanes), axis=0))
            top = jnp.max(top, axis=0, keepdims=True)
            summed = jnp.zeros((8, lanes), jnp.float32)
            for c in range(total // chunk):
                at = pl.ds(c * chunk, chunk)
                weight = jnp.exp2((scores[at, :] - top) * scale)
                scores[at, :] = weight
                summed = summed + jnp.sum(weight.reshape(chunk // 8, 8, lanes), axis=0)
            share = (1.0 / QUERY_GROUP_SIZE) / jnp.sum(summed, axis=0, keepdims=True)
            for c in range(total // chunk):
                at = pl.ds(c * chunk, chunk)
                part = scores[at, :] * share
                gathered = mixed[at, :]
                for j in range(lanes // rows):
                    gathered = gathered + part[:, j * rows : (j + 1) * rows]
                mixed[at, :] = gathered
            return also

        lax.fori_loop(0, QUERY_GROUP_SIZE // fold, visit_pair, 0)
        for k in range(slots):
            tile = jnp.transpose(mixed[pl.ds(k * rows, rows), :])
            row = jnp.sum(tile, axis=0, keepdims=True)
            mass_ref[me ^ k, pl.ds(head + (first if beside_refs else 0), 1), :] = row
        return carried

    lax.fori_loop(0, count, visit_head, 0)


def attention_mass(block_order, queries, key_slots, heads, beside=()):
    slots = len(key_slots)
    rows = key_slots[0].shape[0]
    total = rows * slots
    lanes = 2 * rows
    work = total * rows * heads[1] * QUERY_GROUP_SIZE
    if beside:
        shape = (slots + slots // 8, 8, rows)
    else:
        shape = (slots, heads[1], rows)
    return pl.pallas_call(
        functools.partial(attention_kernel, slots, heads),
        out_shape=jax.ShapeDtypeStruct(shape, jnp.float32),
        in_specs=[SMEM, VMEM] + [VMEM] * (slots + len(beside)),
        out_specs=VMEM,
        scratch_shapes=[
            pltpu.VMEM((heads[1], total, HEAD_SIZE), jnp.bfloat16),
            pltpu.VMEM((total, rows), jnp.float32),
            pltpu.VMEM((total, lanes), jnp.float32),
            pltpu.VMEM((total, rows), jnp.float32),
        ],
        compiler_params=pltpu.CompilerParams(vmem_limit_bytes=VMEM_LIMIT),
        cost_estimate=pl.CostEstimate(
            flops=20 * work * HEAD_SIZE, bytes_accessed=2 * queries.size, transcendentals=work
        ),
    )(block_order, queries, *key_slots, *beside)


def gradient_kernel(slots, columns_ref, output_ref, hidden_ref, *refs):
    message_refs, fall_refs = refs[:2], refs[2:4]
    keep_ref, send_ref, mass_ref, small_ref = refs[4:8]
    out_grad, slope, wide, grad, reaches = refs[8:]
    me, part = lax.axis_index("seq"), lax.axis_index("dp") % 2
    rows = hidden_ref.shape[0]
    total = rows * slots
    units = hidden_ref.shape[1]
    heads = KEY_VALUE_HEADS
    side = slots // 2
    sums = []
    for d in range(2):
        for k in range(slots):
            reaches[d, k] = message_refs[d][slots + k // 8, k % 8 : k % 8 + 1, :]
        mass = message_refs[d][:slots, :heads]
        residue = message_refs[d][:slots, heads:] - jnp.log(1.0 + mass)
        out_grad[d] = residue / total
        sums.append((jnp.sum(residue * residue), mass))
    loss_sum = sums[0][0] * (0.5 / total)
    mass_ref[...] = message_refs[0][me, :heads]
    grad_bias = jnp.sum(jnp.sum(out_grad[0], axis=0), axis=1, keepdims=True)
    output_rows = output_ref[...]
    output_three = jnp.concatenate([output_rows] * 3, axis=0)
    first_bias = jnp.zeros((8, units), jnp.float32)
    order = near_order(slots)
    for j in range(slots):
        d, mask = order[j // 2]
        mask = mask + j % 2
        scaled = out_grad[d, me ^ mask] * reaches[d, me ^ mask]
        back = lax.dot_general(
            jnp.concatenate(split3(scaled), axis=0),
            output_three,
            (((0,), (0,)), ((), ())),
            preferred_element_type=jnp.float32,
        )
        fall = back * fall_refs[j % 2][j // 2]
        first_bias = first_bias + jnp.sum(fall.reshape(rows // 8, 8, units), axis=0)
        at = slice(j * rows, (j + 1) * rows)
        slope[at, :] = fall.astype(jnp.bfloat16)
        wide[:, at] = columns_ref[2 * ((me ^ mask) % side) + (part ^ d)]
    grad[...] = jnp.dot(wide[...], slope[...], preferred_element_type=jnp.float32)
    share = keep_ref.shape[0]
    low = pl.multiple_of((me // side) * share, share)
    keep_ref[...] = grad[pl.ds(low, share), :]
    pack(send_ref, grad[pl.ds(pl.multiple_of(share - low, share), share), :])
    second = lax.dot_general(
        jnp.concatenate(split3(out_grad[0, me]), axis=0),
        hidden_ref[...],
        (((1,), (0,)), ((), ())),
        preferred_element_type=jnp.float32,
    )
    second = second[:heads] + second[heads : 2 * heads] + second[2 * heads :]
    lines = units // 128
    first_bias = jnp.sum(first_bias, axis=0, keepdims=True)
    small_ref[...] = jnp.zeros_like(small_ref)
    for c in range(lines):
        at = slice(c * 128, (c + 1) * 128)
        small_ref[pl.ds(c * heads, heads), :] = second[:, at]
        small_ref[pl.ds(lines * heads + c, 1), :] = first_bias[:, at]
    lane = lax.broadcasted_iota(jnp.int32, (1, 128), 1)
    last = jnp.where(lane == 0, loss_sum, 0.0)
    for head in range(heads):
        last = jnp.where(lane == 1 + head, grad_bias[head : head + 1], last)
    small_ref[pl.ds(lines * (heads + 1), 1), :] = last


def gradient(messages, columns, output_weight, hidden, falls):
    slots, depth, rows = columns.shape
    units = hidden.shape[1]
    return pl.pallas_call(
        functools.partial(gradient_kernel, slots),
        out_shape=(
            jax.ShapeDtypeStruct((depth // 2, units), jnp.float32),
            jax.ShapeDtypeStruct((depth // 2 + 16, units), jnp.float32),
            jax.ShapeDtypeStruct((KEY_VALUE_HEADS, rows), jnp.float32),
            jax.ShapeDtypeStruct((small_rows(units), 128), jnp.float32),
        ),
        in_specs=[VMEM] * 7,
        out_specs=(VMEM,) * 4,
        scratch_shapes=[
            pltpu.VMEM((2, slots, KEY_VALUE_HEADS, rows), jnp.float32),
            pltpu.VMEM((slots * rows, units), jnp.bfloat16),
            pltpu.VMEM((depth, slots * rows), jnp.bfloat16),
            pltpu.VMEM((depth, units), jnp.float32),
            pltpu.VMEM((2, slots, 1, rows), jnp.float32),
        ],
        compiler_params=pltpu.CompilerParams(vmem_limit_bytes=VMEM_LIMIT),
        cost_estimate=pl.CostEstimate(
            flops=2 * depth * slots * rows * units,
            bytes_accessed=2 * columns.size + 8 * slots * rows * units,
            transcendentals=0,
        ),
    )(columns, output_weight, hidden, *messages, *falls)


def small_rows(units):
    return -(-(units // 128 * (KEY_VALUE_HEADS + 1) + 1) // 8) * 8


def square_kernel(small_ref, keep_ref, other_ref, total_ref, send_ref):
    total = keep_ref[...] + unpack(other_ref)
    pack(total_ref, total)
    square = jnp.sum(jnp.sum(total * total, axis=0, keepdims=True), axis=1, keepdims=True)
    row = total.shape[1] // 128 * (KEY_VALUE_HEADS + 1)
    lane = lax.broadcasted_iota(jnp.int32, (1, 128), 1)
    send_ref[...] = small_ref[...]
    last = small_ref[pl.ds(row, 1), :]
    send_ref[pl.ds(row, 1), :] = jnp.where(lane == 1 + KEY_VALUE_HEADS, square, last)


def squares(small, keep, other):
    return pl.pallas_call(
        square_kernel,
        out_shape=(
            jax.ShapeDtypeStruct(other.shape, jnp.float32),
            jax.ShapeDtypeStruct(small.shape, jnp.float32),
        ),
        in_specs=[VMEM] * 3,
        out_specs=(VMEM, VMEM),
        compiler_params=pltpu.CompilerParams(vmem_limit_bytes=VMEM_LIMIT),
    )(small, keep, other)


def scale_kernel(slots, entries, message_ref, *refs):
    part_refs = refs[:2]
    step_ref, second_ref, first_bias_ref, bias_ref, loss_ref = refs[2:]
    part = lax.axis_index("dp") % 2
    devices = message_ref.shape[0]
    heads = KEY_VALUE_HEADS
    total = jnp.sum(message_ref[...], axis=0)
    once = message_ref[0]
    for d in range(slots, devices, slots):
        once = once + message_ref[d]
    twice = message_ref[0] + message_ref[slots // 2]
    for d in range(2 * slots, devices, 2 * slots):
        twice = twice + message_ref[d] + message_ref[d + slots // 2]
    lines = first_bias_ref.shape[1] // 128
    row = lines * (heads + 1)
    square = total[row : row + 1, 1 + heads : 2 + heads]
    inverse = 1.0 / jnp.sqrt(square / entries + 1e-06)
    share = part_refs[0].shape[0] - 16
    for k in range(2):
        at = pl.ds(pl.multiple_of((part ^ k) * share, share), share)
        step_ref[at, :] = unpack(part_refs[k]) * inverse

    def normal(piece):
        spread = jnp.sum(jnp.sum(piece * piece, axis=0, keepdims=True), axis=1, keepdims=True)
        return 1.0 / jnp.sqrt(spread / piece.size + 1e-06)

    second = total[: lines * heads]
    second = second * normal(second)
    first_bias = twice[lines * heads : row]
    first_bias = first_bias * normal(first_bias)
    for c in range(lines):
        at = slice(c * 128, (c + 1) * 128)
        second_ref[:, at] = second[c * heads : (c + 1) * heads]
        first_bias_ref[:, at] = first_bias[c : c + 1]
    last = once[row : row + 1]
    lane = lax.broadcasted_iota(jnp.int32, (1, 128), 1)
    loss_ref[0] = jnp.sum(jnp.where(lane == 0, last, 0.0))
    for head in range(heads):
        bias_ref[head] = jnp.sum(jnp.where(lane == 1 + head, last, 0.0))


def scaled(message, parts, slots, entries):
    share, units = parts[0].shape[0] - 16, parts[0].shape[1]
    return pl.pallas_call(
        functools.partial(scale_kernel, slots, entries),
        out_shape=(
            jax.ShapeDtypeStruct((2 * share, units), jnp.float32),
            jax.ShapeDtypeStruct((KEY_VALUE_HEADS, units), jnp.float32),
            jax.ShapeDtypeStruct((1, units), jnp.float32),
            jax.ShapeDtypeStruct((KEY_VALUE_HEADS,), jnp.float32),
            jax.ShapeDtypeStruct((1,), jnp.float32),
        ),
        in_specs=[VMEM] * 3,
        out_specs=(VMEM, VMEM, VMEM, SMEM, SMEM),
        compiler_params=pltpu.CompilerParams(vmem_limit_bytes=VMEM_LIMIT),
    )(message, *parts)


def send_all(value, axes, amount):
    copies = jnp.broadcast_to(value[None], (amount,) + value.shape)
    return lax.all_to_all(copies, axes, 0, 0, tiled=True)


def per_device(
    queries,
    rotated_key_rows,
    hidden_states,
    block_order,
    first_weight,
    first_bias,
    output_weight,
    output_bias,
):
    seq, dp = lax.axis_size("seq"), lax.axis_size("dp")
    rows, model = hidden_states.shape[1:]
    units = first_weight.shape[1]
    tokens = hidden_states.reshape(rows, model)

    key_far = gather_far(rotated_key_rows.reshape(rows, -1), "seq")
    turned, hidden, fall, predicted, reach = prepare(
        tokens, first_weight, first_bias, output_weight, output_bias, seq
    )
    key_even = gather_even(key_far, "seq")
    falls = fall.astype(jnp.float16)[None]
    mask = seq // 4
    while mask > 2:
        falls = double(falls, "seq", mask)
        mask //= 2
    turned, *key_even = lax.optimization_barrier((turned, *key_even))
    key_slots = gather_odd(key_even, "seq")

    side = seq // 2
    groups = [
        [(d + k) * seq + h * side + r for r in range(side) for k in range(2)]
        for d in range(0, dp, 2)
        for h in range(2)
    ]
    columns = lax.all_to_all(
        turned.reshape(seq, -1, rows), ("dp", "seq"), 0, 0, tiled=True, axis_index_groups=groups
    )
    late = queries.reshape(rows, -1)
    half = KEY_VALUE_HEADS // 2
    early = attention_mass(block_order, late, key_slots, (0, half))
    falls = double(falls, "seq", 2)
    early, late, falls = lax.optimization_barrier((early, late, falls))
    message = attention_mass(
        block_order, late, key_slots, (half, half), (early, predicted, reach)
    )
    falls = double(falls, "dp", 1)
    mask = 1
    while mask < seq // 4:
        message = message + swap(message, "seq", mask)
        mask *= 2
    messages = gather_far(message, "seq")
    message = (messages[0] + messages[1]) + (messages[2] + messages[3])
    message, falls = lax.optimization_barrier((message, falls))
    falls = [falls.astype(jnp.float32), swap(falls, "seq", 1).astype(jnp.float32)]

    keep, send, own_mass, small = gradient(
        (message, swap(message, "dp", 1)), columns, output_weight, hidden, falls
    )
    mask = 2
    while mask < dp:
        keep = keep + swap(keep, "dp", mask)
        send = send + swap(send, "dp", mask)
        mask *= 2
    other = swap(halved(send)[1], "seq", side).astype(jnp.float32)
    total, small = squares(small, keep, other)
    total, sent = halved(total)
    totals = [total, swap(sent, "dp", 1).astype(jnp.float32)]
    message = send_all(small, ("dp", "seq"), dp * seq)
    step_first, second, bias_step, bias, loss = scaled(
        message, totals, seq, model * units * (dp // 2)
    )
    return (
        own_mass.reshape(1, KEY_VALUE_HEADS, rows),
        loss.reshape(()),
        step_first,
        second,
        bias_step.reshape(units),
        bias,
    )


def solution(mesh):
    tokens = P("dp", "seq", None)
    return jax.shard_map(
        per_device,
        mesh=mesh,
        in_specs=(tokens, tokens, tokens, P(), P(), P(), P(), P()),
        out_specs=(P("dp", None, "seq"), P(), P("seq", None), P(), P(), P()),
        check_vma=False,
    )
```

time: 169 us -> 138 us (0.82)
  waiting for transfers between devices: 68.9 us -> 43.3 us
  Pallas kernels: 31.7 us -> 41.6 us
  local copies, waits for them, and re-layouts: 14.4 us -> 5.59 us
  starting transfers between devices: 42.7 us -> 35.7 us
  other arithmetic: 4.59 us -> 10.9 us
  matrix products: 5.6 us -> 0 us
    ppermute x30 -> x27, waiting for transfers between devices: 66.1 us -> 43.3 us  [swap(): lax.ppermute(value, axis, [(i, i ^ mask) for i in range(lax.axis_size(axi...]
    pallas_call x4 -> x6, Pallas kernels: 31.7 us -> 41.6 us  [the longest x2 23.5 us: attention_mass(): pl.pallas_call(functools.partial(attention_kernel, slots, heads), out_sha...]
    dot_general x2 -> x0, matrix products: 5.6 us -> none  [the longest x1 4.88 us: per_device(): jnp.dot(tokens, first_weight, preferred_element_type=jnp.float32)]
    convert_element_type x1 -> x4, other arithmetic: 0.14 us -> 5.25 us  [the longest x2 3.49 us: halved(): return (value, value.astype(jnp.float16))]
    ppermute x30 -> x27, starting transfers between devices: 32 us -> 27.3 us  [swap(): lax.ppermute(value, axis, [(i, i ^ mask) for i in range(lax.axis_size(axi...]
    transpose x1 -> x0, local copies, waits for them, and re-layouts: 4.08 us -> none  [per_device(): jnp.transpose(tokens).reshape(seq, model // seq, rows)]
    all_to_all x1, waiting for transfers between devices: 2.76 us -> 0.01 us  [send_all(): return lax.all_to_all(copies, axes, 0, 0, tiled=True)]
    squeeze x1 -> x0, local copies, waits for them, and re-layouts: 2.08 us -> none  [per_device(): parts = [grads[0]] + [swap(grads[k], 'dp', k) for k in range(1, dp)]]
  transfers between devices with their start and end apart: 32 -> 29, of which waited for: 14 -> 15; matrix products, arithmetic and copies ran while one was open for 10% -> 6% of each run, Pallas kernels for 12% -> 22%
where the time goes in v3:
time: 138 us
  waiting for transfers between devices  43.3 us (31%)
  Pallas kernels  41.6 us (30%)
  starting transfers between devices  35.7 us (26%)
  other arithmetic  10.9 us (8%)
  local copies, waits for them, and re-layouts  5.59 us (4%)
    ppermute x27, waiting for transfers between devices, swap(): lax.ppermute(value, axis, [(i, i ^ mask) for i in range(lax.axis_size(axi...  43.3 us
    ppermute x27, starting transfers between devices, swap(): lax.ppermute(value, axis, [(i, i ^ mask) for i in range(lax.axis_size(axi...  27.3 us
    pallas_call x2, Pallas kernels, attention_mass(): pl.pallas_call(functools.partial(attention_kernel, slots, heads), out_sha...  23.5 us
    pallas_call x1, Pallas kernels, prepare(): pl.pallas_call(functools.partial(prepare_kernel, chunks), out_shape=(jax....  7.4 us
    pallas_call x1, Pallas kernels, gradient(): pl.pallas_call(functools.partial(gradient_kernel, slots), out_shape=(jax....  5.92 us
    all_to_all x1, starting transfers between devices, send_all(): return lax.all_to_all(copies, axes, 0, 0, tiled=True)  4.31 us
    unnamed x40, local copies, waits for them, and re-layouts  4.11 us
    all_to_all x1, starting transfers between devices, per_device(): lax.all_to_all(turned.reshape(seq, -1, rows), ('dp', 'seq'), 0, 0, tiled=...  4.05 us
  transfers between devices with their start and end apart: 29, of which 15 were waited for; matrix products, arithmetic and copies ran while one was open for 6% of the time, Pallas kernels for 22%

profile of v3, /device:TPU:0, one launch (start us, length us, event | category | flops | bytes accessed | tf_op | source)
XLA Modules:
  0.0 137.8 jit_solution(8867311525401006525)
XLA Ops:
  0.6 5.1 %collective-permute-start.5 = (bf16[128,512]{1,0:T(8,128)(2,1)}, bf16[128,512]{1,0:T(8,128)(2,1)S(1)}, u32[]{:S(2)}, u32[]{:S(2)}) collective-permute-start(bf16[128,512]{1,0:T(8,128)(2,1)} %bitcast.15), channel_id=1, source_target_pairs={{0,12},{1,13},{2,14},{3,15},{4,8},{5,9},{6,10},{7,11},{8,4},{9,5},... | collective-permute-start | bytes 393224 | tf_op jit(solution)/shard_map/ppermute | solution.py:21
  5.8 0.6 collective-permute-start.1
  6.4 7.4 %shard_map.127 = (bf16[16,2,256,128]{3,2,1,0:T(8,128)(2,1)}, bf16[128,512]{1,0:T(8,128)(2,1)}, f32[128,512]{1,0:T(8,128)}, f32[4,128]{1,0:T(4,128)}, f32[1,128]{1,0:T(1,128)}) custom-call(bf16[128,8192]{1,0:T(8,128)(2,1)} %bitcast.11, bf16[8192,512]{1,0:T(8,128)(2,1)} %weight_ref.1, f32[1,512]{1,0:T(1,128)} %bitcast.12, bf16[4,512]{1,0:T(4,128)(2,1)} %output_ref.3, ...), custom_call_target="tpu_custom_call" | custom-call | flops 1073741824 | bytes 12582912 | tf_op jit(solution)/shard_map/pallas_call | solution.py:150
  13.8 1.0 convert_bitcast_fusion
  14.8 1.4 %collective-permute-start.15 = (f16[1,128,512]{2,1,0:T(8,128)(2,1)S(1)}, f16[1,128,512]{2,1,0:T(8,128)(2,1)S(1)}, u32[]{:S(2)}, u32[]{:S(2)}) collective-permute-start(f16[1,128,512]{2,1,0:T(8,128)(2,1)S(1)} %convert_bitcast_fusion), channel_id=1, source_target_pairs={{0,4},{1,5},{2,6},{3,7},{4,0},{5,1},{6,2},{7,3},{8,12},{9,13},{10,... | collective-permute-start | bytes 393224 | tf_op jit(solution)/shard_map/ppermute | solution.py:21
  16.2 1.5 %collective-permute-start = (bf16[128,512]{1,0:T(8,128)(2,1)S(1)}, bf16[128,512]{1,0:T(8,128)(2,1)S(1)}, u32[]{:S(2)}, u32[]{:S(2)}) collective-permute-start(bf16[128,512]{1,0:T(8,128)(2,1)S(1)} %bitcast.20), channel_id=1, source_target_pairs={{0,2},{1,3},{2,0},{3,1},{4,6},{5,7},{6,4},{7,5},{8,10},{9,11},{10,... | collective-permute-start | bytes 393224 | tf_op jit(solution)/shard_map/ppermute | solution.py:21
  17.8 0.5 collective-permute-start.6
  18.3 1.5 %collective-permute-start.4 = (bf16[128,512]{1,0:T(8,128)(2,1)S(1)}, bf16[128,512]{1,0:T(8,128)(2,1)S(1)}, u32[]{:S(2)}, u32[]{:S(2)}) collective-permute-start(bf16[128,512]{1,0:T(8,128)(2,1)S(1)} %collective-permute-done.3.refs_8_), channel_id=1, source_target_pairs={{0,2},{1,3},{2,0},{3,1},{4,6},{5,7},{6,4},{7,5},{8,10},{9,11},{10,... | collective-permute-start | bytes 393224 | tf_op jit(solution)/shard_map/ppermute | solution.py:21
  19.8 0.5 collective-permute-start.2
  20.4 1.6 %collective-permute-start.16 = (f16[2,128,512]{2,1,0:T(8,128)(2,1)S(1)}, f16[2,128,512]{2,1,0:T(8,128)(2,1)S(1)}, u32[]{:S(2)}, u32[]{:S(2)}) collective-permute-start(f16[2,128,512]{2,1,0:T(8,128)(2,1)S(1)} %pad_maximum_fusion.2), channel_id=1, source_target_pairs={{0,2},{1,3},{2,0},{3,1},{4,6},{5,7},{6,4},{7,5},{8,10},{9,11},{10,... | collective-permute-start | bytes 786440 | tf_op jit(solution)/shard_map/ppermute | solution.py:21
  22.0 0.7 collective-permute-done.refs_2_
  22.7 2.8 %collective-permute-done.6.refs_14_ = bf16[128,512]{1,0:T(8,128)(2,1)S(1)} collective-permute-done((bf16[128,512]{1,0:T(8,128)(2,1)S(1)}, bf16[128,512]{1,0:T(8,128)(2,1)S(1)}, u32[]{:S(2)}, u32[]{:S(2)}) %collective-permute-start.6) | collective-permute-done | bytes 131104 | tf_op jit(solution)/shard_map/ppermute | solution.py:21
  25.5 2.8 %collective-permute-done.4.refs_10_ = bf16[128,512]{1,0:T(8,128)(2,1)S(1)} collective-permute-done((bf16[128,512]{1,0:T(8,128)(2,1)S(1)}, bf16[128,512]{1,0:T(8,128)(2,1)S(1)}, u32[]{:S(2)}, u32[]{:S(2)}) %collective-permute-start.4) | collective-permute-done | bytes 131104 | tf_op jit(solution)/shard_map/ppermute | solution.py:21
  28.3 2.8 %collective-permute-done.2.refs_6_ = bf16[128,512]{1,0:T(8,128)(2,1)S(1)} collective-permute-done((bf16[128,512]{1,0:T(8,128)(2,1)S(1)}, bf16[128,512]{1,0:T(8,128)(2,1)S(1)}, u32[]{:S(2)}, u32[]{:S(2)}) %collective-permute-start.2) | collective-permute-done | bytes 131104 | tf_op jit(solution)/shard_map/ppermute | solution.py:21
  31.1 0.6 copy-done.11
  31.7 4.0 %all-to-all-start = ((bf16[16,512,128]{2,1,0:T(8,128)(2,1)}), bf16[16,512,128]{2,1,0:T(8,128)(2,1)S(1)}, u32[]{:S(2)}, u32[]{:S(2)}) async-start(bf16[16,512,128]{2,1,0:T(8,128)(2,1)} %bitcast.10), calls=%async_computation | async-start | bytes 4194304 | tf_op jit(solution)/shard_map/all_to_all | solution.py:514
  39.5 0.4 collective-permute-done.14.refs_15_
  40.2 0.4 copy-done.19
  40.6 11.7 %shard_map.128.refs_16_ = f32[16,2,128]{2,1,0:T(2,128)} custom-call(s32[32]{0:T(128)} %order_ref.3, bf16[128,4096]{1,0:T(8,128)(2,1)} %bitcast.13, bf16[128,512]{1,0:T(8,128)(2,1)} %bitcast.18, bf16[128,512]{1,0:T(8,128)(2,1)} %copy-done.12, bf16[128,512]{1,0:T(8,128)(2,1)} %copy-done.8, bf16[128,512]{1,0:T(8,128)(2,1)} %copy-done.13, ...), custom_call_target="tpu_custom_call" | custom-call | flops 10737418240 | bytes 1048576 | tf_op jit(solution)/shard_map/pallas_call | solution.py:276
  52.3 1.8 %collective-permute-start.22 = (f16[4,128,512]{2,1,0:T(8,128)(2,1)S(1)}, f16[4,128,512]{2,1,0:T(8,128)(2,1)S(1)}, u32[]{:S(2)}, u32[]{:S(2)}) collective-permute-start(f16[4,128,512]{2,1,0:T(8,128)(2,1)S(1)} %pad_maximum_fusion.1), channel_id=1, source_target_pairs={{0,16},{16,0},{1,17},{17,1},{2,18},{18,2},{3,19},{19,3},{4,20},{20... | collective-permute-start | bytes 1572872 | tf_op jit(solution)/shard_map/ppermute | solution.py:21
  54.1 11.8 %shard_map.129 = f32[18,8,128]{2,1,0:T(8,128)} custom-call(s32[32]{0:T(128)} %order_ref.3, bf16[128,4096]{1,0:T(8,128)(2,1)} %bitcast.14, bf16[128,512]{1,0:T(8,128)(2,1)} %bitcast.19, bf16[128,512]{1,0:T(8,128)(2,1)} %copy-done.12, bf16[128,512]{1,0:T(8,128)(2,1)} %copy-done.8, bf16[128,512]{1,0:T(8,128)(2,1)} %copy-done.13, bf16[128,512]{1,0:T(8,128)(2,1)} %copy-done.7, ...), custom_call_target="tpu_custom_call" | custom-call | flops 10737418240 | bytes 1048576 | tf_op jit(solution)/shard_map/pallas_call | solution.py:276
  65.9 1.5 %collective-permute-done.17 = f32[18,8,128]{2,1,0:T(8,128)S(1)} collective-permute-done((f32[18,8,128]{2,1,0:T(8,128)}, f32[18,8,128]{2,1,0:T(8,128)S(1)}, u32[]{:S(2)}, u32[]{:S(2)}) %collective-permute-start.17) | collective-permute-done | bytes 73760 | tf_op jit(solution)/shard_map/ppermute | solution.py:21
  67.4 0.9 add.15
  68.3 1.5 %collective-permute-start.18 = (f32[18,8,128]{2,1,0:T(8,128)S(1)}, f32[18,8,128]{2,1,0:T(8,128)S(1)}, u32[]{:S(2)}, u32[]{:S(2)}) collective-permute-start(f32[18,8,128]{2,1,0:T(8,128)S(1)} %add.15), channel_id=1, source_target_pairs={{0,2},{1,3},{2,0},{3,1},{4,6},{5,7},{6,4},{7,5},{8,10},{9,11},{10,... | collective-permute-start | bytes 221192 | tf_op jit(solution)/shard_map/ppermute | solution.py:21
  69.8 2.9 %collective-permute-done.18 = f32[18,8,128]{2,1,0:T(8,128)S(1)} collective-permute-done((f32[18,8,128]{2,1,0:T(8,128)S(1)}, f32[18,8,128]{2,1,0:T(8,128)S(1)}, u32[]{:S(2)}, u32[]{:S(2)}) %collective-permute-start.18) | collective-permute-done | bytes 73760 | tf_op jit(solution)/shard_map/ppermute | solution.py:21
  72.7 3.7 %collective-permute-start.21 = (f32[18,8,128]{2,1,0:T(8,128)S(1)}, f32[18,8,128]{2,1,0:T(8,128)S(1)}, u32[]{:S(2)}, u32[]{:S(2)}) collective-permute-start(f32[18,8,128]{2,1,0:T(8,128)S(1)} %add.16), channel_id=1, source_target_pairs={{0,12},{1,13},{2,14},{3,15},{4,8},{5,9},{6,10},{7,11},{8,4},{9,5},... | collective-permute-start | bytes 221192 | tf_op jit(solution)/shard_map/ppermute | solution.py:21
  76.4 0.8 collective-permute-start.19
  77.2 2.5 %collective-permute-done.21 = f32[18,8,128]{2,1,0:T(8,128)S(1)} collective-permute-done((f32[18,8,128]{2,1,0:T(8,128)S(1)}, f32[18,8,128]{2,1,0:T(8,128)S(1)}, u32[]{:S(2)}, u32[]{:S(2)}) %collective-permute-start.21) | collective-permute-done | bytes 73760 | tf_op jit(solution)/shard_map/ppermute | solution.py:21
  79.7 2.4 %collective-permute-done.20 = f32[18,8,128]{2,1,0:T(8,128)S(1)} collective-permute-done((f32[18,8,128]{2,1,0:T(8,128)S(1)}, f32[18,8,128]{2,1,0:T(8,128)S(1)}, u32[]{:S(2)}, u32[]{:S(2)}) %collective-permute-start.20) | collective-permute-done | bytes 73760 | tf_op jit(solution)/shard_map/ppermute | solution.py:21
  82.5 0.8 collective-permute-start.23
  83.3 1.6 %convert_element_type.22.refs_2_ = f32[8,128,512]{2,1,0:T(8,128)} convert(f16[8,128,512]{2,1,0:T(8,128)(2,1)S(1)} %pad_maximum_fusion) | non-fusion elementwise | flops 524288 | bytes 3145728 | tf_op jit(solution)/shard_map/convert_element_type | solution.py:533
  85.1 1.6 %convert_element_type.23.refs_3_ = f32[8,128,512]{2,1,0:T(8,128)} convert(f16[8,128,512]{2,1,0:T(8,128)(2,1)S(1)} %collective-permute-done.24) | non-fusion elementwise | flops 524288 | bytes 3145728 | tf_op jit(solution)/shard_map/convert_element_type | solution.py:533
  87.1 0.6 copy-done.3
  87.8 0.7 copy-done
  88.5 5.9 %shard_map.130 = (f32[256,512]{1,0:T(8,128)}, f32[272,512]{1,0:T(8,128)}, f32[4,128]{1,0:T(4,128)}, f32[24,128]{1,0:T(8,128)}) custom-call(bf16[16,512,128]{2,1,0:T(8,128)(2,1)} %copy-done, bf16[4,512]{1,0:T(4,128)(2,1)} %output_ref.3, bf16[128,512]{1,0:T(8,128)(2,1)} %get-tuple-element.38.hidden_ref, f32[18,8,128]{2,1,0:T(8,128)} %copy-done.2, ...), custom_call_target="tpu_custom_call" | custom-call | flops 1073741824 | bytes 10485760 | tf_op jit(solution)/shard_map/pallas_call | solution.py:363
  94.4 1.3 reduce-precision_convert_fusion
  95.8 1.7 %collective-permute-start.25 = (f16[272,512]{1,0:T(8,128)(2,1)S(1)}, f16[272,512]{1,0:T(8,128)(2,1)S(1)}, u32[]{:S(2)}, u32[]{:S(2)}) collective-permute-start(f16[272,512]{1,0:T(8,128)(2,1)S(1)} %reduce-precision_convert_fusion), channel_id=1, source_target_pairs={{0,8},{1,9},{2,10},{3,11},{4,12},{5,13},{6,14},{7,15},{8,0},{9,1},... | collective-permute-start | bytes 835592 | tf_op jit(solution)/shard_map/ppermute | solution.py:21
  97.4 13.6 %collective-permute-done.25 = f16[272,512]{1,0:T(8,128)(2,1)S(1)} collective-permute-done((f16[272,512]{1,0:T(8,128)(2,1)S(1)}, f16[272,512]{1,0:T(8,128)(2,1)S(1)}, u32[]{:S(2)}, u32[]{:S(2)}) %collective-permute-start.25) | collective-permute-done | bytes 278560 | tf_op jit(solution)/shard_map/ppermute | solution.py:21
  111.0 0.9 convert_element_type.25.other_ref
  111.9 2.3 %shard_map.131 = (f32[272,512]{1,0:T(8,128)}, f32[24,128]{1,0:T(8,128)}) custom-call(f32[24,128]{1,0:T(8,128)} %get-tuple-element.56.small_ref, f32[256,512]{1,0:T(8,128)} %get-tuple-element.57.keep_ref, f32[272,512]{1,0:T(8,128)} %convert_element_type.25.other_ref), custom_call_target="tpu_custom_call" | custom-call | tf_op jit(solution)/shard_map/pallas_call | solution.py:405
  114.1 1.5 %broadcast_in_dim.14 = f32[32,24,128]{2,1,0:T(8,128)} broadcast(f32[24,128]{1,0:T(8,128)} %get-tuple-element.59), dimensions={1,2} | broadcast | bytes 405504 | tf_op jit(solution)/shard_map/broadcast_in_dim | solution.py:476
  115.6 4.3 %all-to-all-start.1 = ((f32[32,24,128]{2,1,0:T(8,128)}), f32[32,24,128]{2,1,0:T(8,128)S(1)}, u32[]{:S(2)}, u32[]{:S(2)}) async-start(f32[32,24,128]{2,1,0:T(8,128)} %broadcast_in_dim.14), calls=%async_computation.1 | async-start | bytes 786432 | tf_op jit(solution)/shard_map/all_to_all | solution.py:477
  119.9 2.2 %reduce-precision_convert_fusion.1 = (f16[272,512]{1,0:T(8,128)(2,1)S(1)}, f32[272,512]{1,0:T(8,128)}) fusion(f32[272,512]{1,0:T(8,128)} %get-tuple-element.60), kind=kLoop, calls=%fused_computation.6 | loop fusion | flops 278528 | bytes 1392640 | tf_op jit(solution)/shard_map/convert_element_type | solution.py:71
  122.1 1.8 %collective-permute-start.26 = (f16[272,512]{1,0:T(8,128)(2,1)S(1)}, f16[272,512]{1,0:T(8,128)(2,1)S(1)}, u32[]{:S(2)}, u32[]{:S(2)}) collective-permute-start(f16[272,512]{1,0:T(8,128)(2,1)S(1)} %get-tuple-element.66), channel_id=1, source_target_pairs={{0,16},{16,0},{1,17},{17,1},{2,18},{18,2},{3,19},{19,3},{4,20},{20... | collective-permute-start | bytes 835592 | tf_op jit(solution)/shard_map/ppermute | solution.py:21
  123.9 9.7 %collective-permute-done.26 = f16[272,512]{1,0:T(8,128)(2,1)S(1)} collective-permute-done((f16[272,512]{1,0:T(8,128)(2,1)S(1)}, f16[272,512]{1,0:T(8,128)(2,1)S(1)}, u32[]{:S(2)}, u32[]{:S(2)}) %collective-permute-start.26) | collective-permute-done | bytes 278560 | tf_op jit(solution)/shard_map/ppermute | solution.py:21
  133.5 0.9 convert_element_type.27.refs_1_
  134.4 0.8 copy-done.1
  135.2 2.6 %shard_map.132 = (f32[512,512]{1,0:T(8,128)}, f32[4,512]{1,0:T(4,128)}, f32[1,512]{1,0:T(1,128)}, f32[4]{0:T(128)}, f32[1]{0:T(128)}) custom-call(f32[32,24,128]{2,1,0:T(8,128)} %copy-done.1, f32[272,512]{1,0:T(8,128)} %get-tuple-element.67.refs_0_, f32[272,512]{1,0:T(8,128)} %convert_element_type.27.refs_1_), custom_call_target="tpu_custom_call" | custom-call | tf_op jit(solution)/shard_map/pallas_call | solution.py:460
  (70 shorter events, 4.9 us)
Async XLA Ops:
  0.6 17.1 %collective-permute-start.5 = (bf16[128,512]{1,0:T(8,128)(2,1)}, bf16[128,512]{1,0:T(8,128)(2,1)S(1)}, u32[]{:S(2)}, u32[]{:S(2)}) collective-permute-start(bf16[128,512]{1,0:T(8,128)(2,1)} %bitcast.15), channel_id=1, source_target_pairs={{0,12},{1,13},{2,14},{3,15},{4,8},{5,9},{6,10},{7,11},{8,4},{9,5},... | collective-permute-start | bytes 393224 | tf_op jit(solution)/shard_map/ppermute | solution.py:21
  5.7 12.5 %collective-permute-start.3 = (bf16[128,512]{1,0:T(8,128)(2,1)}, bf16[128,512]{1,0:T(8,128)(2,1)S(1)}, u32[]{:S(2)}, u32[]{:S(2)}) collective-permute-start(bf16[128,512]{1,0:T(8,128)(2,1)} %bitcast.16), channel_id=1, source_target_pairs={{0,8},{1,9},{2,10},{3,11},{4,12},{5,13},{6,14},{7,15},{8,0},{9,1},... | collective-permute-start | bytes 393224 | tf_op jit(solution)/shard_map/ppermute | solution.py:21
  5.8 14.0 %collective-permute-start.1 = (bf16[128,512]{1,0:T(8,128)(2,1)}, bf16[128,512]{1,0:T(8,128)(2,1)S(1)}, u32[]{:S(2)}, u32[]{:S(2)}) collective-permute-start(bf16[128,512]{1,0:T(8,128)(2,1)} %bitcast.17), channel_id=1, source_target_pairs={{0,4},{1,5},{2,6},{3,7},{4,0},{5,1},{6,2},{7,3},{8,12},{9,13},{10,... | collective-permute-start | bytes 393224 | tf_op jit(solution)/shard_map/ppermute | solution.py:21
  6.4 9.8 %copy-start.4 = (bf16[1,128,512]{2,1,0:T(8,128)(2,1)S(1)}, bf16[1,128,512]{2,1,0:T(8,128)(2,1)}, u32[]{:S(2)}) copy-start(bf16[1,128,512]{2,1,0:T(8,128)(2,1)} %param.9) | copy-start | bytes 393220
  14.8 5.5 %collective-permute-start.15 = (f16[1,128,512]{2,1,0:T(8,128)(2,1)S(1)}, f16[1,128,512]{2,1,0:T(8,128)(2,1)S(1)}, u32[]{:S(2)}, u32[]{:S(2)}) collective-permute-start(f16[1,128,512]{2,1,0:T(8,128)(2,1)S(1)} %convert_bitcast_fusion), channel_id=1, source_target_pairs={{0,4},{1,5},{2,6},{3,7},{4,0},{5,1},{6,2},{7,3},{8,12},{9,13},{10,... | collective-permute-start | bytes 393224 | tf_op jit(solution)/shard_map/ppermute | solution.py:21
  16.2 6.4 %collective-permute-start = (bf16[128,512]{1,0:T(8,128)(2,1)S(1)}, bf16[128,512]{1,0:T(8,128)(2,1)S(1)}, u32[]{:S(2)}, u32[]{:S(2)}) collective-permute-start(bf16[128,512]{1,0:T(8,128)(2,1)S(1)} %bitcast.20), channel_id=1, source_target_pairs={{0,2},{1,3},{2,0},{3,1},{4,6},{5,7},{6,4},{7,5},{8,10},{9,11},{10,... | collective-permute-start | bytes 393224 | tf_op jit(solution)/shard_map/ppermute | solution.py:21
  17.8 20.0 %copy-start.5 = (bf16[128,512]{1,0:T(8,128)(2,1)}, bf16[128,512]{1,0:T(8,128)(2,1)S(1)}, u32[]{:S(2)}) copy-start(bf16[128,512]{1,0:T(8,128)(2,1)S(1)} %collective-permute-done.5.refs_12_) | copy-start | bytes 393220
  17.8 7.7 %collective-permute-start.6 = (bf16[128,512]{1,0:T(8,128)(2,1)S(1)}, bf16[128,512]{1,0:T(8,128)(2,1)S(1)}, u32[]{:S(2)}, u32[]{:S(2)}) collective-permute-start(bf16[128,512]{1,0:T(8,128)(2,1)S(1)} %collective-permute-done.5.refs_12_), channel_id=1, source_target_pairs={{0,2},{1,3},{2,0},{3,1},{4,6},{5,7},{6,4},{7,5},{8,10},{9,11},{10,... | collective-permute-start | bytes 393224 | tf_op jit(solution)/shard_map/ppermute | solution.py:21
  18.3 19.0 %copy-start.6 = (bf16[128,512]{1,0:T(8,128)(2,1)}, bf16[128,512]{1,0:T(8,128)(2,1)S(1)}, u32[]{:S(2)}) copy-start(bf16[128,512]{1,0:T(8,128)(2,1)S(1)} %collective-permute-done.3.refs_8_) | copy-start | bytes 393220
  18.3 10.0 %collective-permute-start.4 = (bf16[128,512]{1,0:T(8,128)(2,1)S(1)}, bf16[128,512]{1,0:T(8,128)(2,1)S(1)}, u32[]{:S(2)}, u32[]{:S(2)}) collective-permute-start(bf16[128,512]{1,0:T(8,128)(2,1)S(1)} %collective-permute-done.3.refs_8_), channel_id=1, source_target_pairs={{0,2},{1,3},{2,0},{3,1},{4,6},{5,7},{6,4},{7,5},{8,10},{9,11},{10,... | collective-permute-start | bytes 393224 | tf_op jit(solution)/shard_map/ppermute | solution.py:21
  19.8 16.6 %copy-start.7 = (bf16[128,512]{1,0:T(8,128)(2,1)}, bf16[128,512]{1,0:T(8,128)(2,1)S(1)}, u32[]{:S(2)}) copy-start(bf16[128,512]{1,0:T(8,128)(2,1)S(1)} %collective-permute-done.1.refs_4_) | copy-start | bytes 393220
  19.8 11.3 %collective-permute-start.2 = (bf16[128,512]{1,0:T(8,128)(2,1)S(1)}, bf16[128,512]{1,0:T(8,128)(2,1)S(1)}, u32[]{:S(2)}, u32[]{:S(2)}) collective-permute-start(bf16[128,512]{1,0:T(8,128)(2,1)S(1)} %collective-permute-done.1.refs_4_), channel_id=1, source_target_pairs={{0,2},{1,3},{2,0},{3,1},{4,6},{5,7},{6,4},{7,5},{8,10},{9,11},{10,... | collective-permute-start | bytes 393224 | tf_op jit(solution)/shard_map/ppermute | solution.py:21
  20.4 17.8 %collective-permute-start.16 = (f16[2,128,512]{2,1,0:T(8,128)(2,1)S(1)}, f16[2,128,512]{2,1,0:T(8,128)(2,1)S(1)}, u32[]{:S(2)}, u32[]{:S(2)}) collective-permute-start(f16[2,128,512]{2,1,0:T(8,128)(2,1)S(1)} %pad_maximum_fusion.2), channel_id=1, source_target_pairs={{0,2},{1,3},{2,0},{3,1},{4,6},{5,7},{6,4},{7,5},{8,10},{9,11},{10,... | collective-permute-start | bytes 786440 | tf_op jit(solution)/shard_map/ppermute | solution.py:21
  22.7 13.5 %copy-start.8 = (bf16[128,512]{1,0:T(8,128)(2,1)}, bf16[128,512]{1,0:T(8,128)(2,1)S(1)}, u32[]{:S(2)}) copy-start(bf16[128,512]{1,0:T(8,128)(2,1)S(1)} %collective-permute-done.refs_2_) | copy-start | bytes 393220
  25.5 5.6 %copy-start.9 = (bf16[128,512]{1,0:T(8,128)(2,1)}, bf16[128,512]{1,0:T(8,128)(2,1)S(1)}, u32[]{:S(2)}) copy-start(bf16[128,512]{1,0:T(8,128)(2,1)S(1)} %collective-permute-done.6.refs_14_) | copy-start | bytes 393220
  28.3 2.8 %copy-start.10 = (bf16[128,512]{1,0:T(8,128)(2,1)}, bf16[128,512]{1,0:T(8,128)(2,1)S(1)}, u32[]{:S(2)}) copy-start(bf16[128,512]{1,0:T(8,128)(2,1)S(1)} %collective-permute-done.4.refs_10_) | copy-start | bytes 393220
  31.1 0.6 copy-start.11
  31.7 55.4 %all-to-all-start = ((bf16[16,512,128]{2,1,0:T(8,128)(2,1)}), bf16[16,512,128]{2,1,0:T(8,128)(2,1)S(1)}, u32[]{:S(2)}, u32[]{:S(2)}) async-start(bf16[16,512,128]{2,1,0:T(8,128)(2,1)} %bitcast.10), calls=%async_computation | async-start | bytes 4194304 | tf_op jit(solution)/shard_map/all_to_all | solution.py:514
  35.8 1.4 %collective-permute-start.7 = (bf16[128,512]{1,0:T(8,128)(2,1)S(1)}, bf16[128,512]{1,0:T(8,128)(2,1)S(1)}, u32[]{:S(2)}, u32[]{:S(2)}) collective-permute-start(bf16[128,512]{1,0:T(8,128)(2,1)S(1)} %bitcast.21), channel_id=1, source_target_pairs={{0,1},{1,0},{2,3},{3,2},{4,5},{5,4},{6,7},{7,6},{8,9},{9,8},{10,11... | collective-permute-start | bytes 393224 | tf_op jit(solution)/shard_map/ppermute | solution.py:21
  36.2 1.4 collective-permute-start.8
  36.4 1.4 collective-permute-start.9
  36.7 2.2 %collective-permute-start.10 = (bf16[128,512]{1,0:T(8,128)(2,1)}, bf16[128,512]{1,0:T(8,128)(2,1)S(1)}, u32[]{:S(2)}, u32[]{:S(2)}) collective-permute-start(bf16[128,512]{1,0:T(8,128)(2,1)} %copy-done.11), channel_id=1, source_target_pairs={{0,1},{1,0},{2,3},{3,2},{4,5},{5,4},{6,7},{7,6},{8,9},{9,8},{10,11... | collective-permute-start | bytes 393224 | tf_op jit(solution)/shard_map/ppermute | solution.py:21
  37.2 0.9 copy-start.12
  37.2 1.7 %collective-permute-start.11 = (bf16[128,512]{1,0:T(8,128)(2,1)S(1)}, bf16[128,512]{1,0:T(8,128)(2,1)S(1)}, u32[]{:S(2)}, u32[]{:S(2)}) collective-permute-start(bf16[128,512]{1,0:T(8,128)(2,1)S(1)} %collective-permute-done.3.refs_8_), channel_id=1, source_target_pairs={{0,1},{1,0},{2,3},{3,2},{4,5},{5,4},{6,7},{7,6},{8,9},{9,8},{10,11... | collective-permute-start | bytes 393224 | tf_op jit(solution)/shard_map/ppermute | solution.py:21
  37.6 0.6 copy-start.13
  37.6 1.6 %collective-permute-start.12 = (bf16[128,512]{1,0:T(8,128)(2,1)}, bf16[128,512]{1,0:T(8,128)(2,1)S(1)}, u32[]{:S(2)}, u32[]{:S(2)}) collective-permute-start(bf16[128,512]{1,0:T(8,128)(2,1)} %copy-done.10), channel_id=1, source_target_pairs={{0,1},{1,0},{2,3},{3,2},{4,5},{5,4},{6,7},{7,6},{8,9},{9,8},{10,11... | collective-permute-start | bytes 393224 | tf_op jit(solution)/shard_map/ppermute | solution.py:21
  37.8 0.7 copy-start.14
  37.8 1.4 %collective-permute-start.13 = (bf16[128,512]{1,0:T(8,128)(2,1)S(1)}, bf16[128,512]{1,0:T(8,128)(2,1)S(1)}, u32[]{:S(2)}, u32[]{:S(2)}) collective-permute-start(bf16[128,512]{1,0:T(8,128)(2,1)S(1)} %collective-permute-done.5.refs_12_), channel_id=1, source_target_pairs={{0,1},{1,0},{2,3},{3,2},{4,5},{5,4},{6,7},{7,6},{8,9},{9,8},{10,11... | collective-permute-start | bytes 393224 | tf_op jit(solution)/shard_map/ppermute | solution.py:21
  38.4 1.6 %collective-permute-start.14 = (bf16[128,512]{1,0:T(8,128)(2,1)}, bf16[128,512]{1,0:T(8,128)(2,1)S(1)}, u32[]{:S(2)}, u32[]{:S(2)}) collective-permute-start(bf16[128,512]{1,0:T(8,128)(2,1)} %copy-done.9), channel_id=1, source_target_pairs={{0,1},{1,0},{2,3},{3,2},{4,5},{5,4},{6,7},{7,6},{8,9},{9,8},{10,11... | collective-permute-start | bytes 393224 | tf_op jit(solution)/shard_map/ppermute | solution.py:21
  38.9 0.6 copy-start.15
  38.9 1.1 copy-start.16
  39.1 0.9 copy-start.17
  39.5 0.6 copy-start.18
  40.0 0.7 copy-start.19
  52.3 29.8 %collective-permute-start.22 = (f16[4,128,512]{2,1,0:T(8,128)(2,1)S(1)}, f16[4,128,512]{2,1,0:T(8,128)(2,1)S(1)}, u32[]{:S(2)}, u32[]{:S(2)}) collective-permute-start(f16[4,128,512]{2,1,0:T(8,128)(2,1)S(1)} %pad_maximum_fusion.1), channel_id=1, source_target_pairs={{0,16},{16,0},{1,17},{17,1},{2,18},{18,2},{3,19},{19,3},{4,20},{20... | collective-permute-start | bytes 1572872 | tf_op jit(solution)/shard_map/ppermute | solution.py:21
  65.9 1.5 %collective-permute-start.17 = (f32[18,8,128]{2,1,0:T(8,128)}, f32[18,8,128]{2,1,0:T(8,128)S(1)}, u32[]{:S(2)}, u32[]{:S(2)}) collective-permute-start(f32[18,8,128]{2,1,0:T(8,128)} %shard_map.129), channel_id=1, source_target_pairs={{0,1},{1,0},{2,3},{3,2},{4,5},{5,4},{6,7},{7,6},{8,9},{9,8},{10,11... | collective-permute-start | bytes 221192 | tf_op jit(solution)/shard_map/ppermute | solution.py:21
  68.3 4.4 %collective-permute-start.18 = (f32[18,8,128]{2,1,0:T(8,128)S(1)}, f32[18,8,128]{2,1,0:T(8,128)S(1)}, u32[]{:S(2)}, u32[]{:S(2)}) collective-permute-start(f32[18,8,128]{2,1,0:T(8,128)S(1)} %add.15), channel_id=1, source_target_pairs={{0,2},{1,3},{2,0},{3,1},{4,6},{5,7},{6,4},{7,5},{8,10},{9,11},{10,... | collective-permute-start | bytes 221192 | tf_op jit(solution)/shard_map/ppermute | solution.py:21
  72.7 7.0 %collective-permute-start.21 = (f32[18,8,128]{2,1,0:T(8,128)S(1)}, f32[18,8,128]{2,1,0:T(8,128)S(1)}, u32[]{:S(2)}, u32[]{:S(2)}) collective-permute-start(f32[18,8,128]{2,1,0:T(8,128)S(1)} %add.16), channel_id=1, source_target_pairs={{0,12},{1,13},{2,14},{3,15},{4,8},{5,9},{6,10},{7,11},{8,4},{9,5},... | collective-permute-start | bytes 221192 | tf_op jit(solution)/shard_map/ppermute | solution.py:21
  76.4 5.7 %collective-permute-start.20 = (f32[18,8,128]{2,1,0:T(8,128)S(1)}, f32[18,8,128]{2,1,0:T(8,128)S(1)}, u32[]{:S(2)}, u32[]{:S(2)}) collective-permute-start(f32[18,8,128]{2,1,0:T(8,128)S(1)} %add.16), channel_id=1, source_target_pairs={{0,8},{1,9},{2,10},{3,11},{4,12},{5,13},{6,14},{7,15},{8,0},{9,1},... | collective-permute-start | bytes 221192 | tf_op jit(solution)/shard_map/ppermute | solution.py:21
  76.4 5.7 %collective-permute-start.19 = (f32[18,8,128]{2,1,0:T(8,128)S(1)}, f32[18,8,128]{2,1,0:T(8,128)S(1)}, u32[]{:S(2)}, u32[]{:S(2)}) collective-permute-start(f32[18,8,128]{2,1,0:T(8,128)S(1)} %add.16), channel_id=1, source_target_pairs={{0,4},{1,5},{2,6},{3,7},{4,0},{5,1},{6,2},{7,3},{8,12},{9,13},{10,... | collective-permute-start | bytes 221192 | tf_op jit(solution)/shard_map/ppermute | solution.py:21
  82.1 2.8 %copy-start.2 = (f32[18,8,128]{2,1,0:T(8,128)}, f32[18,8,128]{2,1,0:T(8,128)S(1)}, u32[]{:S(2)}) copy-start(f32[18,8,128]{2,1,0:T(8,128)S(1)} %add_add_fusion.refs_0_) | copy-start | bytes 221188
  82.4 2.7 %collective-permute-start.24 = (f16[8,128,512]{2,1,0:T(8,128)(2,1)S(1)}, f16[8,128,512]{2,1,0:T(8,128)(2,1)S(1)}, u32[]{:S(2)}, u32[]{:S(2)}) collective-permute-start(f16[8,128,512]{2,1,0:T(8,128)(2,1)S(1)} %pad_maximum_fusion), channel_id=1, source_target_pairs={{0,1},{1,0},{2,3},{3,2},{4,5},{5,4},{6,7},{7,6},{8,9},{9,8},{10,11... | collective-permute-start | bytes 3145736 | tf_op jit(solution)/shard_map/ppermute | solution.py:21
  82.5 4.7 %collective-permute-start.23 = (f32[18,8,128]{2,1,0:T(8,128)S(1)}, f32[18,8,128]{2,1,0:T(8,128)S(1)}, u32[]{:S(2)}, u32[]{:S(2)}) collective-permute-start(f32[18,8,128]{2,1,0:T(8,128)S(1)} %add_add_fusion.refs_0_), channel_id=1, source_target_pairs={{0,16},{16,0},{1,17},{17,1},{2,18},{18,2},{3,19},{19,3},{4,20},{20... | collective-permute-start | bytes 221192 | tf_op jit(solution)/shard_map/ppermute | solution.py:21
  87.1 1.4 copy-start
  95.8 15.2 %collective-permute-start.25 = (f16[272,512]{1,0:T(8,128)(2,1)S(1)}, f16[272,512]{1,0:T(8,128)(2,1)S(1)}, u32[]{:S(2)}, u32[]{:S(2)}) collective-permute-start(f16[272,512]{1,0:T(8,128)(2,1)S(1)} %reduce-precision_convert_fusion), channel_id=1, source_target_pairs={{0,8},{1,9},{2,10},{3,11},{4,12},{5,13},{6,14},{7,15},{8,0},{9,1},... | collective-permute-start | bytes 835592 | tf_op jit(solution)/shard_map/ppermute | solution.py:21
  115.6 18.8 %all-to-all-start.1 = ((f32[32,24,128]{2,1,0:T(8,128)}), f32[32,24,128]{2,1,0:T(8,128)S(1)}, u32[]{:S(2)}, u32[]{:S(2)}) async-start(f32[32,24,128]{2,1,0:T(8,128)} %broadcast_in_dim.14), calls=%async_computation.1 | async-start | bytes 786432 | tf_op jit(solution)/shard_map/all_to_all | solution.py:477
  122.1 11.4 %collective-permute-start.26 = (f16[272,512]{1,0:T(8,128)(2,1)S(1)}, f16[272,512]{1,0:T(8,128)(2,1)S(1)}, u32[]{:S(2)}, u32[]{:S(2)}) collective-permute-start(f16[272,512]{1,0:T(8,128)(2,1)S(1)} %get-tuple-element.66), channel_id=1, source_target_pairs={{0,16},{16,0},{1,17},{17,1},{2,18},{18,2},{3,19},{19,3},{4,20},{20... | collective-permute-start | bytes 835592 | tf_op jit(solution)/shard_map/ppermute | solution.py:21
  134.4 0.8 copy-start.1
  (1 other events, 0.6 us)

commit v4 on v3

--- a/solution.py
+++ b/solution.py
@@ -12,6 +12,7 @@
 BLK = 64
 QUERY_GROUP_SIZE = 8
 LOG2_E = 1.4426950408889634
+PREDICTED_SCALE = 1.0 / 16.0
 VMEM_LIMIT = 60 * 1024 * 1024
 VMEM = pl.BlockSpec(memory_space=pltpu.VMEM)
 SMEM = pl.BlockSpec(memory_space=pltpu.SMEM)
@@ -40,17 +41,28 @@
     return [slot for pair in pairs for slot in pair]
 
 
-def double(stacked, axis, mask):
-    return jnp.concatenate([stacked, swap(stacked, axis, mask)], axis=0)
-
-
 def near_order(amount):
-    order = [(0, 0)]
-    mask = amount // 4
-    while mask > 1:
-        order = order + [(0, at ^ mask) for _, at in order]
-        mask //= 2
-    return order + [(1, at) for _, at in order]
+    order = [0]
+    mask = 2
+    while mask < amount // 4:
+        order = order + [at ^ mask for at in order]
+        mask *= 2
+    return [(d, at ^ far) for d in (0, 1) for far in (0, amount // 4) for at in order]
+
+
+def gather_near(value):
+    dp, seq = lax.axis_size("dp"), lax.axis_size("seq")
+    slots = [value]
+    mask = 2
+    while mask < seq // 4:
+        slots = slots + [swap(slot, "seq", mask) for slot in slots]
+        mask *= 2
+    stacked = jnp.stack(slots)
+    gathered = [stacked]
+    for d, at in ((0, seq // 4), (1, 0), (1, seq // 4)):
+        pairs = [(i * seq + j, (i ^ d) * seq + (j ^ at)) for i in range(dp) for j in range(seq)]
+        gathered.append(lax.ppermute(stacked, ("dp", "seq"), pairs))
+    return gathered
 
 
 def pack(ref, value):
@@ -89,8 +101,6 @@
     turned_ref,
     hidden_ref,
     fall_ref,
-    predicted_ref,
-    reach_ref,
     tokens,
     weight,
     turned,
@@ -129,12 +139,19 @@
     predicted = lax.dot_general(
         output_ref[...], hidden, (((1,), (1,)), ((), ())), preferred_element_type=jnp.float32
     )
-    for head in range(predicted.shape[0]):
-        predicted_ref[head : head + 1, :] = predicted[head : head + 1] + output_bias_ref[head]
+    heads = predicted.shape[0]
+    head = lax.broadcasted_iota(jnp.int32, predicted.shape, 0)
+    for k in range(heads):
+        predicted = predicted + jnp.where(head == k, output_bias_ref[k], 0.0)
     fall = gate * (1.0 + pre_act * (1.0 - gate))
     reach = jnp.maximum(jnp.max(jnp.abs(fall), axis=1, keepdims=True), 1e-30)
-    fall_ref[...] = fall / reach
-    reach_ref[...] = jnp.transpose(jnp.broadcast_to(reach, (rows, rows)))[:1]
+    power = jnp.ceil(jnp.log2(reach))
+    fall_ref[:rows, :] = fall * jnp.exp2(-power)
+    fall_ref[rows:, :] = jnp.zeros((fall_ref.shape[0] - rows, fall.shape[1]), jnp.float32)
+    for k, piece in enumerate(split3(predicted * PREDICTED_SCALE)):
+        fall_ref[rows + k * heads : rows + (k + 1) * heads, :rows] = piece.astype(jnp.float32)
+    power = jnp.transpose(jnp.broadcast_to(power, (rows, rows)))[:1]
+    fall_ref[rows + 3 * heads : rows + 3 * heads + 1, :rows] = power
     for c in range(chunks):
         copy_out(c).wait()
 
@@ -145,19 +162,16 @@
     share = model // slots // 2
     block = max(share, min(1024, model // 2))
     chunks = model // block
-    heads = output_weight.shape[0]
     anywhere = pl.BlockSpec(memory_space=pl.ANY)
     return pl.pallas_call(
         functools.partial(prepare_kernel, chunks),
         out_shape=(
             jax.ShapeDtypeStruct((slots, 2, share, rows), jnp.bfloat16),
             jax.ShapeDtypeStruct((rows, units), jnp.bfloat16),
-            jax.ShapeDtypeStruct((rows, units), jnp.float32),
-            jax.ShapeDtypeStruct((heads, rows), jnp.float32),
-            jax.ShapeDtypeStruct((1, rows), jnp.float32),
+            jax.ShapeDtypeStruct((rows + 16, units), jnp.float32),
         ),
         in_specs=[anywhere, anywhere, VMEM, VMEM, SMEM],
-        out_specs=(anywhere, VMEM, VMEM, VMEM, VMEM),
+        out_specs=(anywhere, VMEM, VMEM),
         scratch_shapes=[
             pltpu.VMEM((chunks, rows, block), jnp.bfloat16),
             pltpu.VMEM((chunks, block, units), jnp.bfloat16),
@@ -173,16 +187,13 @@
     )(tokens, first_weight, first_bias[None], output_weight, output_bias)
 
 
-def attention_kernel(slots, heads, order_ref, query_ref, *refs):
-    key_refs, mass_ref = refs[:slots], refs[-5]
-    keys, bias, scores, mixed = refs[-4:]
-    beside_refs = refs[slots:-5]
+def attention_kernel(slots, order_ref, query_ref, *refs):
+    key_refs, mass_ref = refs[:slots], refs[slots]
+    keys, bias, scores, shares = refs[slots + 1 :]
     rows = key_refs[0].shape[0]
     total = rows * slots
-    lanes = scores.shape[1]
+    lanes = scores.shape[2]
     fold = lanes // rows
-    first, count = heads
-    chunk = 256
     blocks = rows // BLK
     me = lax.axis_index("seq")
     scale = HEAD_SIZE ** (-0.5) * LOG2_E
@@ -193,29 +204,18 @@
             at = jnp.where(index // BLK == b, order_ref[owner * blocks + b], at)
         return at * BLK + index % BLK
 
-    if beside_refs:
-        early_ref, predicted_ref, reach_ref = beside_refs
-        mass_ref[...] = jnp.zeros_like(mass_ref)
-        mass_ref[:slots, :first, :] = early_ref[...]
-        mass_ref[me, KEY_VALUE_HEADS:, :] = predicted_ref[...]
-        beside = mass_ref.shape[0] - slots
-        spot = lax.broadcasted_iota(jnp.int32, (beside, 8, rows), 0) * 8
-        spot = spot + lax.broadcasted_iota(jnp.int32, (beside, 8, rows), 1)
-        mass_ref[slots:] = jnp.where(spot == me, reach_ref[...][None], 0.0)
+    side = slots // 2
     query_pos = pos_of(me, lax.broadcasted_iota(jnp.int32, (rows, rows), 1))
     key_index = lax.broadcasted_iota(jnp.int32, (rows, rows), 0)
     for k in range(slots):
         at = pl.ds(k * rows, rows)
-        for head in range(count):
-            columns = slice((first + head) * HEAD_SIZE, (first + head + 1) * HEAD_SIZE)
-            keys[head, at, :] = key_refs[k][:, columns]
+        for head in range(KEY_VALUE_HEADS):
+            keys[head, at, :] = key_refs[k][:, head * HEAD_SIZE : (head + 1) * HEAD_SIZE]
         bias[at, :] = jnp.where(pos_of(me ^ k, key_index) <= query_pos, 0.0, -1e30)
 
     def visit_head(head, carried):
-        mixed[...] = jnp.zeros_like(mixed)
-
-        def visit_pair(pair, also):
-            start = (first + head) * QUERY_GROUP_SIZE + pair * fold
+        def visit_pair(pair):
+            start = head * QUERY_GROUP_SIZE + pair * fold
             query = jnp.concatenate(
                 [
                     query_ref[:, pl.ds(pl.multiple_of((start + j) * HEAD_SIZE, HEAD_SIZE), HEAD_SIZE)]
@@ -223,121 +223,123 @@
                 ],
                 axis=0,
             )
-            top = jnp.full((8, lanes), -1e30, jnp.float32)
-            for c in range(total // chunk):
-                at = pl.ds(c * chunk, chunk)
+            query = jnp.transpose(query)
+            tops, sums = [], []
+            for k in range(slots):
+                at = pl.ds(k * rows, rows)
                 raw = lax.dot_general(
                     keys[head, at, :],
                     query,
-                    (((1,), (1,)), ((), ())),
+                    (((1,), (0,)), ((), ())),
                     preferred_element_type=jnp.float32,
                 )
-                shade = bias[at, :]
-                raw = raw + jnp.concatenate([shade] * (lanes // rows), axis=1)
-                scores[at, :] = raw
-                top = jnp.maximum(top, jnp.max(raw.reshape(chunk // 8, 8, lanes), axis=0))
-            top = jnp.max(top, axis=0, keepdims=True)
-            summed = jnp.zeros((8, lanes), jnp.float32)
-            for c in range(total // chunk):
-                at = pl.ds(c * chunk, chunk)
-                weight = jnp.exp2((scores[at, :] - top) * scale)
-                scores[at, :] = weight
-                summed = summed + jnp.sum(weight.reshape(chunk // 8, 8, lanes), axis=0)
+                raw = (raw + jnp.concatenate([bias[at, :]] * fold, axis=1)).reshape(-1, 8, lanes)
+                top = jnp.max(raw, axis=0)
+                weight = jnp.exp2((raw - top[None]) * scale)
+                scores[pair, at, :] = weight.reshape(rows, lanes)
+                tops.append(top)
+                sums.append(jnp.sum(weight, axis=0))
+            best = functools.reduce(jnp.maximum, tops)
+            best = jnp.max(best, axis=0, keepdims=True)
+            parts = [jnp.exp2((top - best) * scale) for top in tops]
+            summed = sum(part * one for part, one in zip(parts, sums))
             share = (1.0 / QUERY_GROUP_SIZE) / jnp.sum(summed, axis=0, keepdims=True)
-            for c in range(total // chunk):
-                at = pl.ds(c * chunk, chunk)
-                part = scores[at, :] * share
-                gathered = mixed[at, :]
-                for j in range(lanes // rows):
-                    gathered = gathered + part[:, j * rows : (j + 1) * rows]
-                mixed[at, :] = gathered
-            return also
-
-        lax.fori_loop(0, QUERY_GROUP_SIZE // fold, visit_pair, 0)
+            for k in range(slots):
+                shares[pair, k] = parts[k] * share
+
+        for pair in range(QUERY_GROUP_SIZE // fold):
+            visit_pair(pair)
         for k in range(slots):
-            tile = jnp.transpose(mixed[pl.ds(k * rows, rows), :])
+            tile = jnp.zeros((rows // 8, 8, rows), jnp.float32)
+            for pair in range(QUERY_GROUP_SIZE // fold):
+                part = scores[pair, pl.ds(k * rows, rows), :].reshape(rows // 8, 8, lanes)
+                part = part * shares[pair, k][None]
+                for j in range(fold):
+                    tile = tile + part[:, :, j * rows : (j + 1) * rows]
+            tile = jnp.transpose(tile.reshape(rows, rows))
             row = jnp.sum(tile, axis=0, keepdims=True)
-            mass_ref[me ^ k, pl.ds(head + (first if beside_refs else 0), 1), :] = row
+            mass_ref[k // side, (me ^ k) % side, pl.ds(head, 1), :] = row
         return carried
 
-    lax.fori_loop(0, count, visit_head, 0)
-
-
-def attention_mass(block_order, queries, key_slots, heads, beside=()):
+    lax.fori_loop(0, KEY_VALUE_HEADS, visit_head, 0)
+
+
+def attention_mass(block_order, queries, key_slots):
     slots = len(key_slots)
     rows = key_slots[0].shape[0]
     total = rows * slots
     lanes = 2 * rows
-    work = total * rows * heads[1] * QUERY_GROUP_SIZE
-    if beside:
-        shape = (slots + slots // 8, 8, rows)
-    else:
-        shape = (slots, heads[1], rows)
+    work = total * rows * KEY_VALUE_HEADS * QUERY_GROUP_SIZE
+    shape = (2, slots // 2, KEY_VALUE_HEADS, rows)
     return pl.pallas_call(
-        functools.partial(attention_kernel, slots, heads),
+        functools.partial(attention_kernel, slots),
         out_shape=jax.ShapeDtypeStruct(shape, jnp.float32),
-        in_specs=[SMEM, VMEM] + [VMEM] * (slots + len(beside)),
+        in_specs=[SMEM] + [VMEM] * (slots + 1),
         out_specs=VMEM,
         scratch_shapes=[
-            pltpu.VMEM((heads[1], total, HEAD_SIZE), jnp.bfloat16),
+            pltpu.VMEM((KEY_VALUE_HEADS, total, HEAD_SIZE), jnp.bfloat16),
             pltpu.VMEM((total, rows), jnp.float32),
-            pltpu.VMEM((total, lanes), jnp.float32),
-            pltpu.VMEM((total, rows), jnp.float32),
+            pltpu.VMEM((QUERY_GROUP_SIZE * rows // lanes, total, lanes), jnp.float32),
+            pltpu.VMEM((QUERY_GROUP_SIZE * rows // lanes, slots, 8, lanes), jnp.float32),
         ],
         compiler_params=pltpu.CompilerParams(vmem_limit_bytes=VMEM_LIMIT),
         cost_estimate=pl.CostEstimate(
-            flops=20 * work * HEAD_SIZE, bytes_accessed=2 * queries.size, transcendentals=work
-        ),
-    )(block_order, queries, *key_slots, *beside)
+            flops=100 * work * HEAD_SIZE, bytes_accessed=2 * queries.size, transcendentals=work
+        ),
+    )(block_order, queries, *key_slots)
 
 
 def gradient_kernel(slots, columns_ref, output_ref, hidden_ref, *refs):
     message_refs, fall_refs = refs[:2], refs[2:4]
     keep_ref, send_ref, mass_ref, small_ref = refs[4:8]
-    out_grad, slope, wide, grad, reaches = refs[8:]
+    slope, wide, grad = refs[8:]
     me, part = lax.axis_index("seq"), lax.axis_index("dp") % 2
     rows = hidden_ref.shape[0]
     total = rows * slots
     units = hidden_ref.shape[1]
     heads = KEY_VALUE_HEADS
     side = slots // 2
-    sums = []
-    for d in range(2):
-        for k in range(slots):
-            reaches[d, k] = message_refs[d][slots + k // 8, k % 8 : k % 8 + 1, :]
-        mass = message_refs[d][:slots, :heads]
-        residue = message_refs[d][:slots, heads:] - jnp.log(1.0 + mass)
-        out_grad[d] = residue / total
-        sums.append((jnp.sum(residue * residue), mass))
-    loss_sum = sums[0][0] * (0.5 / total)
-    mass_ref[...] = message_refs[0][me, :heads]
-    grad_bias = jnp.sum(jnp.sum(out_grad[0], axis=0), axis=1, keepdims=True)
+    mass_ref[...] = message_refs[0][me % side]
     output_rows = output_ref[...]
     output_three = jnp.concatenate([output_rows] * 3, axis=0)
     first_bias = jnp.zeros((8, units), jnp.float32)
+    squared = jnp.zeros((heads, rows), jnp.float32)
+    grad_bias = jnp.zeros((heads, rows), jnp.float32)
     order = near_order(slots)
     for j in range(slots):
         d, mask = order[j // 2]
         mask = mask + j % 2
-        scaled = out_grad[d, me ^ mask] * reaches[d, me ^ mask]
+        held = fall_refs[j % 2][j // 2]
+        beside = held[rows:, :rows]
+        predicted = (beside[:heads] + beside[heads : 2 * heads]) + beside[2 * heads : 3 * heads]
+        mass = message_refs[d][(me ^ mask) % side]
+        residue = predicted * (1.0 / PREDICTED_SCALE) - jnp.log(1.0 + mass)
+        out_grad = residue / total
+        if j == 0:
+            own_grad = out_grad
+        squared = squared + residue * residue
+        grad_bias = grad_bias + out_grad
+        scaled = out_grad * jnp.exp2(beside[3 * heads : 3 * heads + 1])
         back = lax.dot_general(
             jnp.concatenate(split3(scaled), axis=0),
             output_three,
             (((0,), (0,)), ((), ())),
             preferred_element_type=jnp.float32,
         )
-        fall = back * fall_refs[j % 2][j // 2]
+        fall = back * held[:rows]
         first_bias = first_bias + jnp.sum(fall.reshape(rows // 8, 8, units), axis=0)
         at = slice(j * rows, (j + 1) * rows)
         slope[at, :] = fall.astype(jnp.bfloat16)
         wide[:, at] = columns_ref[2 * ((me ^ mask) % side) + (part ^ d)]
+    loss_sum = jnp.sum(squared) * (0.5 / total)
+    grad_bias = jnp.sum(grad_bias, axis=1, keepdims=True)
     grad[...] = jnp.dot(wide[...], slope[...], preferred_element_type=jnp.float32)
     share = keep_ref.shape[0]
     low = pl.multiple_of((me // side) * share, share)
     keep_ref[...] = grad[pl.ds(low, share), :]
     pack(send_ref, grad[pl.ds(pl.multiple_of(share - low, share), share), :])
     second = lax.dot_general(
-        jnp.concatenate(split3(out_grad[0, me]), axis=0),
+        jnp.concatenate(split3(own_grad), axis=0),
         hidden_ref[...],
         (((1,), (0,)), ((), ())),
         preferred_element_type=jnp.float32,
@@ -371,11 +373,9 @@
         in_specs=[VMEM] * 7,
         out_specs=(VMEM,) * 4,
         scratch_shapes=[
-            pltpu.VMEM((2, slots, KEY_VALUE_HEADS, rows), jnp.float32),
             pltpu.VMEM((slots * rows, units), jnp.bfloat16),
             pltpu.VMEM((depth, slots * rows), jnp.bfloat16),
             pltpu.VMEM((depth, units), jnp.float32),
-            pltpu.VMEM((2, slots, 1, rows), jnp.float32),
         ],
         compiler_params=pltpu.CompilerParams(vmem_limit_bytes=VMEM_LIMIT),
         cost_estimate=pl.CostEstimate(
@@ -396,17 +396,18 @@
     square = jnp.sum(jnp.sum(total * total, axis=0, keepdims=True), axis=1, keepdims=True)
     row = total.shape[1] // 128 * (KEY_VALUE_HEADS + 1)
     lane = lax.broadcasted_iota(jnp.int32, (1, 128), 1)
-    send_ref[...] = small_ref[...]
-    last = small_ref[pl.ds(row, 1), :]
-    send_ref[pl.ds(row, 1), :] = jnp.where(lane == 1 + KEY_VALUE_HEADS, square, last)
-
-
-def squares(small, keep, other):
+    last = jnp.where(lane == 1 + KEY_VALUE_HEADS, square, small_ref[row : row + 1, :])
+    for k in range(send_ref.shape[0]):
+        send_ref[k] = small_ref[...]
+        send_ref[k, row : row + 1, :] = last
+
+
+def squares(small, keep, other, devices):
     return pl.pallas_call(
         square_kernel,
         out_shape=(
             jax.ShapeDtypeStruct(other.shape, jnp.float32),
-            jax.ShapeDtypeStruct(small.shape, jnp.float32),
+            jax.ShapeDtypeStruct((devices,) + small.shape, jnp.float32),
         ),
         in_specs=[VMEM] * 3,
         out_specs=(VMEM, VMEM),
@@ -421,9 +422,6 @@
     devices = message_ref.shape[0]
     heads = KEY_VALUE_HEADS
     total = jnp.sum(message_ref[...], axis=0)
-    once = message_ref[0]
-    for d in range(slots, devices, slots):
-        once = once + message_ref[d]
     twice = message_ref[0] + message_ref[slots // 2]
     for d in range(2 * slots, devices, 2 * slots):
         twice = twice + message_ref[d] + message_ref[d + slots // 2]
@@ -448,7 +446,7 @@
         at = slice(c * 128, (c + 1) * 128)
         second_ref[:, at] = second[c * heads : (c + 1) * heads]
         first_bias_ref[:, at] = first_bias[c : c + 1]
-    last = once[row : row + 1]
+    last = twice[row : row + 1]
     lane = lax.broadcasted_iota(jnp.int32, (1, 128), 1)
     loss_ref[0] = jnp.sum(jnp.where(lane == 0, last, 0.0))
     for head in range(heads):
@@ -470,11 +468,6 @@
         out_specs=(VMEM, VMEM, VMEM, SMEM, SMEM),
         compiler_params=pltpu.CompilerParams(vmem_limit_bytes=VMEM_LIMIT),
     )(message, *parts)
-
-
-def send_all(value, axes, amount):
-    copies = jnp.broadcast_to(value[None], (amount,) + value.shape)
-    return lax.all_to_all(copies, axes, 0, 0, tiled=True)
 
 
 def per_device(
@@ -493,17 +486,14 @@
     tokens = hidden_states.reshape(rows, model)
 
     key_far = gather_far(rotated_key_rows.reshape(rows, -1), "seq")
-    turned, hidden, fall, predicted, reach = prepare(
+    turned, hidden, falls = prepare(
         tokens, first_weight, first_bias, output_weight, output_bias, seq
     )
-    key_even = gather_even(key_far, "seq")
-    falls = fall.astype(jnp.float16)[None]
-    mask = seq // 4
-    while mask > 2:
-        falls = double(falls, "seq", mask)
-        mask //= 2
-    turned, *key_even = lax.optimization_barrier((turned, *key_even))
+    falls, *far = lax.optimization_barrier((falls, *key_far[1:]))
+    key_even = gather_even(key_far[:1] + far, "seq")
+    falls = gather_near(falls.astype(jnp.float16))
     key_slots = gather_odd(key_even, "seq")
+    turned, falls, *_ = lax.optimization_barrier((turned, falls, *key_even))
 
     side = seq // 2
     groups = [
@@ -514,24 +504,18 @@
     columns = lax.all_to_all(
         turned.reshape(seq, -1, rows), ("dp", "seq"), 0, 0, tiled=True, axis_index_groups=groups
     )
-    late = queries.reshape(rows, -1)
-    half = KEY_VALUE_HEADS // 2
-    early = attention_mass(block_order, late, key_slots, (0, half))
-    falls = double(falls, "seq", 2)
-    early, late, falls = lax.optimization_barrier((early, late, falls))
-    message = attention_mass(
-        block_order, late, key_slots, (half, half), (early, predicted, reach)
-    )
-    falls = double(falls, "dp", 1)
+    message = attention_mass(block_order, queries.reshape(rows, -1), key_slots)
+    message, *falls = lax.optimization_barrier((message, *falls))
+    falls = jnp.concatenate(falls, axis=0)
+    falls = [falls.astype(jnp.float32), swap(falls, "seq", 1).astype(jnp.float32)]
     mask = 1
     while mask < seq // 4:
         message = message + swap(message, "seq", mask)
         mask *= 2
-    messages = gather_far(message, "seq")
-    message = (messages[0] + messages[1]) + (messages[2] + messages[3])
-    message, falls = lax.optimization_barrier((message, falls))
-    falls = [falls.astype(jnp.float32), swap(falls, "seq", 1).astype(jnp.float32)]
-
+    top = seq // 4
+    message = (message[0] + swap(message[0], "seq", top)) + (
+        swap(message[1], "seq", 2 * top) + swap(message[1], "seq", 3 * top)
+    )
     keep, send, own_mass, small = gradient(
         (message, swap(message, "dp", 1)), columns, output_weight, hidden, falls
     )
@@ -541,10 +525,10 @@
         send = send + swap(send, "dp", mask)
         mask *= 2
     other = swap(halved(send)[1], "seq", side).astype(jnp.float32)
-    total, small = squares(small, keep, other)
+    total, small = squares(small, keep, other, dp * seq)
     total, sent = halved(total)
     totals = [total, swap(sent, "dp", 1).astype(jnp.float32)]
-    message = send_all(small, ("dp", "seq"), dp * seq)
+    message = lax.all_to_all(small, ("dp", "seq"), 0, 0, tiled=True)
     step_first, second, bias_step, bias, loss = scaled(
         message, totals, seq, model * units * (dp // 2)
     )

time: 138 us -> 132 us (0.957)
  Pallas kernels: 41.6 us -> 34.1 us
  local copies, waits for them, and re-layouts: 5.59 us -> 2.43 us
  starting transfers between devices: 35.7 us -> 37.8 us
  waiting for transfers between devices: 43.3 us -> 45 us
    pallas_call x2 -> x1, Pallas kernels: 23.5 us -> 15.7 us  [attention_mass(): pl.pallas_call(functools.partial(attention_kernel, slots), out_shape=jax....]
    ppermute x0 -> x3, starting transfers between devices: none -> 3.55 us  [gather_near(): gathered.append(lax.ppermute(stacked, ('dp', 'seq'), pairs))]
    unnamed x40 -> x27, local copies, waits for them, and re-layouts: 4.11 us -> 2.37 us
    ppermute x27 -> x25, waiting for transfers between devices: 43.3 us -> 45 us  [swap(): lax.ppermute(value, axis, [(i, i ^ mask) for i in range(lax.axis_size(axi...]
    broadcast_in_dim x1 -> x0, local copies, waits for them, and re-layouts: 1.48 us -> none  [send_all(): copies = jnp.broadcast_to(value[None], (amount,) + value.shape)]
    ppermute x27 -> x25, starting transfers between devices: 27.3 us -> 26.6 us  [swap(): lax.ppermute(value, axis, [(i, i ^ mask) for i in range(lax.axis_size(axi...]
  transfers between devices with their start and end apart: 29 -> 30, of which waited for: 15 -> 11; matrix products, arithmetic and copies ran while one was open for 6% -> 7% of each run, Pallas kernels for 22% -> 18%
where the time goes in v4:
time: 132 us; the launch traced here: 131 us
  waiting for transfers between devices  45 us (34%)
  starting transfers between devices  37.8 us (29%)
  Pallas kernels  34.1 us (26%)
  other arithmetic  11 us (8%)
  local copies, waits for them, and re-layouts  2.43 us (2%)
    ppermute x25, waiting for transfers between devices, swap(): lax.ppermute(value, axis, [(i, i ^ mask) for i in range(lax.axis_size(axi...  45 us
    ppermute x25, starting transfers between devices, swap(): lax.ppermute(value, axis, [(i, i ^ mask) for i in range(lax.axis_size(axi...  26.6 us
    pallas_call x1, Pallas kernels, attention_mass(): pl.pallas_call(functools.partial(attention_kernel, slots), out_shape=jax....  15.7 us
    pallas_call x1, Pallas kernels, prepare(): pl.pallas_call(functools.partial(prepare_kernel, chunks), out_shape=(jax....  7.43 us
    pallas_call x1, Pallas kernels, gradient(): pl.pallas_call(functools.partial(gradient_kernel, slots), out_shape=(jax....  6.03 us
    all_to_all x1, starting transfers between devices, per_device(): lax.all_to_all(turned.reshape(seq, -1, rows), ('dp', 'seq'), 0, 0, tiled=...  3.84 us
    all_to_all x1, starting transfers between devices, per_device(): message = lax.all_to_all(small, ('dp', 'seq'), 0, 0, tiled=True)  3.72 us
    ppermute x3, starting transfers between devices, gather_near(): gathered.append(lax.ppermute(stacked, ('dp', 'seq'), pairs))  3.55 us
  transfers between devices with their start and end apart: 30, of which 11 were waited for; matrix products, arithmetic and copies ran while one was open for 7% of the time, Pallas kernels for 18%

profile of v4, /device:TPU:0, one launch (start us, length us, event | category | flops | bytes accessed | tf_op | source)
XLA Modules:
  0.0 131.1 jit_solution(9989891268107765069)
XLA Ops:
  0.6 5.1 %collective-permute-start.2 = (bf16[128,512]{1,0:T(8,128)(2,1)}, bf16[128,512]{1,0:T(8,128)(2,1)S(1)}, u32[]{:S(2)}, u32[]{:S(2)}) collective-permute-start(bf16[128,512]{1,0:T(8,128)(2,1)} %bitcast.22), channel_id=1, source_target_pairs={{0,12},{1,13},{2,14},{3,15},{4,8},{5,9},{6,10},{7,11},{8,4},{9,5},... | collective-permute-start | bytes 393224 | tf_op jit(solution)/shard_map/ppermute | solution.py:22
  5.8 0.6 collective-permute-start
  6.4 1.7 %collective-permute-start.7 = (bf16[128,512]{1,0:T(8,128)(2,1)}, bf16[128,512]{1,0:T(8,128)(2,1)S(1)}, u32[]{:S(2)}, u32[]{:S(2)}) collective-permute-start(bf16[128,512]{1,0:T(8,128)(2,1)} %bitcast.25), channel_id=1, source_target_pairs={{0,2},{1,3},{2,0},{3,1},{4,6},{5,7},{6,4},{7,5},{8,10},{9,11},{10,... | collective-permute-start | bytes 393224 | tf_op jit(solution)/shard_map/ppermute | solution.py:22
  8.1 7.4 %shard_map.127 = (bf16[16,2,256,128]{3,2,1,0:T(8,128)(2,1)}, bf16[128,512]{1,0:T(8,128)(2,1)}, f32[144,512]{1,0:T(8,128)}) custom-call(bf16[128,8192]{1,0:T(8,128)(2,1)} %bitcast.18, bf16[8192,512]{1,0:T(8,128)(2,1)} %weight_ref.1, f32[1,512]{1,0:T(1,128)} %bitcast.20, bf16[4,512]{1,0:T(4,128)(2,1)} %output_ref.3, f32[4]{0:T(128)} %output_bias_ref.1), custom_call_target="tpu_custom_call" | custom-call | flops 1073741824 | bytes 12582912 | tf_op jit(solution)/shard_map/pallas_call | solution.py:166
  15.5 1.5 %collective-permute-done.1.refs_8_ = bf16[128,512]{1,0:T(8,128)(2,1)S(1)} collective-permute-done((bf16[128,512]{1,0:T(8,128)(2,1)}, bf16[128,512]{1,0:T(8,128)(2,1)S(1)}, u32[]{:S(2)}, u32[]{:S(2)}) %collective-permute-start.1) | collective-permute-done | bytes 131104 | tf_op jit(solution)/shard_map/ppermute | solution.py:22
  17.0 1.1 convert_element_type.21
  18.1 1.6 %collective-permute-start.3 = (f16[144,512]{1,0:T(8,128)(2,1)S(1)}, f16[144,512]{1,0:T(8,128)(2,1)S(1)}, u32[]{:S(2)}, u32[]{:S(2)}) collective-permute-start(f16[144,512]{1,0:T(8,128)(2,1)S(1)} %convert_element_type.21), channel_id=1, source_target_pairs={{0,2},{1,3},{2,0},{3,1},{4,6},{5,7},{6,4},{7,5},{8,10},{9,11},{10,... | collective-permute-start | bytes 442376 | tf_op jit(solution)/shard_map/ppermute | solution.py:22
  19.7 1.0 convert_bitcast_fusion
  20.8 2.6 %collective-permute-done.3 = f16[144,512]{1,0:T(8,128)(2,1)S(1)} collective-permute-done((f16[144,512]{1,0:T(8,128)(2,1)S(1)}, f16[144,512]{1,0:T(8,128)(2,1)S(1)}, u32[]{:S(2)}, u32[]{:S(2)}) %collective-permute-start.3) | collective-permute-done | bytes 147488 | tf_op jit(solution)/shard_map/ppermute | solution.py:22
  23.4 1.9 %collective-permute-start.6 = (f16[2,144,512]{2,1,0:T(8,128)(2,1)S(1)}, f16[2,144,512]{2,1,0:T(8,128)(2,1)S(1)}, u32[]{:S(2)}, u32[]{:S(2)}) collective-permute-start(f16[2,144,512]{2,1,0:T(8,128)(2,1)S(1)} %pad_maximum_fusion), channel_id=1, source_target_pairs={{0,20},{1,21},{2,22},{3,23},{4,16},{5,17},{6,18},{7,19},{8,28},{9,... | collective-permute-start | bytes 884744 | tf_op jit(solution)/shard_map/ppermute | solution.py:64
  25.3 0.5 collective-permute-start.5
  25.8 1.1 collective-permute-start.4
  27.0 1.6 %collective-permute-start.8 = (bf16[128,512]{1,0:T(8,128)(2,1)S(1)}, bf16[128,512]{1,0:T(8,128)(2,1)}, u32[]{:S(2)}, u32[]{:S(2)}) collective-permute-start(bf16[128,512]{1,0:T(8,128)(2,1)S(1)} %collective-permute-done.refs_4_), channel_id=1, source_target_pairs={{0,2},{1,3},{2,0},{3,1},{4,6},{5,7},{6,4},{7,5},{8,10},{9,11},{10,... | collective-permute-start | bytes 393224 | tf_op jit(solution)/shard_map/ppermute | solution.py:22
  28.6 1.3 collective-permute-start.9
  29.8 3.6 %collective-permute-done.8.refs_6_ = bf16[128,512]{1,0:T(8,128)(2,1)} collective-permute-done((bf16[128,512]{1,0:T(8,128)(2,1)S(1)}, bf16[128,512]{1,0:T(8,128)(2,1)}, u32[]{:S(2)}, u32[]{:S(2)}) %collective-permute-start.8) | collective-permute-done | bytes 131104 | tf_op jit(solution)/shard_map/ppermute | solution.py:22
  33.5 1.5 %collective-permute-start.10 = (bf16[128,512]{1,0:T(8,128)(2,1)S(1)}, bf16[128,512]{1,0:T(8,128)(2,1)}, u32[]{:S(2)}, u32[]{:S(2)}) collective-permute-start(bf16[128,512]{1,0:T(8,128)(2,1)S(1)} %collective-permute-done.2.refs_12_), channel_id=1, source_target_pairs={{0,2},{1,3},{2,0},{3,1},{4,6},{5,7},{6,4},{7,5},{8,10},{9,11},{10,... | collective-permute-start | bytes 393224 | tf_op jit(solution)/shard_map/ppermute | solution.py:22
  35.0 1.2 collective-permute-done.9.refs_10_
  36.2 2.4 %collective-permute-done.10.refs_14_ = bf16[128,512]{1,0:T(8,128)(2,1)} collective-permute-done((bf16[128,512]{1,0:T(8,128)(2,1)S(1)}, bf16[128,512]{1,0:T(8,128)(2,1)}, u32[]{:S(2)}, u32[]{:S(2)}) %collective-permute-start.10) | collective-permute-done | bytes 131104 | tf_op jit(solution)/shard_map/ppermute | solution.py:22
  38.6 0.5 collective-permute-start.14
  39.2 0.4 collective-permute-start.18
  39.7 3.8 %all-to-all-start = ((bf16[16,512,128]{2,1,0:T(8,128)(2,1)}), bf16[16,512,128]{2,1,0:T(8,128)(2,1)S(1)}, u32[]{:S(2)}, u32[]{:S(2)}) async-start(bf16[16,512,128]{2,1,0:T(8,128)(2,1)} %bitcast.17), calls=%async_computation | async-start | bytes 4194304 | tf_op jit(solution)/shard_map/all_to_all | solution.py:504
  43.6 15.7 %shard_map.128 = f32[2,8,4,128]{3,2,1,0:T(4,128)} custom-call(s32[32]{0:T(128)} %order_ref.1, bf16[128,4096]{1,0:T(8,128)(2,1)} %bitcast.21, bf16[128,512]{1,0:T(8,128)(2,1)} %bitcast.27, bf16[128,512]{1,0:T(8,128)(2,1)} %copy-done.9, bf16[128,512]{1,0:T(8,128)(2,1)} %copy-done.8, bf16[128,512]{1,0:T(8,128)(2,1)} %copy-done.10, bf16[128,512]{1,0:T(8,128)(2,1)} %copy-done.7, ...), custom_call_target="tpu_custom_call" | custom-call | flops 107374182400 | bytes 1048576 | tf_op jit(solution)/shard_map/pallas_call | solution.py:274
  59.5 0.5 collective-permute-start.25
  60.4 2.1 %collective-permute-done.19 = f32[2,8,4,128]{3,2,1,0:T(4,128)S(1)} collective-permute-done((f32[2,8,4,128]{3,2,1,0:T(4,128)S(1)}, f32[2,8,4,128]{3,2,1,0:T(4,128)S(1)}, u32[]{:S(2)}, u32[]{:S(2)}) %collective-permute-start.19) | collective-permute-done | bytes 32800 | tf_op jit(solution)/shard_map/ppermute | solution.py:22
  62.5 2.0 %collective-permute-start.20 = (f32[2,8,4,128]{3,2,1,0:T(4,128)S(1)}, f32[2,8,4,128]{3,2,1,0:T(4,128)S(1)}, u32[]{:S(2)}, u32[]{:S(2)}) collective-permute-start(f32[2,8,4,128]{3,2,1,0:T(4,128)S(1)} %add.15), channel_id=1, source_target_pairs={{0,2},{1,3},{2,0},{3,1},{4,6},{5,7},{6,4},{7,5},{8,10},{9,11},{10,... | collective-permute-start | bytes 98312 | tf_op jit(solution)/shard_map/ppermute | solution.py:22
  64.5 4.4 %collective-permute-done.20 = f32[2,8,4,128]{3,2,1,0:T(4,128)S(1)} collective-permute-done((f32[2,8,4,128]{3,2,1,0:T(4,128)S(1)}, f32[2,8,4,128]{3,2,1,0:T(4,128)S(1)}, u32[]{:S(2)}, u32[]{:S(2)}) %collective-permute-start.20) | collective-permute-done | bytes 32800 | tf_op jit(solution)/shard_map/ppermute | solution.py:22
  68.9 2.5 %collective-permute-start.21 = (f32[8,4,128]{2,1,0:T(4,128)S(1)}, f32[8,4,128]{2,1,0:T(4,128)S(1)}, u32[]{:S(2)}, u32[]{:S(2)}) collective-permute-start(f32[8,4,128]{2,1,0:T(4,128)S(1)} %get-tuple-element.64), channel_id=1, source_target_pairs={{0,4},{1,5},{2,6},{3,7},{4,0},{5,1},{6,2},{7,3},{8,12},{9,13},{10,... | collective-permute-start | bytes 49160 | tf_op jit(solution)/shard_map/ppermute | solution.py:22
  71.4 2.0 %collective-permute-start.23 = (f32[8,4,128]{2,1,0:T(4,128)S(1)}, f32[8,4,128]{2,1,0:T(4,128)S(1)}, u32[]{:S(2)}, u32[]{:S(2)}) collective-permute-start(f32[8,4,128]{2,1,0:T(4,128)S(1)} %get-tuple-element.65), channel_id=1, source_target_pairs={{0,12},{1,13},{2,14},{3,15},{4,8},{5,9},{6,10},{7,11},{8,4},{9,5},... | collective-permute-start | bytes 49160 | tf_op jit(solution)/shard_map/ppermute | solution.py:22
  73.4 0.5 collective-permute-start.22
  73.9 3.2 %collective-permute-done.23 = f32[8,4,128]{2,1,0:T(4,128)S(1)} collective-permute-done((f32[8,4,128]{2,1,0:T(4,128)S(1)}, f32[8,4,128]{2,1,0:T(4,128)S(1)}, u32[]{:S(2)}, u32[]{:S(2)}) %collective-permute-start.23) | collective-permute-done | bytes 16416 | tf_op jit(solution)/shard_map/ppermute | solution.py:22
  77.1 0.9 collective-permute-done.22
  78.0 2.6 %collective-permute-start.24 = (f32[8,4,128]{2,1,0:T(4,128)S(1)}, f32[8,4,128]{2,1,0:T(4,128)S(1)}, u32[]{:S(2)}, u32[]{:S(2)}) collective-permute-start(f32[8,4,128]{2,1,0:T(4,128)S(1)} %add_add_fusion.refs_0_), channel_id=1, source_target_pairs={{0,16},{16,0},{1,17},{17,1},{2,18},{18,2},{3,19},{19,3},{4,20},{20... | collective-permute-start | bytes 49160 | tf_op jit(solution)/shard_map/ppermute | solution.py:22
  80.7 1.8 %convert_element_type.22.refs_2_ = f32[8,144,512]{2,1,0:T(8,128)} convert(f16[8,144,512]{2,1,0:T(8,128)(2,1)S(1)} %constant_dynamic-update-slice_fusion) | non-fusion elementwise | flops 589824 | bytes 3538944 | tf_op jit(solution)/shard_map/convert_element_type | solution.py:510
  82.4 1.8 %convert_element_type.23.refs_3_ = f32[8,144,512]{2,1,0:T(8,128)} convert(f16[8,144,512]{2,1,0:T(8,128)(2,1)S(1)} %collective-permute-done.25) | non-fusion elementwise | flops 589824 | bytes 3538944 | tf_op jit(solution)/shard_map/convert_element_type | solution.py:510
  84.2 0.6 copy-done.4
  84.8 0.8 copy-done
  85.5 6.0 %shard_map.129 = (f32[256,512]{1,0:T(8,128)}, f32[272,512]{1,0:T(8,128)}, f32[4,128]{1,0:T(4,128)}, f32[24,128]{1,0:T(8,128)}) custom-call(bf16[16,512,128]{2,1,0:T(8,128)(2,1)} %copy-done, bf16[4,512]{1,0:T(4,128)(2,1)} %output_ref.3, bf16[128,512]{1,0:T(8,128)(2,1)} %get-tuple-element.41.hidden_ref, f32[8,4,128]{2,1,0:T(4,128)} %copy-done.2, ...), custom_call_target="tpu_custom_call" | custom-call | flops 1073741824 | bytes 10485760 | tf_op jit(solution)/shard_map/pallas_call | solution.py:365
  91.6 1.3 %reduce-precision_convert_fusion = f16[272,512]{1,0:T(8,128)(2,1)S(1)} fusion(f32[272,512]{1,0:T(8,128)} %get-tuple-element.54), kind=kLoop, calls=%fused_computation | loop fusion | flops 278528 | bytes 835584 | tf_op jit(solution)/shard_map/convert_element_type | solution.py:83
  93.0 13.3 %collective-permute-done.26 = f16[272,512]{1,0:T(8,128)(2,1)S(1)} collective-permute-done((f16[272,512]{1,0:T(8,128)(2,1)S(1)}, f16[272,512]{1,0:T(8,128)(2,1)S(1)}, u32[]{:S(2)}, u32[]{:S(2)}) %collective-permute-start.26) | collective-permute-done | bytes 278560 | tf_op jit(solution)/shard_map/ppermute | solution.py:22
  106.3 0.9 convert_element_type.25.other_ref
  107.2 2.4 %shard_map.130 = (f32[272,512]{1,0:T(8,128)}, f32[32,24,128]{2,1,0:T(8,128)}) custom-call(f32[24,128]{1,0:T(8,128)} %get-tuple-element.52.small_ref, f32[256,512]{1,0:T(8,128)} %get-tuple-element.53.keep_ref, f32[272,512]{1,0:T(8,128)} %convert_element_type.25.other_ref), custom_call_target="tpu_custom_call" | custom-call | tf_op jit(solution)/shard_map/pallas_call | solution.py:406
  109.5 3.7 %all-to-all-start.1 = ((f32[32,24,128]{2,1,0:T(8,128)}), f32[32,24,128]{2,1,0:T(8,128)S(1)}, u32[]{:S(2)}, u32[]{:S(2)}) async-start(f32[32,24,128]{2,1,0:T(8,128)} %get-tuple-element.55), calls=%async_computation.1 | async-start | bytes 786432 | tf_op jit(solution)/shard_map/all_to_all | solution.py:531
  113.3 2.2 %reduce-precision_convert_fusion.1 = (f16[272,512]{1,0:T(8,128)(2,1)S(1)}, f32[272,512]{1,0:T(8,128)}) fusion(f32[272,512]{1,0:T(8,128)} %get-tuple-element.56), kind=kLoop, calls=%fused_computation.9 | loop fusion | flops 278528 | bytes 1392640 | tf_op jit(solution)/shard_map/convert_element_type | solution.py:83
  115.4 1.8 %collective-permute-start.27 = (f16[272,512]{1,0:T(8,128)(2,1)S(1)}, f16[272,512]{1,0:T(8,128)(2,1)S(1)}, u32[]{:S(2)}, u32[]{:S(2)}) collective-permute-start(f16[272,512]{1,0:T(8,128)(2,1)S(1)} %get-tuple-element.62), channel_id=1, source_target_pairs={{0,16},{16,0},{1,17},{17,1},{2,18},{18,2},{3,19},{19,3},{4,20},{20... | collective-permute-start | bytes 835592 | tf_op jit(solution)/shard_map/ppermute | solution.py:22
  117.2 9.7 %collective-permute-done.27 = f16[272,512]{1,0:T(8,128)(2,1)S(1)} collective-permute-done((f16[272,512]{1,0:T(8,128)(2,1)S(1)}, f16[272,512]{1,0:T(8,128)(2,1)S(1)}, u32[]{:S(2)}, u32[]{:S(2)}) %collective-permute-start.27) | collective-permute-done | bytes 278560 | tf_op jit(solution)/shard_map/ppermute | solution.py:22
  126.9 0.9 convert_element_type.27.refs_1_
  127.7 0.8 copy-done.1
  128.5 2.6 %shard_map.131 = (f32[512,512]{1,0:T(8,128)}, f32[4,512]{1,0:T(4,128)}, f32[1,512]{1,0:T(1,128)}, f32[4]{0:T(128)}, f32[1]{0:T(128)}) custom-call(f32[32,24,128]{2,1,0:T(8,128)} %copy-done.1, f32[272,512]{1,0:T(8,128)} %get-tuple-element.63.refs_0_, f32[272,512]{1,0:T(8,128)} %convert_element_type.27.refs_1_), custom_call_target="tpu_custom_call" | custom-call | tf_op jit(solution)/shard_map/pallas_call | solution.py:458
  (58 shorter events, 1.0 us)
Async XLA Ops:
  0.6 14.9 %collective-permute-start.2 = (bf16[128,512]{1,0:T(8,128)(2,1)}, bf16[128,512]{1,0:T(8,128)(2,1)S(1)}, u32[]{:S(2)}, u32[]{:S(2)}) collective-permute-start(bf16[128,512]{1,0:T(8,128)(2,1)} %bitcast.22), channel_id=1, source_target_pairs={{0,12},{1,13},{2,14},{3,15},{4,8},{5,9},{6,10},{7,11},{8,4},{9,5},... | collective-permute-start | bytes 393224 | tf_op jit(solution)/shard_map/ppermute | solution.py:22
  5.7 11.3 %collective-permute-start.1 = (bf16[128,512]{1,0:T(8,128)(2,1)}, bf16[128,512]{1,0:T(8,128)(2,1)S(1)}, u32[]{:S(2)}, u32[]{:S(2)}) collective-permute-start(bf16[128,512]{1,0:T(8,128)(2,1)} %bitcast.23), channel_id=1, source_target_pairs={{0,8},{1,9},{2,10},{3,11},{4,12},{5,13},{6,14},{7,15},{8,0},{9,1},... | collective-permute-start | bytes 393224 | tf_op jit(solution)/shard_map/ppermute | solution.py:22
  5.8 11.3 %collective-permute-start = (bf16[128,512]{1,0:T(8,128)(2,1)}, bf16[128,512]{1,0:T(8,128)(2,1)S(1)}, u32[]{:S(2)}, u32[]{:S(2)}) collective-permute-start(bf16[128,512]{1,0:T(8,128)(2,1)} %bitcast.24), channel_id=1, source_target_pairs={{0,4},{1,5},{2,6},{3,7},{4,0},{5,1},{6,2},{7,3},{8,12},{9,13},{10,... | collective-permute-start | bytes 393224 | tf_op jit(solution)/shard_map/ppermute | solution.py:22
  6.4 13.3 %collective-permute-start.7 = (bf16[128,512]{1,0:T(8,128)(2,1)}, bf16[128,512]{1,0:T(8,128)(2,1)S(1)}, u32[]{:S(2)}, u32[]{:S(2)}) collective-permute-start(bf16[128,512]{1,0:T(8,128)(2,1)} %bitcast.25), channel_id=1, source_target_pairs={{0,2},{1,3},{2,0},{3,1},{4,6},{5,7},{6,4},{7,5},{8,10},{9,11},{10,... | collective-permute-start | bytes 393224 | tf_op jit(solution)/shard_map/ppermute | solution.py:22
  8.1 18.9 %collective-permute-start.11 = (bf16[128,512]{1,0:T(8,128)(2,1)}, bf16[128,512]{1,0:T(8,128)(2,1)S(1)}, u32[]{:S(2)}, u32[]{:S(2)}) collective-permute-start(bf16[128,512]{1,0:T(8,128)(2,1)} %bitcast.26), channel_id=1, source_target_pairs={{0,1},{1,0},{2,3},{3,2},{4,5},{5,4},{6,7},{7,6},{8,9},{9,8},{10,11... | collective-permute-start | bytes 393224 | tf_op jit(solution)/shard_map/ppermute | solution.py:22
  15.5 24.2 %copy-start.5 = (bf16[128,512]{1,0:T(8,128)(2,1)}, bf16[128,512]{1,0:T(8,128)(2,1)S(1)}, u32[]{:S(2)}) copy-start(bf16[128,512]{1,0:T(8,128)(2,1)S(1)} %collective-permute-done.2.refs_12_) | copy-start | bytes 393220
  17.0 22.6 %copy-start.6 = (bf16[128,512]{1,0:T(8,128)(2,1)}, bf16[128,512]{1,0:T(8,128)(2,1)S(1)}, u32[]{:S(2)}) copy-start(bf16[128,512]{1,0:T(8,128)(2,1)S(1)} %collective-permute-done.1.refs_8_) | copy-start | bytes 393220
  17.0 22.2 %copy-start.7 = (bf16[128,512]{1,0:T(8,128)(2,1)}, bf16[128,512]{1,0:T(8,128)(2,1)S(1)}, u32[]{:S(2)}) copy-start(bf16[128,512]{1,0:T(8,128)(2,1)S(1)} %collective-permute-done.refs_4_) | copy-start | bytes 393220
  18.1 5.2 %collective-permute-start.3 = (f16[144,512]{1,0:T(8,128)(2,1)S(1)}, f16[144,512]{1,0:T(8,128)(2,1)S(1)}, u32[]{:S(2)}, u32[]{:S(2)}) collective-permute-start(f16[144,512]{1,0:T(8,128)(2,1)S(1)} %convert_element_type.21), channel_id=1, source_target_pairs={{0,2},{1,3},{2,0},{3,1},{4,6},{5,7},{6,4},{7,5},{8,10},{9,11},{10,... | collective-permute-start | bytes 442376 | tf_op jit(solution)/shard_map/ppermute | solution.py:22
  19.7 19.9 %copy-start.8 = (bf16[128,512]{1,0:T(8,128)(2,1)}, bf16[128,512]{1,0:T(8,128)(2,1)S(1)}, u32[]{:S(2)}) copy-start(bf16[128,512]{1,0:T(8,128)(2,1)S(1)} %collective-permute-done.7.refs_2_) | copy-start | bytes 393220
  19.7 7.3 %collective-permute-start.12 = (bf16[128,512]{1,0:T(8,128)(2,1)S(1)}, bf16[128,512]{1,0:T(8,128)(2,1)S(1)}, u32[]{:S(2)}, u32[]{:S(2)}) collective-permute-start(bf16[128,512]{1,0:T(8,128)(2,1)S(1)} %collective-permute-done.7.refs_2_), channel_id=1, source_target_pairs={{0,1},{1,0},{2,3},{3,2},{4,5},{5,4},{6,7},{7,6},{8,9},{9,8},{10,11... | collective-permute-start | bytes 393224 | tf_op jit(solution)/shard_map/ppermute | solution.py:22
  23.4 15.2 %collective-permute-start.6 = (f16[2,144,512]{2,1,0:T(8,128)(2,1)S(1)}, f16[2,144,512]{2,1,0:T(8,128)(2,1)S(1)}, u32[]{:S(2)}, u32[]{:S(2)}) collective-permute-start(f16[2,144,512]{2,1,0:T(8,128)(2,1)S(1)} %pad_maximum_fusion), channel_id=1, source_target_pairs={{0,20},{1,21},{2,22},{3,23},{4,16},{5,17},{6,18},{7,19},{8,28},{9,... | collective-permute-start | bytes 884744 | tf_op jit(solution)/shard_map/ppermute | solution.py:64
  25.3 13.9 %collective-permute-start.5 = (f16[2,144,512]{2,1,0:T(8,128)(2,1)S(1)}, f16[2,144,512]{2,1,0:T(8,128)(2,1)S(1)}, u32[]{:S(2)}, u32[]{:S(2)}) collective-permute-start(f16[2,144,512]{2,1,0:T(8,128)(2,1)S(1)} %pad_maximum_fusion), channel_id=1, source_target_pairs={{0,16},{1,17},{2,18},{3,19},{4,20},{5,21},{6,22},{7,23},{8,24},{9,... | collective-permute-start | bytes 884744 | tf_op jit(solution)/shard_map/ppermute | solution.py:64
  25.8 13.4 %collective-permute-start.4 = (f16[2,144,512]{2,1,0:T(8,128)(2,1)S(1)}, f16[2,144,512]{2,1,0:T(8,128)(2,1)S(1)}, u32[]{:S(2)}, u32[]{:S(2)}) collective-permute-start(f16[2,144,512]{2,1,0:T(8,128)(2,1)S(1)} %pad_maximum_fusion), channel_id=1, source_target_pairs={{0,4},{1,5},{2,6},{3,7},{4,0},{5,1},{6,2},{7,3},{8,12},{9,13},{10,... | collective-permute-start | bytes 884744 | tf_op jit(solution)/shard_map/ppermute | solution.py:64
  27.0 12.7 %copy-start.9 = (bf16[128,512]{1,0:T(8,128)(2,1)}, bf16[128,512]{1,0:T(8,128)(2,1)S(1)}, u32[]{:S(2)}) copy-start(bf16[128,512]{1,0:T(8,128)(2,1)S(1)} %collective-permute-done.11.refs_1_) | copy-start | bytes 393220
  27.0 1.6 %collective-permute-start.13 = (bf16[128,512]{1,0:T(8,128)(2,1)S(1)}, bf16[128,512]{1,0:T(8,128)(2,1)S(1)}, u32[]{:S(2)}, u32[]{:S(2)}) collective-permute-start(bf16[128,512]{1,0:T(8,128)(2,1)S(1)} %collective-permute-done.refs_4_), channel_id=1, source_target_pairs={{0,1},{1,0},{2,3},{3,2},{4,5},{5,4},{6,7},{7,6},{8,9},{9,8},{10,11... | collective-permute-start | bytes 393224 | tf_op jit(solution)/shard_map/ppermute | solution.py:22
  27.0 12.7 %copy-start.10 = (bf16[128,512]{1,0:T(8,128)(2,1)}, bf16[128,512]{1,0:T(8,128)(2,1)S(1)}, u32[]{:S(2)}) copy-start(bf16[128,512]{1,0:T(8,128)(2,1)S(1)} %collective-permute-done.12.refs_3_) | copy-start | bytes 393220
  27.0 6.5 %collective-permute-start.8 = (bf16[128,512]{1,0:T(8,128)(2,1)S(1)}, bf16[128,512]{1,0:T(8,128)(2,1)}, u32[]{:S(2)}, u32[]{:S(2)}) collective-permute-start(bf16[128,512]{1,0:T(8,128)(2,1)S(1)} %collective-permute-done.refs_4_), channel_id=1, source_target_pairs={{0,2},{1,3},{2,0},{3,1},{4,6},{5,7},{6,4},{7,5},{8,10},{9,11},{10,... | collective-permute-start | bytes 393224 | tf_op jit(solution)/shard_map/ppermute | solution.py:22
  28.6 11.1 %copy-start.11 = (bf16[128,512]{1,0:T(8,128)(2,1)}, bf16[128,512]{1,0:T(8,128)(2,1)S(1)}, u32[]{:S(2)}) copy-start(bf16[128,512]{1,0:T(8,128)(2,1)S(1)} %collective-permute-done.13.refs_5_) | copy-start | bytes 393220
  28.6 7.6 %collective-permute-start.9 = (bf16[128,512]{1,0:T(8,128)(2,1)S(1)}, bf16[128,512]{1,0:T(8,128)(2,1)}, u32[]{:S(2)}, u32[]{:S(2)}) collective-permute-start(bf16[128,512]{1,0:T(8,128)(2,1)S(1)} %collective-permute-done.1.refs_8_), channel_id=1, source_target_pairs={{0,2},{1,3},{2,0},{3,1},{4,6},{5,7},{6,4},{7,5},{8,10},{9,11},{10,... | collective-permute-start | bytes 393224 | tf_op jit(solution)/shard_map/ppermute | solution.py:22
  33.5 5.2 %collective-permute-start.10 = (bf16[128,512]{1,0:T(8,128)(2,1)S(1)}, bf16[128,512]{1,0:T(8,128)(2,1)}, u32[]{:S(2)}, u32[]{:S(2)}) collective-permute-start(bf16[128,512]{1,0:T(8,128)(2,1)S(1)} %collective-permute-done.2.refs_12_), channel_id=1, source_target_pairs={{0,2},{1,3},{2,0},{3,1},{4,6},{5,7},{6,4},{7,5},{8,10},{9,11},{10,... | collective-permute-start | bytes 393224 | tf_op jit(solution)/shard_map/ppermute | solution.py:22
  36.2 7.3 %collective-permute-start.15 = (bf16[128,512]{1,0:T(8,128)(2,1)S(1)}, bf16[128,512]{1,0:T(8,128)(2,1)}, u32[]{:S(2)}, u32[]{:S(2)}) collective-permute-start(bf16[128,512]{1,0:T(8,128)(2,1)S(1)} %collective-permute-done.1.refs_8_), channel_id=1, source_target_pairs={{0,1},{1,0},{2,3},{3,2},{4,5},{5,4},{6,7},{7,6},{8,9},{9,8},{10,11... | collective-permute-start | bytes 393224 | tf_op jit(solution)/shard_map/ppermute | solution.py:22
  38.6 4.9 %collective-permute-start.17 = (bf16[128,512]{1,0:T(8,128)(2,1)S(1)}, bf16[128,512]{1,0:T(8,128)(2,1)}, u32[]{:S(2)}, u32[]{:S(2)}) collective-permute-start(bf16[128,512]{1,0:T(8,128)(2,1)S(1)} %collective-permute-done.2.refs_12_), channel_id=1, source_target_pairs={{0,1},{1,0},{2,3},{3,2},{4,5},{5,4},{6,7},{7,6},{8,9},{9,8},{10,11... | collective-permute-start | bytes 393224 | tf_op jit(solution)/shard_map/ppermute | solution.py:22
  38.6 4.9 %collective-permute-start.14 = (bf16[128,512]{1,0:T(8,128)(2,1)}, bf16[128,512]{1,0:T(8,128)(2,1)}, u32[]{:S(2)}, u32[]{:S(2)}) collective-permute-start(bf16[128,512]{1,0:T(8,128)(2,1)} %collective-permute-done.8.refs_6_), channel_id=1, source_target_pairs={{0,1},{1,0},{2,3},{3,2},{4,5},{5,4},{6,7},{7,6},{8,9},{9,8},{10,11... | collective-permute-start | bytes 393224 | tf_op jit(solution)/shard_map/ppermute | solution.py:22
  39.1 4.4 %collective-permute-start.16 = (bf16[128,512]{1,0:T(8,128)(2,1)}, bf16[128,512]{1,0:T(8,128)(2,1)}, u32[]{:S(2)}, u32[]{:S(2)}) collective-permute-start(bf16[128,512]{1,0:T(8,128)(2,1)} %collective-permute-done.9.refs_10_), channel_id=1, source_target_pairs={{0,1},{1,0},{2,3},{3,2},{4,5},{5,4},{6,7},{7,6},{8,9},{9,8},{10,11... | collective-permute-start | bytes 393224 | tf_op jit(solution)/shard_map/ppermute | solution.py:22
  39.2 4.4 %collective-permute-start.18 = (bf16[128,512]{1,0:T(8,128)(2,1)}, bf16[128,512]{1,0:T(8,128)(2,1)}, u32[]{:S(2)}, u32[]{:S(2)}) collective-permute-start(bf16[128,512]{1,0:T(8,128)(2,1)} %collective-permute-done.10.refs_14_), channel_id=1, source_target_pairs={{0,1},{1,0},{2,3},{3,2},{4,5},{5,4},{6,7},{7,6},{8,9},{9,8},{10,11... | collective-permute-start | bytes 393224 | tf_op jit(solution)/shard_map/ppermute | solution.py:22
  39.7 44.5 %all-to-all-start = ((bf16[16,512,128]{2,1,0:T(8,128)(2,1)}), bf16[16,512,128]{2,1,0:T(8,128)(2,1)S(1)}, u32[]{:S(2)}, u32[]{:S(2)}) async-start(bf16[16,512,128]{2,1,0:T(8,128)(2,1)} %bitcast.17), calls=%async_computation | async-start | bytes 4194304 | tf_op jit(solution)/shard_map/all_to_all | solution.py:504
  59.3 0.8 copy-start.3
  59.5 22.9 %collective-permute-start.25 = (f16[8,144,512]{2,1,0:T(8,128)(2,1)S(1)}, f16[8,144,512]{2,1,0:T(8,128)(2,1)S(1)}, u32[]{:S(2)}, u32[]{:S(2)}) collective-permute-start(f16[8,144,512]{2,1,0:T(8,128)(2,1)S(1)} %constant_dynamic-update-slice_fusion), channel_id=1, source_target_pairs={{0,1},{1,0},{2,3},{3,2},{4,5},{5,4},{6,7},{7,6},{8,9},{9,8},{10,11... | collective-permute-start | bytes 3538952 | tf_op jit(solution)/shard_map/ppermute | solution.py:22
  60.0 2.5 %collective-permute-start.19 = (f32[2,8,4,128]{3,2,1,0:T(4,128)S(1)}, f32[2,8,4,128]{3,2,1,0:T(4,128)S(1)}, u32[]{:S(2)}, u32[]{:S(2)}) collective-permute-start(f32[2,8,4,128]{3,2,1,0:T(4,128)S(1)} %copy-done.3), channel_id=1, source_target_pairs={{0,1},{1,0},{2,3},{3,2},{4,5},{5,4},{6,7},{7,6},{8,9},{9,8},{10,11... | collective-permute-start | bytes 98312 | tf_op jit(solution)/shard_map/ppermute | solution.py:22
  62.5 6.4 %collective-permute-start.20 = (f32[2,8,4,128]{3,2,1,0:T(4,128)S(1)}, f32[2,8,4,128]{3,2,1,0:T(4,128)S(1)}, u32[]{:S(2)}, u32[]{:S(2)}) collective-permute-start(f32[2,8,4,128]{3,2,1,0:T(4,128)S(1)} %add.15), channel_id=1, source_target_pairs={{0,2},{1,3},{2,0},{3,1},{4,6},{5,7},{6,4},{7,5},{8,10},{9,11},{10,... | collective-permute-start | bytes 98312 | tf_op jit(solution)/shard_map/ppermute | solution.py:22
  68.9 5.0 %collective-permute-start.21 = (f32[8,4,128]{2,1,0:T(4,128)S(1)}, f32[8,4,128]{2,1,0:T(4,128)S(1)}, u32[]{:S(2)}, u32[]{:S(2)}) collective-permute-start(f32[8,4,128]{2,1,0:T(4,128)S(1)} %get-tuple-element.64), channel_id=1, source_target_pairs={{0,4},{1,5},{2,6},{3,7},{4,0},{5,1},{6,2},{7,3},{8,12},{9,13},{10,... | collective-permute-start | bytes 49160 | tf_op jit(solution)/shard_map/ppermute | solution.py:22
  71.4 5.7 %collective-permute-start.23 = (f32[8,4,128]{2,1,0:T(4,128)S(1)}, f32[8,4,128]{2,1,0:T(4,128)S(1)}, u32[]{:S(2)}, u32[]{:S(2)}) collective-permute-start(f32[8,4,128]{2,1,0:T(4,128)S(1)} %get-tuple-element.65), channel_id=1, source_target_pairs={{0,12},{1,13},{2,14},{3,15},{4,8},{5,9},{6,10},{7,11},{8,4},{9,5},... | collective-permute-start | bytes 49160 | tf_op jit(solution)/shard_map/ppermute | solution.py:22
  73.4 4.6 %collective-permute-start.22 = (f32[8,4,128]{2,1,0:T(4,128)S(1)}, f32[8,4,128]{2,1,0:T(4,128)S(1)}, u32[]{:S(2)}, u32[]{:S(2)}) collective-permute-start(f32[8,4,128]{2,1,0:T(4,128)S(1)} %get-tuple-element.65), channel_id=1, source_target_pairs={{0,8},{1,9},{2,10},{3,11},{4,12},{5,13},{6,14},{7,15},{8,0},{9,1},... | collective-permute-start | bytes 49160 | tf_op jit(solution)/shard_map/ppermute | solution.py:22
  78.0 4.4 %copy-start.2 = (f32[8,4,128]{2,1,0:T(4,128)}, f32[8,4,128]{2,1,0:T(4,128)S(1)}, u32[]{:S(2)}) copy-start(f32[8,4,128]{2,1,0:T(4,128)S(1)} %add_add_fusion.refs_0_) | copy-start | bytes 49156
  78.0 6.1 %collective-permute-start.24 = (f32[8,4,128]{2,1,0:T(4,128)S(1)}, f32[8,4,128]{2,1,0:T(4,128)S(1)}, u32[]{:S(2)}, u32[]{:S(2)}) collective-permute-start(f32[8,4,128]{2,1,0:T(4,128)S(1)} %add_add_fusion.refs_0_), channel_id=1, source_target_pairs={{0,16},{16,0},{1,17},{17,1},{2,18},{18,2},{3,19},{19,3},{4,20},{20... | collective-permute-start | bytes 49160 | tf_op jit(solution)/shard_map/ppermute | solution.py:22
  84.2 0.6 copy-start.4
  84.2 1.4 %copy-start = (bf16[16,512,128]{2,1,0:T(8,128)(2,1)}, bf16[16,512,128]{2,1,0:T(8,128)(2,1)S(1)}, u32[]{:S(2)}) copy-start(bf16[16,512,128]{2,1,0:T(8,128)(2,1)S(1)} %all-to-all-done.columns_ref) | copy-start | bytes 6291460
  92.9 13.4 %collective-permute-start.26 = (f16[272,512]{1,0:T(8,128)(2,1)S(1)}, f16[272,512]{1,0:T(8,128)(2,1)S(1)}, u32[]{:S(2)}, u32[]{:S(2)}) collective-permute-start(f16[272,512]{1,0:T(8,128)(2,1)S(1)} %reduce-precision_convert_fusion), channel_id=1, source_target_pairs={{0,8},{1,9},{2,10},{3,11},{4,12},{5,13},{6,14},{7,15},{8,0},{9,1},... | collective-permute-start | bytes 835592 | tf_op jit(solution)/shard_map/ppermute | solution.py:22
  109.5 18.2 %all-to-all-start.1 = ((f32[32,24,128]{2,1,0:T(8,128)}), f32[32,24,128]{2,1,0:T(8,128)S(1)}, u32[]{:S(2)}, u32[]{:S(2)}) async-start(f32[32,24,128]{2,1,0:T(8,128)} %get-tuple-element.55), calls=%async_computation.1 | async-start | bytes 786432 | tf_op jit(solution)/shard_map/all_to_all | solution.py:531
  115.4 11.4 %collective-permute-start.27 = (f16[272,512]{1,0:T(8,128)(2,1)S(1)}, f16[272,512]{1,0:T(8,128)(2,1)S(1)}, u32[]{:S(2)}, u32[]{:S(2)}) collective-permute-start(f16[272,512]{1,0:T(8,128)(2,1)S(1)} %get-tuple-element.62), channel_id=1, source_target_pairs={{0,16},{16,0},{1,17},{17,1},{2,18},{18,2},{3,19},{19,3},{4,20},{20... | collective-permute-start | bytes 835592 | tf_op jit(solution)/shard_map/ppermute | solution.py:22
  127.7 0.8 copy-start.1

commit v5 on v4

--- a/solution.py
+++ b/solution.py
@@ -22,23 +22,33 @@
     return lax.ppermute(value, axis, [(i, i ^ mask) for i in range(lax.axis_size(axis))])
 
 
-def gather_far(value, axis):
-    top = lax.axis_size(axis) // 4
-    return [value] + [swap(value, axis, step * top) for step in (1, 2, 3)]
-
-
-def gather_even(far, axis):
-    top = lax.axis_size(axis) // 4
-    slots = {step * top: far[step] for step in range(4)}
-    for mask in range(2, top, 2):
-        for step in range(4):
-            slots[step * top + mask] = swap(slots[step * top], axis, mask)
-    return [slots[k] for k in range(0, 4 * top, 2)]
-
-
-def gather_odd(even, axis):
-    pairs = [(slot, swap(slot, axis, 1)) for slot in even]
-    return [slot for pair in pairs for slot in pair]
+def far_groups(amount):
+    top = amount // 4
+    return [[0], [top], [2 * top, 3 * top]]
+
+
+def key_masks(amount):
+    masks = []
+    for near in range(0, amount // 4, 2):
+        for group in far_groups(amount):
+            masks += [[mask ^ near for mask in group], [mask ^ near ^ 1 for mask in group]]
+    return masks
+
+
+def far_keys(value):
+    top = lax.axis_size("seq") // 4
+    return [swap(value, "seq", step * top) for step in (1, 2, 3)]
+
+
+def key_stacks(value, far):
+    stacks, arrived = [], []
+    for near in range(0, lax.axis_size("seq") // 4, 2):
+        for stack in (value[None], far[0][None], jnp.stack(far[1:])):
+            if near:
+                stack = swap(stack, "seq", near)
+                arrived.append(stack)
+            stacks += [stack, swap(stack, "seq", 1)]
+    return stacks, arrived
 
 
 def near_order(amount):
@@ -188,9 +198,11 @@
 
 
 def attention_kernel(slots, order_ref, query_ref, *refs):
-    key_refs, mass_ref = refs[:slots], refs[slots]
-    keys, bias, scores, shares = refs[slots + 1 :]
-    rows = key_refs[0].shape[0]
+    masks = key_masks(slots)
+    key_refs, mass_ref = refs[: len(masks)], refs[len(masks)]
+    keys, bias, scores, shares = refs[len(masks) + 1 :]
+    rows = query_ref.shape[0]
+    from_slot = {mask: (i, j) for i, group in enumerate(masks) for j, mask in enumerate(group)}
     total = rows * slots
     lanes = scores.shape[2]
     fold = lanes // rows
@@ -210,7 +222,8 @@
     for k in range(slots):
         at = pl.ds(k * rows, rows)
         for head in range(KEY_VALUE_HEADS):
-            keys[head, at, :] = key_refs[k][:, head * HEAD_SIZE : (head + 1) * HEAD_SIZE]
+            i, j = from_slot[k]
+            keys[head, at, :] = key_refs[i][j, :, head * HEAD_SIZE : (head + 1) * HEAD_SIZE]
         bias[at, :] = jnp.where(pos_of(me ^ k, key_index) <= query_pos, 0.0, -1e30)
 
     def visit_head(head, carried):
@@ -264,9 +277,8 @@
     lax.fori_loop(0, KEY_VALUE_HEADS, visit_head, 0)
 
 
-def attention_mass(block_order, queries, key_slots):
-    slots = len(key_slots)
-    rows = key_slots[0].shape[0]
+def attention_mass(block_order, queries, stacks, slots):
+    rows = queries.shape[0]
     total = rows * slots
     lanes = 2 * rows
     work = total * rows * KEY_VALUE_HEADS * QUERY_GROUP_SIZE
@@ -274,7 +286,7 @@
     return pl.pallas_call(
         functools.partial(attention_kernel, slots),
         out_shape=jax.ShapeDtypeStruct(shape, jnp.float32),
-        in_specs=[SMEM] + [VMEM] * (slots + 1),
+        in_specs=[SMEM] + [VMEM] * (len(stacks) + 1),
         out_specs=VMEM,
         scratch_shapes=[
             pltpu.VMEM((KEY_VALUE_HEADS, total, HEAD_SIZE), jnp.bfloat16),
@@ -286,7 +298,7 @@
         cost_estimate=pl.CostEstimate(
             flops=100 * work * HEAD_SIZE, bytes_accessed=2 * queries.size, transcendentals=work
         ),
-    )(block_order, queries, *key_slots)
+    )(block_order, queries, *stacks)
 
 
 def gradient_kernel(slots, columns_ref, output_ref, hidden_ref, *refs):
@@ -485,15 +497,15 @@
     units = first_weight.shape[1]
     tokens = hidden_states.reshape(rows, model)
 
-    key_far = gather_far(rotated_key_rows.reshape(rows, -1), "seq")
+    keys = rotated_key_rows.reshape(rows, -1)
+    far = far_keys(keys)
     turned, hidden, falls = prepare(
         tokens, first_weight, first_bias, output_weight, output_bias, seq
     )
-    falls, *far = lax.optimization_barrier((falls, *key_far[1:]))
-    key_even = gather_even(key_far[:1] + far, "seq")
+    falls, *far = lax.optimization_barrier((falls, *far))
+    stacks, arrived = key_stacks(keys, far)
     falls = gather_near(falls.astype(jnp.float16))
-    key_slots = gather_odd(key_even, "seq")
-    turned, falls, *_ = lax.optimization_barrier((turned, falls, *key_even))
+    turned, _ = lax.optimization_barrier((turned, arrived[1]))
 
     side = seq // 2
     groups = [
@@ -504,13 +516,16 @@
     columns = lax.all_to_all(
         turned.reshape(seq, -1, rows), ("dp", "seq"), 0, 0, tiled=True, axis_index_groups=groups
     )
-    message = attention_mass(block_order, queries.reshape(rows, -1), key_slots)
+    front, *falls = lax.optimization_barrier((queries.reshape(rows, -1), *falls))
+    message = attention_mass(block_order, front, stacks, seq)
     message, *falls = lax.optimization_barrier((message, *falls))
     falls = jnp.concatenate(falls, axis=0)
     falls = [falls.astype(jnp.float32), swap(falls, "seq", 1).astype(jnp.float32)]
-    mask = 1
+    message = message + swap(message, "seq", 1)
+    mask = 2
     while mask < seq // 4:
-        message = message + swap(message, "seq", mask)
+        other, *falls = lax.optimization_barrier((swap(message, "seq", mask), *falls))
+        message = message + other
         mask *= 2
     top = seq // 4
     message = (message[0] + swap(message[0], "seq", top)) + (
@@ -526,8 +541,8 @@
         mask *= 2
     other = swap(halved(send)[1], "seq", side).astype(jnp.float32)
     total, small = squares(small, keep, other, dp * seq)
-    total, sent = halved(total)
-    totals = [total, swap(sent, "dp", 1).astype(jnp.float32)]
+    sent, total = lax.optimization_barrier((halved(total)[1], total))
+    totals = [halved(total)[0], swap(sent, "dp", 1).astype(jnp.float32)]
     message = lax.all_to_all(small, ("dp", "seq"), 0, 0, tiled=True)
     step_first, second, bias_step, bias, loss = scaled(
         message, totals, seq, model * units * (dp // 2)

time: 132 us -> 128 us (0.970)
  waiting for transfers between devices: 45 us -> 42.2 us
    ppermute x25 -> x22, waiting for transfers between devices: 45 us -> 38.4 us  [swap(): lax.ppermute(value, axis, [(i, i ^ mask) for i in range(lax.axis_size(axi...]
    ppermute x3, waiting for transfers between devices: 0.01 us -> 3.8 us  [gather_near(): gathered.append(lax.ppermute(stacked, ('dp', 'seq'), pairs))]
    ppermute x25 -> x22, starting transfers between devices: 26.6 us -> 25 us  [swap(): lax.ppermute(value, axis, [(i, i ^ mask) for i in range(lax.axis_size(axi...]
  transfers between devices with their start and end apart: 30 -> 27, of which waited for: 11 -> 12; matrix products, arithmetic and copies ran while one was open for 7% -> 7% of each run, Pallas kernels for 18% -> 18%
where the time goes in v5:
time: 128 us
  waiting for transfers between devices  42.2 us (33%)
  starting transfers between devices  37 us (29%)
  Pallas kernels  34 us (27%)
  other arithmetic  11.1 us (9%)
  local copies, waits for them, and re-layouts  2.49 us (2%)
    ppermute x22, waiting for transfers between devices, swap(): lax.ppermute(value, axis, [(i, i ^ mask) for i in range(lax.axis_size(axi...  38.4 us
    ppermute x22, starting transfers between devices, swap(): lax.ppermute(value, axis, [(i, i ^ mask) for i in range(lax.axis_size(axi...  25 us
    pallas_call x1, Pallas kernels, attention_mass(): pl.pallas_call(functools.partial(attention_kernel, slots), out_shape=jax....  15.6 us
    pallas_call x1, Pallas kernels, prepare(): pl.pallas_call(functools.partial(prepare_kernel, chunks), out_shape=(jax....  7.45 us
    pallas_call x1, Pallas kernels, gradient(): pl.pallas_call(functools.partial(gradient_kernel, slots), out_shape=(jax....  6.03 us
    all_to_all x1, starting transfers between devices, per_device(): message = lax.all_to_all(small, ('dp', 'seq'), 0, 0, tiled=True)  4.69 us
    ppermute x3, waiting for transfers between devices, gather_near(): gathered.append(lax.ppermute(stacked, ('dp', 'seq'), pairs))  3.8 us
    all_to_all x1, starting transfers between devices, per_device(): lax.all_to_all(turned.reshape(seq, -1, rows), ('dp', 'seq'), 0, 0, tiled=...  3.72 us
  transfers between devices with their start and end apart: 27, of which 12 were waited for; matrix products, arithmetic and copies ran while one was open for 7% of the time, Pallas kernels for 18%

profile of v5, /device:TPU:0, one launch (start us, length us, event | category | flops | bytes accessed | tf_op | source)
XLA Modules:
  0.0 127.6 jit_solution(17398144760268089341)
XLA Ops:
  0.6 5.1 %collective-permute-start.2 = (bf16[128,512]{1,0:T(8,128)(2,1)}, bf16[128,512]{1,0:T(8,128)(2,1)S(1)}, u32[]{:S(2)}, u32[]{:S(2)}) collective-permute-start(bf16[128,512]{1,0:T(8,128)(2,1)} %bitcast.27), channel_id=1, source_target_pairs={{0,12},{1,13},{2,14},{3,15},{4,8},{5,9},{6,10},{7,11},{8,4},{9,5},... | collective-permute-start | bytes 393224 | tf_op jit(solution)/shard_map/ppermute | solution.py:22
  5.8 0.6 collective-permute-start
  6.4 1.7 %collective-permute-start.11 = (bf16[1,128,512]{2,1,0:T(8,128)(2,1)}, bf16[1,128,512]{2,1,0:T(8,128)(2,1)}, u32[]{:S(2)}, u32[]{:S(2)}) collective-permute-start(bf16[1,128,512]{2,1,0:T(8,128)(2,1)} %refs_0_.1), channel_id=1, source_target_pairs={{0,2},{1,3},{2,0},{3,1},{4,6},{5,7},{6,4},{7,5},{8,10},{9,11},{10,... | collective-permute-start | bytes 393224 | tf_op jit(solution)/shard_map/ppermute | solution.py:22
  8.1 7.4 %shard_map.127 = (bf16[16,2,256,128]{3,2,1,0:T(8,128)(2,1)}, bf16[128,512]{1,0:T(8,128)(2,1)}, f32[144,512]{1,0:T(8,128)}) custom-call(bf16[128,8192]{1,0:T(8,128)(2,1)} %bitcast.21, bf16[8192,512]{1,0:T(8,128)(2,1)} %weight_ref.1, f32[1,512]{1,0:T(1,128)} %bitcast.25, bf16[4,512]{1,0:T(4,128)(2,1)} %output_ref.3, f32[4]{0:T(128)} %output_bias_ref.1), custom_call_target="tpu_custom_call" | custom-call | flops 1073741824 | bytes 12582912 | tf_op jit(solution)/shard_map/pallas_call | solution.py:176
  15.5 1.5 %collective-permute-done.1 = bf16[128,512]{1,0:T(8,128)(2,1)S(1)} collective-permute-done((bf16[128,512]{1,0:T(8,128)(2,1)}, bf16[128,512]{1,0:T(8,128)(2,1)S(1)}, u32[]{:S(2)}, u32[]{:S(2)}) %collective-permute-start.1) | collective-permute-done | bytes 131104 | tf_op jit(solution)/shard_map/ppermute | solution.py:22
  17.0 1.0 convert_element_type.21
  18.0 1.6 %collective-permute-start.4 = (f16[144,512]{1,0:T(8,128)(2,1)S(1)}, f16[144,512]{1,0:T(8,128)(2,1)S(1)}, u32[]{:S(2)}, u32[]{:S(2)}) collective-permute-start(f16[144,512]{1,0:T(8,128)(2,1)S(1)} %convert_element_type.21), channel_id=1, source_target_pairs={{0,2},{1,3},{2,0},{3,1},{4,6},{5,7},{6,4},{7,5},{8,10},{9,11},{10,... | collective-permute-start | bytes 442376 | tf_op jit(solution)/shard_map/ppermute | solution.py:22
  19.6 1.0 convert_bitcast_fusion
  20.6 0.6 collective-permute-start.14
  21.2 3.2 %collective-permute-done.4 = f16[144,512]{1,0:T(8,128)(2,1)S(1)} collective-permute-done((f16[144,512]{1,0:T(8,128)(2,1)S(1)}, f16[144,512]{1,0:T(8,128)(2,1)S(1)}, u32[]{:S(2)}, u32[]{:S(2)}) %collective-permute-start.4) | collective-permute-done | bytes 147488 | tf_op jit(solution)/shard_map/ppermute | solution.py:22
  24.4 1.3 %collective-permute-start.7 = (f16[2,144,512]{2,1,0:T(8,128)(2,1)S(1)}, f16[2,144,512]{2,1,0:T(8,128)(2,1)S(1)}, u32[]{:S(2)}, u32[]{:S(2)}) collective-permute-start(f16[2,144,512]{2,1,0:T(8,128)(2,1)S(1)} %pad_maximum_fusion), channel_id=1, source_target_pairs={{0,20},{1,21},{2,22},{3,23},{4,16},{5,17},{6,18},{7,19},{8,28},{9,... | collective-permute-start | bytes 884744 | tf_op jit(solution)/shard_map/ppermute | solution.py:74
  25.8 0.5 collective-permute-start.6
  26.3 1.7 %collective-permute-start.5 = (f16[2,144,512]{2,1,0:T(8,128)(2,1)S(1)}, f16[2,144,512]{2,1,0:T(8,128)(2,1)S(1)}, u32[]{:S(2)}, u32[]{:S(2)}) collective-permute-start(f16[2,144,512]{2,1,0:T(8,128)(2,1)S(1)} %pad_maximum_fusion), channel_id=1, source_target_pairs={{0,4},{1,5},{2,6},{3,7},{4,0},{5,1},{6,2},{7,3},{8,12},{9,13},{10,... | collective-permute-start | bytes 884744 | tf_op jit(solution)/shard_map/ppermute | solution.py:74
  28.0 2.0 %collective-permute-start.3 = (bf16[1,128,512]{2,1,0:T(8,128)(2,1)}, bf16[1,128,512]{2,1,0:T(8,128)(2,1)}, u32[]{:S(2)}, u32[]{:S(2)}) collective-permute-start(bf16[1,128,512]{2,1,0:T(8,128)(2,1)} %bitcast.3.refs_2_), channel_id=1, source_target_pairs={{0,2},{1,3},{2,0},{3,1},{4,6},{5,7},{6,4},{7,5},{8,10},{9,11},{10,... | collective-permute-start | bytes 393224 | tf_op jit(solution)/shard_map/ppermute | solution.py:22
  30.0 3.3 %collective-permute-done.3.refs_8_ = bf16[1,128,512]{2,1,0:T(8,128)(2,1)} collective-permute-done((bf16[1,128,512]{2,1,0:T(8,128)(2,1)}, bf16[1,128,512]{2,1,0:T(8,128)(2,1)}, u32[]{:S(2)}, u32[]{:S(2)}) %collective-permute-start.3) | collective-permute-done | bytes 131104 | tf_op jit(solution)/shard_map/ppermute | solution.py:22
  33.3 0.5 collective-permute-start.15
  33.8 0.8 collective-permute-done.7
  34.6 3.0 %collective-permute-done.6 = f16[2,144,512]{2,1,0:T(8,128)(2,1)S(1)} collective-permute-done((f16[2,144,512]{2,1,0:T(8,128)(2,1)S(1)}, f16[2,144,512]{2,1,0:T(8,128)(2,1)S(1)}, u32[]{:S(2)}, u32[]{:S(2)}) %collective-permute-start.6) | collective-permute-done | bytes 294944 | tf_op jit(solution)/shard_map/ppermute | solution.py:74
  37.6 0.5 collective-permute-start.13
  38.1 3.7 %all-to-all-start = ((bf16[16,512,128]{2,1,0:T(8,128)(2,1)}), bf16[16,512,128]{2,1,0:T(8,128)(2,1)S(1)}, u32[]{:S(2)}, u32[]{:S(2)}) async-start(bf16[16,512,128]{2,1,0:T(8,128)(2,1)} %bitcast.20), calls=%async_computation | async-start | bytes 4194304 | tf_op jit(solution)/shard_map/all_to_all | solution.py:516
  41.9 15.6 %shard_map.128 = f32[2,8,4,128]{3,2,1,0:T(4,128)} custom-call(s32[32]{0:T(128)} %order_ref.1, bf16[128,4096]{1,0:T(8,128)(2,1)} %bitcast.26, bf16[1,128,512]{2,1,0:T(8,128)(2,1)} %refs_0_.1, bf16[1,128,512]{2,1,0:T(8,128)(2,1)} %collective-permute-done.8.refs_1_, bf16[1,128,512]{2,1,0:T(8,128)(2,1)} %bitcast.3.refs_2_, ...), custom_call_target="tpu_custom_call" | custom-call | flops 107374182400 | bytes 1048576 | tf_op jit(solution)/shard_map/pallas_call | solution.py:286
  58.6 2.2 %collective-permute-done.16 = f32[2,8,4,128]{3,2,1,0:T(4,128)S(1)} collective-permute-done((f32[2,8,4,128]{3,2,1,0:T(4,128)S(1)}, f32[2,8,4,128]{3,2,1,0:T(4,128)S(1)}, u32[]{:S(2)}, u32[]{:S(2)}) %collective-permute-start.16) | collective-permute-done | bytes 32800 | tf_op jit(solution)/shard_map/ppermute | solution.py:22
  60.7 1.9 %collective-permute-start.17 = (f32[2,8,4,128]{3,2,1,0:T(4,128)S(1)}, f32[2,8,4,128]{3,2,1,0:T(4,128)S(1)}, u32[]{:S(2)}, u32[]{:S(2)}) collective-permute-start(f32[2,8,4,128]{3,2,1,0:T(4,128)S(1)} %add.15), channel_id=1, source_target_pairs={{0,2},{1,3},{2,0},{3,1},{4,6},{5,7},{6,4},{7,5},{8,10},{9,11},{10,... | collective-permute-start | bytes 98312 | tf_op jit(solution)/shard_map/ppermute | solution.py:22
  62.6 1.8 %convert_element_type.22.refs_2_ = f32[8,144,512]{2,1,0:T(8,128)} convert(f16[8,144,512]{2,1,0:T(8,128)(2,1)S(1)} %constant_dynamic-update-slice_fusion) | non-fusion elementwise | flops 589824 | bytes 3538944 | tf_op jit(solution)/shard_map/convert_element_type | solution.py:523
  64.4 1.8 %convert_element_type.23.refs_3_ = f32[8,144,512]{2,1,0:T(8,128)} convert(f16[8,144,512]{2,1,0:T(8,128)(2,1)S(1)} %collective-permute-done.18) | non-fusion elementwise | flops 589824 | bytes 3538944 | tf_op jit(solution)/shard_map/convert_element_type | solution.py:523
  66.1 0.9 collective-permute-done.17
  67.1 2.5 %collective-permute-start.19 = (f32[8,4,128]{2,1,0:T(4,128)S(1)}, f32[8,4,128]{2,1,0:T(4,128)S(1)}, u32[]{:S(2)}, u32[]{:S(2)}) collective-permute-start(f32[8,4,128]{2,1,0:T(4,128)S(1)} %get-tuple-element.74), channel_id=1, source_target_pairs={{0,4},{1,5},{2,6},{3,7},{4,0},{5,1},{6,2},{7,3},{8,12},{9,13},{10,... | collective-permute-start | bytes 49160 | tf_op jit(solution)/shard_map/ppermute | solution.py:22
  69.6 2.3 %collective-permute-start.21 = (f32[8,4,128]{2,1,0:T(4,128)S(1)}, f32[8,4,128]{2,1,0:T(4,128)S(1)}, u32[]{:S(2)}, u32[]{:S(2)}) collective-permute-start(f32[8,4,128]{2,1,0:T(4,128)S(1)} %get-tuple-element.75), channel_id=1, source_target_pairs={{0,12},{1,13},{2,14},{3,15},{4,8},{5,9},{6,10},{7,11},{8,4},{9,5},... | collective-permute-start | bytes 49160 | tf_op jit(solution)/shard_map/ppermute | solution.py:22
  71.9 0.5 collective-permute-start.20
  72.4 2.7 %collective-permute-done.21 = f32[8,4,128]{2,1,0:T(4,128)S(1)} collective-permute-done((f32[8,4,128]{2,1,0:T(4,128)S(1)}, f32[8,4,128]{2,1,0:T(4,128)S(1)}, u32[]{:S(2)}, u32[]{:S(2)}) %collective-permute-start.21) | collective-permute-done | bytes 16416 | tf_op jit(solution)/shard_map/ppermute | solution.py:22
  75.1 1.4 %collective-permute-done.20 = f32[8,4,128]{2,1,0:T(4,128)S(1)} collective-permute-done((f32[8,4,128]{2,1,0:T(4,128)S(1)}, f32[8,4,128]{2,1,0:T(4,128)S(1)}, u32[]{:S(2)}, u32[]{:S(2)}) %collective-permute-start.20) | collective-permute-done | bytes 16416 | tf_op jit(solution)/shard_map/ppermute | solution.py:22
  76.6 2.6 %collective-permute-start.22 = (f32[8,4,128]{2,1,0:T(4,128)S(1)}, f32[8,4,128]{2,1,0:T(4,128)S(1)}, u32[]{:S(2)}, u32[]{:S(2)}) collective-permute-start(f32[8,4,128]{2,1,0:T(4,128)S(1)} %add_add_fusion.refs_0_), channel_id=1, source_target_pairs={{0,16},{16,0},{1,17},{17,1},{2,18},{18,2},{3,19},{19,3},{4,20},{20... | collective-permute-start | bytes 49160 | tf_op jit(solution)/shard_map/ppermute | solution.py:22
  79.2 1.7 %collective-permute-done.22.refs_1_ = f32[8,4,128]{2,1,0:T(4,128)S(1)} collective-permute-done((f32[8,4,128]{2,1,0:T(4,128)S(1)}, f32[8,4,128]{2,1,0:T(4,128)S(1)}, u32[]{:S(2)}, u32[]{:S(2)}) %collective-permute-start.22) | collective-permute-done | bytes 16416 | tf_op jit(solution)/shard_map/ppermute | solution.py:22
  80.9 0.6 copy-done.6
  81.5 0.8 copy-done
  82.3 6.0 %shard_map.129 = (f32[256,512]{1,0:T(8,128)}, f32[272,512]{1,0:T(8,128)}, f32[4,128]{1,0:T(4,128)}, f32[24,128]{1,0:T(8,128)}) custom-call(bf16[16,512,128]{2,1,0:T(8,128)(2,1)} %copy-done, bf16[4,512]{1,0:T(4,128)(2,1)} %output_ref.3, bf16[128,512]{1,0:T(8,128)(2,1)} %get-tuple-element.44.hidden_ref, f32[8,4,128]{2,1,0:T(4,128)} %copy-done.4, ...), custom_call_target="tpu_custom_call" | custom-call | flops 1073741824 | bytes 10485760 | tf_op jit(solution)/shard_map/pallas_call | solution.py:377
  88.3 1.3 %reduce-precision_convert_fusion.1 = f16[272,512]{1,0:T(8,128)(2,1)S(1)} fusion(f32[272,512]{1,0:T(8,128)} %get-tuple-element.64), kind=kLoop, calls=%fused_computation.1 | loop fusion | flops 278528 | bytes 835584 | tf_op jit(solution)/shard_map/convert_element_type | solution.py:93
  89.7 12.7 %collective-permute-done.23 = f16[272,512]{1,0:T(8,128)(2,1)S(1)} collective-permute-done((f16[272,512]{1,0:T(8,128)(2,1)S(1)}, f16[272,512]{1,0:T(8,128)(2,1)S(1)}, u32[]{:S(2)}, u32[]{:S(2)}) %collective-permute-start.23) | collective-permute-done | bytes 278560 | tf_op jit(solution)/shard_map/ppermute | solution.py:22
  102.4 0.9 convert_element_type.25.other_ref
  103.3 2.3 %shard_map.130 = (f32[272,512]{1,0:T(8,128)}, f32[32,24,128]{2,1,0:T(8,128)}) custom-call(f32[24,128]{1,0:T(8,128)} %get-tuple-element.62.small_ref, f32[256,512]{1,0:T(8,128)} %get-tuple-element.63.keep_ref, f32[272,512]{1,0:T(8,128)} %convert_element_type.25.other_ref), custom_call_target="tpu_custom_call" | custom-call | tf_op jit(solution)/shard_map/pallas_call | solution.py:418
  105.6 4.7 %all-to-all-start.1 = ((f32[32,24,128]{2,1,0:T(8,128)}), f32[32,24,128]{2,1,0:T(8,128)S(1)}, u32[]{:S(2)}, u32[]{:S(2)}) async-start(f32[32,24,128]{2,1,0:T(8,128)} %get-tuple-element.65), calls=%async_computation.1 | async-start | bytes 786432 | tf_op jit(solution)/shard_map/all_to_all | solution.py:546
  110.3 1.3 %reduce-precision_convert_fusion = f16[272,512]{1,0:T(8,128)(2,1)S(1)} fusion(f32[272,512]{1,0:T(8,128)} %get-tuple-element.67), kind=kLoop, calls=%fused_computation | loop fusion | flops 278528 | bytes 835584 | tf_op jit(solution)/shard_map/convert_element_type | solution.py:93
  111.6 1.8 %collective-permute-start.24 = (f16[272,512]{1,0:T(8,128)(2,1)S(1)}, f16[272,512]{1,0:T(8,128)(2,1)S(1)}, u32[]{:S(2)}, u32[]{:S(2)}) collective-permute-start(f16[272,512]{1,0:T(8,128)(2,1)S(1)} %reduce-precision_convert_fusion), channel_id=1, source_target_pairs={{0,16},{16,0},{1,17},{17,1},{2,18},{18,2},{3,19},{19,3},{4,20},{20... | collective-permute-start | bytes 835592 | tf_op jit(solution)/shard_map/ppermute | solution.py:22
  113.5 1.1 reduce_precision.11.refs_0_
  114.5 8.9 %collective-permute-done.24 = f16[272,512]{1,0:T(8,128)(2,1)S(1)} collective-permute-done((f16[272,512]{1,0:T(8,128)(2,1)S(1)}, f16[272,512]{1,0:T(8,128)(2,1)S(1)}, u32[]{:S(2)}, u32[]{:S(2)}) %collective-permute-start.24) | collective-permute-done | bytes 278560 | tf_op jit(solution)/shard_map/ppermute | solution.py:22
  123.4 0.9 convert_element_type.27.refs_1_
  124.3 0.7 copy-done.2
  125.1 2.6 %shard_map.131 = (f32[512,512]{1,0:T(8,128)}, f32[4,512]{1,0:T(4,128)}, f32[1,512]{1,0:T(1,128)}, f32[4]{0:T(128)}, f32[1]{0:T(128)}) custom-call(f32[32,24,128]{2,1,0:T(8,128)} %copy-done.2, f32[272,512]{1,0:T(8,128)} %reduce_precision.11.refs_0_, f32[272,512]{1,0:T(8,128)} %convert_element_type.27.refs_1_), custom_call_target="tpu_custom_call" | custom-call | tf_op jit(solution)/shard_map/pallas_call | solution.py:470
  (44 shorter events, 1.3 us)
Async XLA Ops:
  0.6 14.9 %collective-permute-start.2 = (bf16[128,512]{1,0:T(8,128)(2,1)}, bf16[128,512]{1,0:T(8,128)(2,1)S(1)}, u32[]{:S(2)}, u32[]{:S(2)}) collective-permute-start(bf16[128,512]{1,0:T(8,128)(2,1)} %bitcast.27), channel_id=1, source_target_pairs={{0,12},{1,13},{2,14},{3,15},{4,8},{5,9},{6,10},{7,11},{8,4},{9,5},... | collective-permute-start | bytes 393224 | tf_op jit(solution)/shard_map/ppermute | solution.py:22
  5.7 11.3 %collective-permute-start.1 = (bf16[128,512]{1,0:T(8,128)(2,1)}, bf16[128,512]{1,0:T(8,128)(2,1)S(1)}, u32[]{:S(2)}, u32[]{:S(2)}) collective-permute-start(bf16[128,512]{1,0:T(8,128)(2,1)} %bitcast.28), channel_id=1, source_target_pairs={{0,8},{1,9},{2,10},{3,11},{4,12},{5,13},{6,14},{7,15},{8,0},{9,1},... | collective-permute-start | bytes 393224 | tf_op jit(solution)/shard_map/ppermute | solution.py:22
  5.8 11.3 %collective-permute-start = (bf16[128,512]{1,0:T(8,128)(2,1)}, bf16[128,512]{1,0:T(8,128)(2,1)}, u32[]{:S(2)}, u32[]{:S(2)}) collective-permute-start(bf16[128,512]{1,0:T(8,128)(2,1)} %bitcast.29), channel_id=1, source_target_pairs={{0,4},{1,5},{2,6},{3,7},{4,0},{5,1},{6,2},{7,3},{8,12},{9,13},{10,... | collective-permute-start | bytes 393224 | tf_op jit(solution)/shard_map/ppermute | solution.py:22
  6.4 19.9 %collective-permute-start.8 = (bf16[1,128,512]{2,1,0:T(8,128)(2,1)}, bf16[1,128,512]{2,1,0:T(8,128)(2,1)}, u32[]{:S(2)}, u32[]{:S(2)}) collective-permute-start(bf16[1,128,512]{2,1,0:T(8,128)(2,1)} %refs_0_.1), channel_id=1, source_target_pairs={{0,1},{1,0},{2,3},{3,2},{4,5},{5,4},{6,7},{7,6},{8,9},{9,8},{10,11... | collective-permute-start | bytes 393224 | tf_op jit(solution)/shard_map/ppermute | solution.py:22
  6.4 21.6 %collective-permute-start.11 = (bf16[1,128,512]{2,1,0:T(8,128)(2,1)}, bf16[1,128,512]{2,1,0:T(8,128)(2,1)}, u32[]{:S(2)}, u32[]{:S(2)}) collective-permute-start(bf16[1,128,512]{2,1,0:T(8,128)(2,1)} %refs_0_.1), channel_id=1, source_target_pairs={{0,2},{1,3},{2,0},{3,1},{4,6},{5,7},{6,4},{7,5},{8,10},{9,11},{10,... | collective-permute-start | bytes 393224 | tf_op jit(solution)/shard_map/ppermute | solution.py:22
  18.0 6.3 %collective-permute-start.4 = (f16[144,512]{1,0:T(8,128)(2,1)S(1)}, f16[144,512]{1,0:T(8,128)(2,1)S(1)}, u32[]{:S(2)}, u32[]{:S(2)}) collective-permute-start(f16[144,512]{1,0:T(8,128)(2,1)S(1)} %convert_element_type.21), channel_id=1, source_target_pairs={{0,2},{1,3},{2,0},{3,1},{4,6},{5,7},{6,4},{7,5},{8,10},{9,11},{10,... | collective-permute-start | bytes 442376 | tf_op jit(solution)/shard_map/ppermute | solution.py:22
  20.6 17.5 %copy-start.3 = (bf16[2,128,512]{2,1,0:T(8,128)(2,1)}, bf16[2,128,512]{2,1,0:T(8,128)(2,1)S(1)}, u32[]{:S(2)}) copy-start(bf16[2,128,512]{2,1,0:T(8,128)(2,1)S(1)} %pad_maximum_fusion.1.refs_4_) | copy-start | bytes 786436
  20.6 12.7 %collective-permute-start.14 = (bf16[2,128,512]{2,1,0:T(8,128)(2,1)S(1)}, bf16[2,128,512]{2,1,0:T(8,128)(2,1)}, u32[]{:S(2)}, u32[]{:S(2)}) collective-permute-start(bf16[2,128,512]{2,1,0:T(8,128)(2,1)S(1)} %pad_maximum_fusion.1.refs_4_), channel_id=1, source_target_pairs={{0,2},{1,3},{2,0},{3,1},{4,6},{5,7},{6,4},{7,5},{8,10},{9,11},{10,... | collective-permute-start | bytes 786440 | tf_op jit(solution)/shard_map/ppermute | solution.py:22
  24.4 10.1 %collective-permute-start.7 = (f16[2,144,512]{2,1,0:T(8,128)(2,1)S(1)}, f16[2,144,512]{2,1,0:T(8,128)(2,1)S(1)}, u32[]{:S(2)}, u32[]{:S(2)}) collective-permute-start(f16[2,144,512]{2,1,0:T(8,128)(2,1)S(1)} %pad_maximum_fusion), channel_id=1, source_target_pairs={{0,20},{1,21},{2,22},{3,23},{4,16},{5,17},{6,18},{7,19},{8,28},{9,... | collective-permute-start | bytes 884744 | tf_op jit(solution)/shard_map/ppermute | solution.py:74
  25.8 11.8 %collective-permute-start.6 = (f16[2,144,512]{2,1,0:T(8,128)(2,1)S(1)}, f16[2,144,512]{2,1,0:T(8,128)(2,1)S(1)}, u32[]{:S(2)}, u32[]{:S(2)}) collective-permute-start(f16[2,144,512]{2,1,0:T(8,128)(2,1)S(1)} %pad_maximum_fusion), channel_id=1, source_target_pairs={{0,16},{1,17},{2,18},{3,19},{4,20},{5,21},{6,22},{7,23},{8,24},{9,... | collective-permute-start | bytes 884744 | tf_op jit(solution)/shard_map/ppermute | solution.py:74
  26.3 11.3 %collective-permute-start.5 = (f16[2,144,512]{2,1,0:T(8,128)(2,1)S(1)}, f16[2,144,512]{2,1,0:T(8,128)(2,1)S(1)}, u32[]{:S(2)}, u32[]{:S(2)}) collective-permute-start(f16[2,144,512]{2,1,0:T(8,128)(2,1)S(1)} %pad_maximum_fusion), channel_id=1, source_target_pairs={{0,4},{1,5},{2,6},{3,7},{4,0},{5,1},{6,2},{7,3},{8,12},{9,13},{10,... | collective-permute-start | bytes 884744 | tf_op jit(solution)/shard_map/ppermute | solution.py:74
  28.0 5.3 %collective-permute-start.3 = (bf16[1,128,512]{2,1,0:T(8,128)(2,1)}, bf16[1,128,512]{2,1,0:T(8,128)(2,1)}, u32[]{:S(2)}, u32[]{:S(2)}) collective-permute-start(bf16[1,128,512]{2,1,0:T(8,128)(2,1)} %bitcast.3.refs_2_), channel_id=1, source_target_pairs={{0,2},{1,3},{2,0},{3,1},{4,6},{5,7},{6,4},{7,5},{8,10},{9,11},{10,... | collective-permute-start | bytes 393224 | tf_op jit(solution)/shard_map/ppermute | solution.py:22
  33.3 8.6 %collective-permute-start.10 = (bf16[2,128,512]{2,1,0:T(8,128)(2,1)S(1)}, bf16[2,128,512]{2,1,0:T(8,128)(2,1)}, u32[]{:S(2)}, u32[]{:S(2)}) collective-permute-start(bf16[2,128,512]{2,1,0:T(8,128)(2,1)S(1)} %pad_maximum_fusion.1.refs_4_), channel_id=1, source_target_pairs={{0,1},{1,0},{2,3},{3,2},{4,5},{5,4},{6,7},{7,6},{8,9},{9,8},{10,11... | collective-permute-start | bytes 786440 | tf_op jit(solution)/shard_map/ppermute | solution.py:22
  33.3 8.6 %collective-permute-start.15 = (bf16[2,128,512]{2,1,0:T(8,128)(2,1)}, bf16[2,128,512]{2,1,0:T(8,128)(2,1)}, u32[]{:S(2)}, u32[]{:S(2)}) collective-permute-start(bf16[2,128,512]{2,1,0:T(8,128)(2,1)} %collective-permute-done.14.refs_10_), channel_id=1, source_target_pairs={{0,1},{1,0},{2,3},{3,2},{4,5},{5,4},{6,7},{7,6},{8,9},{9,8},{10,11... | collective-permute-start | bytes 786440 | tf_op jit(solution)/shard_map/ppermute | solution.py:22
  34.6 7.3 %collective-permute-start.9 = (bf16[1,128,512]{2,1,0:T(8,128)(2,1)}, bf16[1,128,512]{2,1,0:T(8,128)(2,1)}, u32[]{:S(2)}, u32[]{:S(2)}) collective-permute-start(bf16[1,128,512]{2,1,0:T(8,128)(2,1)} %bitcast.3.refs_2_), channel_id=1, source_target_pairs={{0,1},{1,0},{2,3},{3,2},{4,5},{5,4},{6,7},{7,6},{8,9},{9,8},{10,11... | collective-permute-start | bytes 393224 | tf_op jit(solution)/shard_map/ppermute | solution.py:22
  37.6 4.2 %collective-permute-start.12 = (bf16[1,128,512]{2,1,0:T(8,128)(2,1)}, bf16[1,128,512]{2,1,0:T(8,128)(2,1)}, u32[]{:S(2)}, u32[]{:S(2)}) collective-permute-start(bf16[1,128,512]{2,1,0:T(8,128)(2,1)} %collective-permute-done.11.refs_6_), channel_id=1, source_target_pairs={{0,1},{1,0},{2,3},{3,2},{4,5},{5,4},{6,7},{7,6},{8,9},{9,8},{10,11... | collective-permute-start | bytes 393224 | tf_op jit(solution)/shard_map/ppermute | solution.py:22
  37.6 4.3 %collective-permute-start.13 = (bf16[1,128,512]{2,1,0:T(8,128)(2,1)}, bf16[1,128,512]{2,1,0:T(8,128)(2,1)}, u32[]{:S(2)}, u32[]{:S(2)}) collective-permute-start(bf16[1,128,512]{2,1,0:T(8,128)(2,1)} %collective-permute-done.3.refs_8_), channel_id=1, source_target_pairs={{0,1},{1,0},{2,3},{3,2},{4,5},{5,4},{6,7},{7,6},{8,9},{9,8},{10,11... | collective-permute-start | bytes 393224 | tf_op jit(solution)/shard_map/ppermute | solution.py:22
  38.1 42.8 %all-to-all-start = ((bf16[16,512,128]{2,1,0:T(8,128)(2,1)}), bf16[16,512,128]{2,1,0:T(8,128)(2,1)S(1)}, u32[]{:S(2)}, u32[]{:S(2)}) async-start(bf16[16,512,128]{2,1,0:T(8,128)(2,1)} %bitcast.20), calls=%async_computation | async-start | bytes 4194304 | tf_op jit(solution)/shard_map/all_to_all | solution.py:516
  57.5 0.8 copy-start.5
  57.7 6.6 %collective-permute-start.18 = (f16[8,144,512]{2,1,0:T(8,128)(2,1)S(1)}, f16[8,144,512]{2,1,0:T(8,128)(2,1)S(1)}, u32[]{:S(2)}, u32[]{:S(2)}) collective-permute-start(f16[8,144,512]{2,1,0:T(8,128)(2,1)S(1)} %constant_dynamic-update-slice_fusion), channel_id=1, source_target_pairs={{0,1},{1,0},{2,3},{3,2},{4,5},{5,4},{6,7},{7,6},{8,9},{9,8},{10,11... | collective-permute-start | bytes 3538952 | tf_op jit(solution)/shard_map/ppermute | solution.py:22
  58.3 2.4 %collective-permute-start.16 = (f32[2,8,4,128]{3,2,1,0:T(4,128)S(1)}, f32[2,8,4,128]{3,2,1,0:T(4,128)S(1)}, u32[]{:S(2)}, u32[]{:S(2)}) collective-permute-start(f32[2,8,4,128]{3,2,1,0:T(4,128)S(1)} %copy-done.5), channel_id=1, source_target_pairs={{0,1},{1,0},{2,3},{3,2},{4,5},{5,4},{6,7},{7,6},{8,9},{9,8},{10,11... | collective-permute-start | bytes 98312 | tf_op jit(solution)/shard_map/ppermute | solution.py:22
  60.7 6.3 %collective-permute-start.17 = (f32[2,8,4,128]{3,2,1,0:T(4,128)S(1)}, f32[2,8,4,128]{3,2,1,0:T(4,128)S(1)}, u32[]{:S(2)}, u32[]{:S(2)}) collective-permute-start(f32[2,8,4,128]{3,2,1,0:T(4,128)S(1)} %add.15), channel_id=1, source_target_pairs={{0,2},{1,3},{2,0},{3,1},{4,6},{5,7},{6,4},{7,5},{8,10},{9,11},{10,... | collective-permute-start | bytes 98312 | tf_op jit(solution)/shard_map/ppermute | solution.py:22
  67.1 5.4 %collective-permute-start.19 = (f32[8,4,128]{2,1,0:T(4,128)S(1)}, f32[8,4,128]{2,1,0:T(4,128)S(1)}, u32[]{:S(2)}, u32[]{:S(2)}) collective-permute-start(f32[8,4,128]{2,1,0:T(4,128)S(1)} %get-tuple-element.74), channel_id=1, source_target_pairs={{0,4},{1,5},{2,6},{3,7},{4,0},{5,1},{6,2},{7,3},{8,12},{9,13},{10,... | collective-permute-start | bytes 49160 | tf_op jit(solution)/shard_map/ppermute | solution.py:22
  69.6 5.5 %collective-permute-start.21 = (f32[8,4,128]{2,1,0:T(4,128)S(1)}, f32[8,4,128]{2,1,0:T(4,128)S(1)}, u32[]{:S(2)}, u32[]{:S(2)}) collective-permute-start(f32[8,4,128]{2,1,0:T(4,128)S(1)} %get-tuple-element.75), channel_id=1, source_target_pairs={{0,12},{1,13},{2,14},{3,15},{4,8},{5,9},{6,10},{7,11},{8,4},{9,5},... | collective-permute-start | bytes 49160 | tf_op jit(solution)/shard_map/ppermute | solution.py:22
  71.9 4.6 %collective-permute-start.20 = (f32[8,4,128]{2,1,0:T(4,128)S(1)}, f32[8,4,128]{2,1,0:T(4,128)S(1)}, u32[]{:S(2)}, u32[]{:S(2)}) collective-permute-start(f32[8,4,128]{2,1,0:T(4,128)S(1)} %get-tuple-element.75), channel_id=1, source_target_pairs={{0,8},{1,9},{2,10},{3,11},{4,12},{5,13},{6,14},{7,15},{8,0},{9,1},... | collective-permute-start | bytes 49160 | tf_op jit(solution)/shard_map/ppermute | solution.py:22
  76.6 4.3 %copy-start.4 = (f32[8,4,128]{2,1,0:T(4,128)}, f32[8,4,128]{2,1,0:T(4,128)S(1)}, u32[]{:S(2)}) copy-start(f32[8,4,128]{2,1,0:T(4,128)S(1)} %add_add_fusion.refs_0_) | copy-start | bytes 49156
  76.6 4.3 %collective-permute-start.22 = (f32[8,4,128]{2,1,0:T(4,128)S(1)}, f32[8,4,128]{2,1,0:T(4,128)S(1)}, u32[]{:S(2)}, u32[]{:S(2)}) collective-permute-start(f32[8,4,128]{2,1,0:T(4,128)S(1)} %add_add_fusion.refs_0_), channel_id=1, source_target_pairs={{0,16},{16,0},{1,17},{17,1},{2,18},{18,2},{3,19},{19,3},{4,20},{20... | collective-permute-start | bytes 49160 | tf_op jit(solution)/shard_map/ppermute | solution.py:22
  80.9 0.6 copy-start.6
  80.9 1.4 %copy-start = (bf16[16,512,128]{2,1,0:T(8,128)(2,1)}, bf16[16,512,128]{2,1,0:T(8,128)(2,1)S(1)}, u32[]{:S(2)}) copy-start(bf16[16,512,128]{2,1,0:T(8,128)(2,1)S(1)} %all-to-all-done.columns_ref) | copy-start | bytes 6291460
  89.6 12.7 %collective-permute-start.23 = (f16[272,512]{1,0:T(8,128)(2,1)S(1)}, f16[272,512]{1,0:T(8,128)(2,1)S(1)}, u32[]{:S(2)}, u32[]{:S(2)}) collective-permute-start(f16[272,512]{1,0:T(8,128)(2,1)S(1)} %reduce-precision_convert_fusion.1), channel_id=1, source_target_pairs={{0,8},{1,9},{2,10},{3,11},{4,12},{5,13},{6,14},{7,15},{8,0},{9,1},... | collective-permute-start | bytes 835592 | tf_op jit(solution)/shard_map/ppermute | solution.py:22
  105.6 7.9 %copy-start.1 = (f32[272,512]{1,0:T(8,128)S(1)}, f32[272,512]{1,0:T(8,128)}, u32[]{:S(2)}) copy-start(f32[272,512]{1,0:T(8,128)} %get-tuple-element.67) | copy-start | bytes 1671172
  105.6 18.7 %all-to-all-start.1 = ((f32[32,24,128]{2,1,0:T(8,128)}), f32[32,24,128]{2,1,0:T(8,128)S(1)}, u32[]{:S(2)}, u32[]{:S(2)}) async-start(f32[32,24,128]{2,1,0:T(8,128)} %get-tuple-element.65), calls=%async_computation.1 | async-start | bytes 786432 | tf_op jit(solution)/shard_map/all_to_all | solution.py:546
  111.6 11.8 %collective-permute-start.24 = (f16[272,512]{1,0:T(8,128)(2,1)S(1)}, f16[272,512]{1,0:T(8,128)(2,1)S(1)}, u32[]{:S(2)}, u32[]{:S(2)}) collective-permute-start(f16[272,512]{1,0:T(8,128)(2,1)S(1)} %reduce-precision_convert_fusion), channel_id=1, source_target_pairs={{0,16},{16,0},{1,17},{17,1},{2,18},{18,2},{3,19},{19,3},{4,20},{20... | collective-permute-start | bytes 835592 | tf_op jit(solution)/shard_map/ppermute | solution.py:22
  124.3 0.7 copy-start.2

commit v6 on v5

--- a/solution.py
+++ b/solution.py
@@ -13,7 +13,8 @@
 QUERY_GROUP_SIZE = 8
 LOG2_E = 1.4426950408889634
 PREDICTED_SCALE = 1.0 / 16.0
-VMEM_LIMIT = 60 * 1024 * 1024
+VMEM_LIMIT = 40 * 1024 * 1024
+PREPARE_VMEM_LIMIT = 60 * 1024 * 1024
 VMEM = pl.BlockSpec(memory_space=pltpu.VMEM)
 SMEM = pl.BlockSpec(memory_space=pltpu.SMEM)
 
@@ -188,7 +189,7 @@
             pltpu.VMEM((chunks, block // share, share, rows), jnp.bfloat16),
             pltpu.SemaphoreType.DMA((3, chunks)),
         ],
-        compiler_params=pltpu.CompilerParams(vmem_limit_bytes=VMEM_LIMIT),
+        compiler_params=pltpu.CompilerParams(vmem_limit_bytes=PREPARE_VMEM_LIMIT),
         cost_estimate=pl.CostEstimate(
             flops=2 * rows * model * units,
             bytes_accessed=2 * model * (units + 2 * rows),
@@ -518,7 +519,6 @@
     )
     front, *falls = lax.optimization_barrier((queries.reshape(rows, -1), *falls))
     message = attention_mass(block_order, front, stacks, seq)
-    message, *falls = lax.optimization_barrier((message, *falls))
     falls = jnp.concatenate(falls, axis=0)
     falls = [falls.astype(jnp.float32), swap(falls, "seq", 1).astype(jnp.float32)]
     message = message + swap(message, "seq", 1)

time: 128 us -> 115 us (0.90)
  Pallas kernels: 34 us -> 27.4 us
  other arithmetic: 11.1 us -> 5.1 us
  starting transfers between devices: 37 us -> 34.7 us
  waiting for transfers between devices: 42.2 us -> 44.3 us
    ppermute x22, starting transfers between devices: 25 us -> 21.6 us  [swap(): lax.ppermute(value, axis, [(i, i ^ mask) for i in range(lax.axis_size(axi...]
    convert_element_type x2, other arithmetic: 2.67 us -> 0.57 us  [halved(): return (value, value.astype(jnp.float16))]
    pallas_call x1, Pallas kernels: 15.6 us -> 13.6 us  [attention_mass(): pl.pallas_call(functools.partial(attention_kernel, slots), out_shape=jax....]
    ppermute x22, waiting for transfers between devices: 38.4 us -> 40.4 us  [swap(): lax.ppermute(value, axis, [(i, i ^ mask) for i in range(lax.axis_size(axi...]
    pallas_call x1, Pallas kernels: 6.03 us -> 4.15 us  [gradient(): pl.pallas_call(functools.partial(gradient_kernel, slots), out_shape=(jax....]
    convert_element_type x1, other arithmetic: 1.76 us -> 0.32 us  [per_device(): falls.astype(jnp.float32)]
    pallas_call x1, Pallas kernels: 2.34 us -> 0.96 us  [squares(): pl.pallas_call(square_kernel, out_shape=(jax.ShapeDtypeStruct(other.shape...]
    pallas_call x1, Pallas kernels: 2.57 us -> 1.24 us  [scaled(): pl.pallas_call(functools.partial(scale_kernel, slots, entries), out_shape...]
  transfers between devices with their start and end apart: 27 -> 27, of which waited for: 12 -> 14; matrix products, arithmetic and copies ran while one was open for 7% -> 4% of each run, Pallas kernels for 18% -> 18%
where the time goes in v6:
time: 115 us; the launch traced here: 114 us
  waiting for transfers between devices  44.3 us (39%)
  starting transfers between devices  34.7 us (30%)
  Pallas kernels  27.4 us (24%)
  other arithmetic  5.1 us (4%)
  local copies, waits for them, and re-layouts  1.89 us (2%)
    ppermute x22, waiting for transfers between devices, swap(): lax.ppermute(value, axis, [(i, i ^ mask) for i in range(lax.axis_size(axi...  40.4 us
    ppermute x22, starting transfers between devices, swap(): lax.ppermute(value, axis, [(i, i ^ mask) for i in range(lax.axis_size(axi...  21.6 us
    pallas_call x1, Pallas kernels, attention_mass(): pl.pallas_call(functools.partial(attention_kernel, slots), out_shape=jax....  13.6 us
    pallas_call x1, Pallas kernels, prepare(): pl.pallas_call(functools.partial(prepare_kernel, chunks), out_shape=(jax....  7.43 us
    all_to_all x1, starting transfers between devices, per_device(): message = lax.all_to_all(small, ('dp', 'seq'), 0, 0, tiled=True)  5.07 us
    all_to_all x1, starting transfers between devices, per_device(): lax.all_to_all(turned.reshape(seq, -1, rows), ('dp', 'seq'), 0, 0, tiled=...  4.44 us
    pallas_call x1, Pallas kernels, gradient(): pl.pallas_call(functools.partial(gradient_kernel, slots), out_shape=(jax....  4.15 us
    ppermute x3, waiting for transfers between devices, gather_near(): gathered.append(lax.ppermute(stacked, ('dp', 'seq'), pairs))  3.82 us
  transfers between devices with their start and end apart: 27, of which 14 were waited for; matrix products, arithmetic and copies ran while one was open for 4% of the time, Pallas kernels for 18%

profile of v6, /device:TPU:0, one launch (start us, length us, event | category | flops | bytes accessed | tf_op | source)
XLA Modules:
  0.0 114.3 jit_solution(3921587674111748134)
XLA Ops:
  0.6 5.1 %collective-permute-start.2 = (bf16[128,512]{1,0:T(8,128)(2,1)}, bf16[128,512]{1,0:T(8,128)(2,1)S(1)}, u32[]{:S(2)}, u32[]{:S(2)}) collective-permute-start(bf16[128,512]{1,0:T(8,128)(2,1)} %bitcast.21), channel_id=1, source_target_pairs={{0,12},{1,13},{2,14},{3,15},{4,8},{5,9},{6,10},{7,11},{8,4},{9,5},... | collective-permute-start | bytes 393224 | tf_op jit(solution)/shard_map/ppermute | solution.py:23
  5.8 0.6 collective-permute-start
  6.4 7.4 %shard_map.127 = (bf16[16,2,256,128]{3,2,1,0:T(8,128)(2,1)}, bf16[128,512]{1,0:T(8,128)(2,1)}, f32[144,512]{1,0:T(8,128)}) custom-call(bf16[128,8192]{1,0:T(8,128)(2,1)} %bitcast.28, bf16[8192,512]{1,0:T(8,128)(2,1)} %weight_ref.1, f32[1,512]{1,0:T(1,128)} %bitcast.32, bf16[4,512]{1,0:T(4,128)(2,1)} %output_ref.3, f32[4]{0:T(128)} %output_bias_ref.1), custom_call_target="tpu_custom_call" | custom-call | flops 1073741824 | bytes 12582912 | tf_op jit(solution)/shard_map/pallas_call | solution.py:177
  13.9 3.2 %collective-permute-done.1 = bf16[128,512]{1,0:T(8,128)(2,1)S(1)} collective-permute-done((bf16[128,512]{1,0:T(8,128)(2,1)}, bf16[128,512]{1,0:T(8,128)(2,1)S(1)}, u32[]{:S(2)}, u32[]{:S(2)}) %collective-permute-start.1) | collective-permute-done | bytes 131104 | tf_op jit(solution)/shard_map/ppermute | solution.py:23
  17.0 1.5 %collective-permute-start.3 = (bf16[1,128,512]{2,1,0:T(8,128)(2,1)S(1)}, bf16[1,128,512]{2,1,0:T(8,128)(2,1)S(1)}, u32[]{:S(2)}, u32[]{:S(2)}) collective-permute-start(bf16[1,128,512]{2,1,0:T(8,128)(2,1)S(1)} %bitcast.24), channel_id=1, source_target_pairs={{0,2},{1,3},{2,0},{3,1},{4,6},{5,7},{6,4},{7,5},{8,10},{9,11},{10,... | collective-permute-start | bytes 393224 | tf_op jit(solution)/shard_map/ppermute | solution.py:23
  18.6 1.0 convert_element_type.21
  19.5 0.6 collective-permute-start.4
  20.1 1.0 convert_bitcast_fusion
  21.1 4.1 %collective-permute-done.4 = f16[144,512]{1,0:T(8,128)(2,1)S(1)} collective-permute-done((f16[144,512]{1,0:T(8,128)(2,1)S(1)}, f16[144,512]{1,0:T(8,128)(2,1)S(1)}, u32[]{:S(2)}, u32[]{:S(2)}) %collective-permute-start.4) | collective-permute-done | bytes 147488 | tf_op jit(solution)/shard_map/ppermute | solution.py:23
  25.2 0.1 pad_maximum_fusion
  25.2 0.8 collective-permute-start.7
  26.1 0.8 collective-permute-start.6
  26.9 1.9 %collective-permute-start.5 = (f16[2,144,512]{2,1,0:T(8,128)(2,1)S(1)}, f16[2,144,512]{2,1,0:T(8,128)(2,1)S(1)}, u32[]{:S(2)}, u32[]{:S(2)}) collective-permute-start(f16[2,144,512]{2,1,0:T(8,128)(2,1)S(1)} %pad_maximum_fusion), channel_id=1, source_target_pairs={{0,4},{1,5},{2,6},{3,7},{4,0},{5,1},{6,2},{7,3},{8,12},{9,13},{10,... | collective-permute-start | bytes 884744 | tf_op jit(solution)/shard_map/ppermute | solution.py:75
  28.8 1.2 %collective-permute-start.14 = (bf16[2,128,512]{2,1,0:T(8,128)(2,1)S(1)}, bf16[2,128,512]{2,1,0:T(8,128)(2,1)S(1)}, u32[]{:S(2)}, u32[]{:S(2)}) collective-permute-start(bf16[2,128,512]{2,1,0:T(8,128)(2,1)S(1)} %pad_maximum_fusion.1.refs_4_), channel_id=1, source_target_pairs={{0,2},{1,3},{2,0},{3,1},{4,6},{5,7},{6,4},{7,5},{8,10},{9,11},{10,... | collective-permute-start | bytes 786440 | tf_op jit(solution)/shard_map/ppermute | solution.py:23
  30.0 0.9 collective-permute-start.11
  30.9 4.4 %all-to-all-start = ((bf16[16,512,128]{2,1,0:T(8,128)(2,1)}), bf16[16,512,128]{2,1,0:T(8,128)(2,1)}, u32[]{:S(2)}, u32[]{:S(2)}) async-start(bf16[16,512,128]{2,1,0:T(8,128)(2,1)} %bitcast.27), calls=%async_computation | async-start | bytes 4194304 | tf_op jit(solution)/shard_map/all_to_all | solution.py:517
  35.4 2.6 %collective-permute-done.11.refs_6_ = bf16[1,128,512]{2,1,0:T(8,128)(2,1)S(1)} collective-permute-done((bf16[1,128,512]{2,1,0:T(8,128)(2,1)S(1)}, bf16[1,128,512]{2,1,0:T(8,128)(2,1)S(1)}, u32[]{:S(2)}, u32[]{:S(2)}) %collective-permute-start.11) | collective-permute-done | bytes 131104 | tf_op jit(solution)/shard_map/ppermute | solution.py:23
  38.0 0.5 collective-permute-start.9
  38.5 1.9 %collective-permute-done.6 = f16[2,144,512]{2,1,0:T(8,128)(2,1)S(1)} collective-permute-done((f16[2,144,512]{2,1,0:T(8,128)(2,1)S(1)}, f16[2,144,512]{2,1,0:T(8,128)(2,1)S(1)}, u32[]{:S(2)}, u32[]{:S(2)}) %collective-permute-start.6) | collective-permute-done | bytes 294944 | tf_op jit(solution)/shard_map/ppermute | solution.py:75
  40.5 1.9 %collective-permute-done.5 = f16[2,144,512]{2,1,0:T(8,128)(2,1)S(1)} collective-permute-done((f16[2,144,512]{2,1,0:T(8,128)(2,1)S(1)}, f16[2,144,512]{2,1,0:T(8,128)(2,1)S(1)}, u32[]{:S(2)}, u32[]{:S(2)}) %collective-permute-start.5) | collective-permute-done | bytes 294944 | tf_op jit(solution)/shard_map/ppermute | solution.py:75
  42.5 0.6 collective-permute-start.13
  43.2 0.1 collective-permute-start.18
  43.3 0.8 collective-permute-done.13.refs_9_
  44.1 13.6 %shard_map.128 = f32[2,8,4,128]{3,2,1,0:T(4,128)S(1)} custom-call(s32[32]{0:T(128)S(1)} %copy-done.5, bf16[128,4096]{1,0:T(8,128)(2,1)S(1)} %bitcast.20, bf16[1,128,512]{2,1,0:T(8,128)(2,1)S(1)} %copy-done.4, bf16[1,128,512]{2,1,0:T(8,128)(2,1)S(1)} %collective-permute-done.8.refs_1_, bf16[1,128,512]{2,1,0:T(8,128)(2,1)S(1)} %bitcast.26, ...), custom_call_target="tpu_custom_call" | custom-call | flops 107374182400 | bytes 1048576 | tf_op jit(solution)/shard_map/pallas_call | solution.py:287
  57.7 0.4 collective-permute-start.16
  58.1 0.9 collective-permute-done.16
  59.1 0.3 convert_element_type.22.refs_2_
  59.5 1.7 %convert_element_type.23.refs_3_ = f32[8,144,512]{2,1,0:T(8,128)} convert(f16[8,144,512]{2,1,0:T(8,128)(2,1)S(1)} %collective-permute-done.18) | non-fusion elementwise | flops 589824 | bytes 3538944 | tf_op jit(solution)/shard_map/convert_element_type | solution.py:523
  61.2 3.9 %collective-permute-done.17 = f32[2,8,4,128]{3,2,1,0:T(4,128)S(1)} collective-permute-done((f32[2,8,4,128]{3,2,1,0:T(4,128)S(1)}, f32[2,8,4,128]{3,2,1,0:T(4,128)S(1)}, u32[]{:S(2)}, u32[]{:S(2)}) %collective-permute-start.17) | collective-permute-done | bytes 32800 | tf_op jit(solution)/shard_map/ppermute | solution.py:23
  65.3 0.6 collective-permute-start.21
  65.9 2.8 %collective-permute-start.20 = (f32[8,4,128]{2,1,0:T(4,128)S(1)}, f32[8,4,128]{2,1,0:T(4,128)S(1)}, u32[]{:S(2)}, u32[]{:S(2)}) collective-permute-start(f32[8,4,128]{2,1,0:T(4,128)S(1)} %get-tuple-element.65), channel_id=1, source_target_pairs={{0,8},{1,9},{2,10},{3,11},{4,12},{5,13},{6,14},{7,15},{8,0},{9,1},... | collective-permute-start | bytes 49160 | tf_op jit(solution)/shard_map/ppermute | solution.py:23
  68.7 0.2 collective-permute-done.19
  69.0 1.9 %collective-permute-done.21 = f32[8,4,128]{2,1,0:T(4,128)S(1)} collective-permute-done((f32[8,4,128]{2,1,0:T(4,128)S(1)}, f32[8,4,128]{2,1,0:T(4,128)S(1)}, u32[]{:S(2)}, u32[]{:S(2)}) %collective-permute-start.21) | collective-permute-done | bytes 16416 | tf_op jit(solution)/shard_map/ppermute | solution.py:23
  70.9 2.0 %collective-permute-start.22 = (f32[8,4,128]{2,1,0:T(4,128)S(1)}, f32[8,4,128]{2,1,0:T(4,128)S(1)}, u32[]{:S(2)}, u32[]{:S(2)}) collective-permute-start(f32[8,4,128]{2,1,0:T(4,128)S(1)} %add_add_fusion.refs_0_), channel_id=1, source_target_pairs={{0,16},{16,0},{1,17},{17,1},{2,18},{18,2},{3,19},{19,3},{4,20},{20... | collective-permute-start | bytes 49160 | tf_op jit(solution)/shard_map/ppermute | solution.py:23
  72.9 1.8 %collective-permute-done.22.refs_1_ = f32[8,4,128]{2,1,0:T(4,128)S(1)} collective-permute-done((f32[8,4,128]{2,1,0:T(4,128)S(1)}, f32[8,4,128]{2,1,0:T(4,128)S(1)}, u32[]{:S(2)}, u32[]{:S(2)}) %collective-permute-start.22) | collective-permute-done | bytes 16416 | tf_op jit(solution)/shard_map/ppermute | solution.py:23
  74.7 1.7 %copy-done = f32[8,144,512]{2,1,0:T(8,128)S(1)} copy-done((f32[8,144,512]{2,1,0:T(8,128)S(1)}, f32[8,144,512]{2,1,0:T(8,128)}, u32[]{:S(2)}) %copy-start) | copy-done | bytes 2359320
  76.4 4.1 %shard_map.129 = (f32[256,512]{1,0:T(8,128)S(1)}, f32[272,512]{1,0:T(8,128)S(1)}, f32[4,128]{1,0:T(4,128)}, f32[24,128]{1,0:T(8,128)S(1)}) custom-call(bf16[16,512,128]{2,1,0:T(8,128)(2,1)} %all-to-all-done.columns_ref, bf16[4,512]{1,0:T(4,128)(2,1)S(1)} %copy-done.2, bf16[128,512]{1,0:T(8,128)(2,1)S(1)} %copy-done.1, f32[8,4,128]{2,1,0:T(4,128)S(1)} %add_add_fusion.refs_0_, ...), custom_call_target="tpu_custom_call" | custom-call | flops 1073741824 | bytes 10485760 | tf_op jit(solution)/shard_map/pallas_call | solution.py:378
  80.5 0.3 reduce-precision_convert_fusion.1
  80.8 2.6 %collective-permute-start.23 = (f16[272,512]{1,0:T(8,128)(2,1)S(1)}, f16[272,512]{1,0:T(8,128)(2,1)S(1)}, u32[]{:S(2)}, u32[]{:S(2)}) collective-permute-start(f16[272,512]{1,0:T(8,128)(2,1)S(1)} %reduce-precision_convert_fusion.1), channel_id=1, source_target_pairs={{0,8},{1,9},{2,10},{3,11},{4,12},{5,13},{6,14},{7,15},{8,0},{9,1},... | collective-permute-start | bytes 835592 | tf_op jit(solution)/shard_map/ppermute | solution.py:23
  83.4 10.5 %collective-permute-done.23 = f16[272,512]{1,0:T(8,128)(2,1)S(1)} collective-permute-done((f16[272,512]{1,0:T(8,128)(2,1)S(1)}, f16[272,512]{1,0:T(8,128)(2,1)S(1)}, u32[]{:S(2)}, u32[]{:S(2)}) %collective-permute-start.23) | collective-permute-done | bytes 278560 | tf_op jit(solution)/shard_map/ppermute | solution.py:23
  93.9 1.0 shard_map.130
  94.8 5.1 %all-to-all-start.1 = ((f32[32,24,128]{2,1,0:T(8,128)}), f32[32,24,128]{2,1,0:T(8,128)S(1)}, u32[]{:S(2)}, u32[]{:S(2)}) async-start(f32[32,24,128]{2,1,0:T(8,128)} %get-tuple-element.55), calls=%async_computation.1 | async-start | bytes 786432 | tf_op jit(solution)/shard_map/all_to_all | solution.py:546
  99.9 0.3 reduce-precision_convert_fusion
  100.2 1.8 %collective-permute-start.24 = (f16[272,512]{1,0:T(8,128)(2,1)S(1)}, f16[272,512]{1,0:T(8,128)(2,1)S(1)}, u32[]{:S(2)}, u32[]{:S(2)}) collective-permute-start(f16[272,512]{1,0:T(8,128)(2,1)S(1)} %reduce-precision_convert_fusion), channel_id=1, source_target_pairs={{0,16},{16,0},{1,17},{17,1},{2,18},{18,2},{3,19},{19,3},{4,20},{20... | collective-permute-start | bytes 835592 | tf_op jit(solution)/shard_map/ppermute | solution.py:23
  102.0 0.3 reduce_precision.11.refs_0_
  102.3 10.5 %collective-permute-done.24 = f16[272,512]{1,0:T(8,128)(2,1)S(1)} collective-permute-done((f16[272,512]{1,0:T(8,128)(2,1)S(1)}, f16[272,512]{1,0:T(8,128)(2,1)S(1)}, u32[]{:S(2)}, u32[]{:S(2)}) %collective-permute-start.24) | collective-permute-done | bytes 278560 | tf_op jit(solution)/shard_map/ppermute | solution.py:23
  112.9 0.1 all-to-all-done.1.message_ref
  113.0 1.2 %shard_map.131 = (f32[512,512]{1,0:T(8,128)}, f32[4,512]{1,0:T(4,128)}, f32[1,512]{1,0:T(1,128)}, f32[4]{0:T(128)}, f32[1]{0:T(128)}) custom-call(f32[32,24,128]{2,1,0:T(8,128)S(1)} %all-to-all-done.1.message_ref, f32[272,512]{1,0:T(8,128)S(1)} %reduce_precision.11.refs_0_, f32[272,512]{1,0:T(8,128)S(1)} %convert_element_type.27.refs_1_), custom_call_target="tpu_custom_call" | custom-call | tf_op jit(solution)/shard_map/pallas_call | solution.py:471
  (42 shorter events, 0.7 us)
Async XLA Ops:
  0.6 13.2 %collective-permute-start.2 = (bf16[128,512]{1,0:T(8,128)(2,1)}, bf16[128,512]{1,0:T(8,128)(2,1)S(1)}, u32[]{:S(2)}, u32[]{:S(2)}) collective-permute-start(bf16[128,512]{1,0:T(8,128)(2,1)} %bitcast.21), channel_id=1, source_target_pairs={{0,12},{1,13},{2,14},{3,15},{4,8},{5,9},{6,10},{7,11},{8,4},{9,5},... | collective-permute-start | bytes 393224 | tf_op jit(solution)/shard_map/ppermute | solution.py:23
  5.7 11.3 %collective-permute-start.1 = (bf16[128,512]{1,0:T(8,128)(2,1)}, bf16[128,512]{1,0:T(8,128)(2,1)S(1)}, u32[]{:S(2)}, u32[]{:S(2)}) collective-permute-start(bf16[128,512]{1,0:T(8,128)(2,1)} %bitcast.22), channel_id=1, source_target_pairs={{0,8},{1,9},{2,10},{3,11},{4,12},{5,13},{6,14},{7,15},{8,0},{9,1},... | collective-permute-start | bytes 393224 | tf_op jit(solution)/shard_map/ppermute | solution.py:23
  5.8 11.3 %collective-permute-start = (bf16[128,512]{1,0:T(8,128)(2,1)}, bf16[128,512]{1,0:T(8,128)(2,1)S(1)}, u32[]{:S(2)}, u32[]{:S(2)}) collective-permute-start(bf16[128,512]{1,0:T(8,128)(2,1)} %bitcast.23), channel_id=1, source_target_pairs={{0,4},{1,5},{2,6},{3,7},{4,0},{5,1},{6,2},{7,3},{8,12},{9,13},{10,... | collective-permute-start | bytes 393224 | tf_op jit(solution)/shard_map/ppermute | solution.py:23
  13.8 16.2 %copy-start.4 = (bf16[1,128,512]{2,1,0:T(8,128)(2,1)S(1)}, bf16[1,128,512]{2,1,0:T(8,128)(2,1)}, u32[]{:S(2)}) copy-start(bf16[1,128,512]{2,1,0:T(8,128)(2,1)} %refs_0_.1) | copy-start | bytes 393220
  17.0 13.0 %collective-permute-start.3 = (bf16[1,128,512]{2,1,0:T(8,128)(2,1)S(1)}, bf16[1,128,512]{2,1,0:T(8,128)(2,1)S(1)}, u32[]{:S(2)}, u32[]{:S(2)}) collective-permute-start(bf16[1,128,512]{2,1,0:T(8,128)(2,1)S(1)} %bitcast.24), channel_id=1, source_target_pairs={{0,2},{1,3},{2,0},{3,1},{4,6},{5,7},{6,4},{7,5},{8,10},{9,11},{10,... | collective-permute-start | bytes 393224 | tf_op jit(solution)/shard_map/ppermute | solution.py:23
  19.5 5.6 %collective-permute-start.4 = (f16[144,512]{1,0:T(8,128)(2,1)S(1)}, f16[144,512]{1,0:T(8,128)(2,1)S(1)}, u32[]{:S(2)}, u32[]{:S(2)}) collective-permute-start(f16[144,512]{1,0:T(8,128)(2,1)S(1)} %convert_element_type.21), channel_id=1, source_target_pairs={{0,2},{1,3},{2,0},{3,1},{4,6},{5,7},{6,4},{7,5},{8,10},{9,11},{10,... | collective-permute-start | bytes 442376 | tf_op jit(solution)/shard_map/ppermute | solution.py:23
  25.2 13.2 %collective-permute-start.7 = (f16[2,144,512]{2,1,0:T(8,128)(2,1)S(1)}, f16[2,144,512]{2,1,0:T(8,128)(2,1)S(1)}, u32[]{:S(2)}, u32[]{:S(2)}) collective-permute-start(f16[2,144,512]{2,1,0:T(8,128)(2,1)S(1)} %pad_maximum_fusion), channel_id=1, source_target_pairs={{0,20},{1,21},{2,22},{3,23},{4,16},{5,17},{6,18},{7,19},{8,28},{9,... | collective-permute-start | bytes 884744 | tf_op jit(solution)/shard_map/ppermute | solution.py:75
  26.1 14.4 %collective-permute-start.6 = (f16[2,144,512]{2,1,0:T(8,128)(2,1)S(1)}, f16[2,144,512]{2,1,0:T(8,128)(2,1)S(1)}, u32[]{:S(2)}, u32[]{:S(2)}) collective-permute-start(f16[2,144,512]{2,1,0:T(8,128)(2,1)S(1)} %pad_maximum_fusion), channel_id=1, source_target_pairs={{0,16},{1,17},{2,18},{3,19},{4,20},{5,21},{6,22},{7,23},{8,24},{9,... | collective-permute-start | bytes 884744 | tf_op jit(solution)/shard_map/ppermute | solution.py:75
  26.9 15.5 %collective-permute-start.5 = (f16[2,144,512]{2,1,0:T(8,128)(2,1)S(1)}, f16[2,144,512]{2,1,0:T(8,128)(2,1)S(1)}, u32[]{:S(2)}, u32[]{:S(2)}) collective-permute-start(f16[2,144,512]{2,1,0:T(8,128)(2,1)S(1)} %pad_maximum_fusion), channel_id=1, source_target_pairs={{0,4},{1,5},{2,6},{3,7},{4,0},{5,1},{6,2},{7,3},{8,12},{9,13},{10,... | collective-permute-start | bytes 884744 | tf_op jit(solution)/shard_map/ppermute | solution.py:75
  28.8 9.1 %collective-permute-start.14 = (bf16[2,128,512]{2,1,0:T(8,128)(2,1)S(1)}, bf16[2,128,512]{2,1,0:T(8,128)(2,1)S(1)}, u32[]{:S(2)}, u32[]{:S(2)}) collective-permute-start(bf16[2,128,512]{2,1,0:T(8,128)(2,1)S(1)} %pad_maximum_fusion.1.refs_4_), channel_id=1, source_target_pairs={{0,2},{1,3},{2,0},{3,1},{4,6},{5,7},{6,4},{7,5},{8,10},{9,11},{10,... | collective-permute-start | bytes 786440 | tf_op jit(solution)/shard_map/ppermute | solution.py:23
  30.0 8.0 %collective-permute-start.11 = (bf16[1,128,512]{2,1,0:T(8,128)(2,1)S(1)}, bf16[1,128,512]{2,1,0:T(8,128)(2,1)S(1)}, u32[]{:S(2)}, u32[]{:S(2)}) collective-permute-start(bf16[1,128,512]{2,1,0:T(8,128)(2,1)S(1)} %copy-done.4), channel_id=1, source_target_pairs={{0,2},{1,3},{2,0},{3,1},{4,6},{5,7},{6,4},{7,5},{8,10},{9,11},{10,... | collective-permute-start | bytes 393224 | tf_op jit(solution)/shard_map/ppermute | solution.py:23
  30.9 43.8 %all-to-all-start = ((bf16[16,512,128]{2,1,0:T(8,128)(2,1)}), bf16[16,512,128]{2,1,0:T(8,128)(2,1)}, u32[]{:S(2)}, u32[]{:S(2)}) async-start(bf16[16,512,128]{2,1,0:T(8,128)(2,1)} %bitcast.27), calls=%async_computation | async-start | bytes 4194304 | tf_op jit(solution)/shard_map/all_to_all | solution.py:517
  38.0 4.5 %collective-permute-start.8 = (bf16[1,128,512]{2,1,0:T(8,128)(2,1)S(1)}, bf16[1,128,512]{2,1,0:T(8,128)(2,1)S(1)}, u32[]{:S(2)}, u32[]{:S(2)}) collective-permute-start(bf16[1,128,512]{2,1,0:T(8,128)(2,1)S(1)} %copy-done.4), channel_id=1, source_target_pairs={{0,1},{1,0},{2,3},{3,2},{4,5},{5,4},{6,7},{7,6},{8,9},{9,8},{10,11... | collective-permute-start | bytes 393224 | tf_op jit(solution)/shard_map/ppermute | solution.py:23
  38.0 5.3 %collective-permute-start.9 = (bf16[1,128,512]{2,1,0:T(8,128)(2,1)S(1)}, bf16[1,128,512]{2,1,0:T(8,128)(2,1)S(1)}, u32[]{:S(2)}, u32[]{:S(2)}) collective-permute-start(bf16[1,128,512]{2,1,0:T(8,128)(2,1)S(1)} %bitcast.25), channel_id=1, source_target_pairs={{0,1},{1,0},{2,3},{3,2},{4,5},{5,4},{6,7},{7,6},{8,9},{9,8},{10,11... | collective-permute-start | bytes 393224 | tf_op jit(solution)/shard_map/ppermute | solution.py:23
  38.5 5.6 %collective-permute-start.10 = (bf16[2,128,512]{2,1,0:T(8,128)(2,1)S(1)}, bf16[2,128,512]{2,1,0:T(8,128)(2,1)S(1)}, u32[]{:S(2)}, u32[]{:S(2)}) collective-permute-start(bf16[2,128,512]{2,1,0:T(8,128)(2,1)S(1)} %pad_maximum_fusion.1.refs_4_), channel_id=1, source_target_pairs={{0,1},{1,0},{2,3},{3,2},{4,5},{5,4},{6,7},{7,6},{8,9},{9,8},{10,11... | collective-permute-start | bytes 786440 | tf_op jit(solution)/shard_map/ppermute | solution.py:23
  40.5 2.7 %collective-permute-start.12 = (bf16[1,128,512]{2,1,0:T(8,128)(2,1)S(1)}, bf16[1,128,512]{2,1,0:T(8,128)(2,1)S(1)}, u32[]{:S(2)}, u32[]{:S(2)}) collective-permute-start(bf16[1,128,512]{2,1,0:T(8,128)(2,1)S(1)} %collective-permute-done.11.refs_6_), channel_id=1, source_target_pairs={{0,1},{1,0},{2,3},{3,2},{4,5},{5,4},{6,7},{7,6},{8,9},{9,8},{10,11... | collective-permute-start | bytes 393224 | tf_op jit(solution)/shard_map/ppermute | solution.py:23
  42.4 1.7 %collective-permute-start.15 = (bf16[2,128,512]{2,1,0:T(8,128)(2,1)S(1)}, bf16[2,128,512]{2,1,0:T(8,128)(2,1)S(1)}, u32[]{:S(2)}, u32[]{:S(2)}) collective-permute-start(bf16[2,128,512]{2,1,0:T(8,128)(2,1)S(1)} %collective-permute-done.14.refs_10_), channel_id=1, source_target_pairs={{0,1},{1,0},{2,3},{3,2},{4,5},{5,4},{6,7},{7,6},{8,9},{9,8},{10,11... | collective-permute-start | bytes 786440 | tf_op jit(solution)/shard_map/ppermute | solution.py:23
  42.4 1.7 %copy-start.3 = (bf16[1,128,4096]{2,1,0:T(8,128)(2,1)S(1)}, bf16[1,128,4096]{2,1,0:T(8,128)(2,1)}, u32[]{:S(2)}) copy-start(bf16[1,128,4096]{2,1,0:T(8,128)(2,1)} %param.8) | copy-start | bytes 3145732
  42.4 1.7 %copy-start.5 = (s32[32]{0:T(128)S(1)}, s32[32]{0:T(128)}, u32[]{:S(2)}) copy-start(s32[32]{0:T(128)} %order_ref.1) | copy-start | bytes 388
  42.5 1.6 %collective-permute-start.13 = (bf16[1,128,512]{2,1,0:T(8,128)(2,1)S(1)}, bf16[1,128,512]{2,1,0:T(8,128)(2,1)S(1)}, u32[]{:S(2)}, u32[]{:S(2)}) collective-permute-start(bf16[1,128,512]{2,1,0:T(8,128)(2,1)S(1)} %collective-permute-done.3.refs_8_), channel_id=1, source_target_pairs={{0,1},{1,0},{2,3},{3,2},{4,5},{5,4},{6,7},{7,6},{8,9},{9,8},{10,11... | collective-permute-start | bytes 393224 | tf_op jit(solution)/shard_map/ppermute | solution.py:23
  43.2 16.3 %collective-permute-start.18 = (f16[8,144,512]{2,1,0:T(8,128)(2,1)S(1)}, f16[8,144,512]{2,1,0:T(8,128)(2,1)S(1)}, u32[]{:S(2)}, u32[]{:S(2)}) collective-permute-start(f16[8,144,512]{2,1,0:T(8,128)(2,1)S(1)} %constant_dynamic-update-slice_fusion), channel_id=1, source_target_pairs={{0,1},{1,0},{2,3},{3,2},{4,5},{5,4},{6,7},{7,6},{8,9},{9,8},{10,11... | collective-permute-start | bytes 3538952 | tf_op jit(solution)/shard_map/ppermute | solution.py:23
  57.7 1.3 %collective-permute-start.16 = (f32[2,8,4,128]{3,2,1,0:T(4,128)S(1)}, f32[2,8,4,128]{3,2,1,0:T(4,128)S(1)}, u32[]{:S(2)}, u32[]{:S(2)}) collective-permute-start(f32[2,8,4,128]{3,2,1,0:T(4,128)S(1)} %shard_map.128), channel_id=1, source_target_pairs={{0,1},{1,0},{2,3},{3,2},{4,5},{5,4},{6,7},{7,6},{8,9},{9,8},{10,11... | collective-permute-start | bytes 98312 | tf_op jit(solution)/shard_map/ppermute | solution.py:23
  59.0 6.1 %collective-permute-start.17 = (f32[2,8,4,128]{3,2,1,0:T(4,128)S(1)}, f32[2,8,4,128]{3,2,1,0:T(4,128)S(1)}, u32[]{:S(2)}, u32[]{:S(2)}) collective-permute-start(f32[2,8,4,128]{3,2,1,0:T(4,128)S(1)} %add.15), channel_id=1, source_target_pairs={{0,2},{1,3},{2,0},{3,1},{4,6},{5,7},{6,4},{7,5},{8,10},{9,11},{10,... | collective-permute-start | bytes 98312 | tf_op jit(solution)/shard_map/ppermute | solution.py:23
  59.4 15.3 %copy-start.1 = (bf16[128,512]{1,0:T(8,128)(2,1)S(1)}, bf16[128,512]{1,0:T(8,128)(2,1)}, u32[]{:S(2)}) copy-start(bf16[128,512]{1,0:T(8,128)(2,1)} %get-tuple-element.39.hidden_ref) | copy-start | bytes 393220
  59.4 15.2 %copy-start.2 = (bf16[4,512]{1,0:T(4,128)(2,1)S(1)}, bf16[4,512]{1,0:T(4,128)(2,1)}, u32[]{:S(2)}) copy-start(bf16[4,512]{1,0:T(4,128)(2,1)} %output_ref.3) | copy-start | bytes 12292
  65.2 3.8 %collective-permute-start.19 = (f32[8,4,128]{2,1,0:T(4,128)S(1)}, f32[8,4,128]{2,1,0:T(4,128)S(1)}, u32[]{:S(2)}, u32[]{:S(2)}) collective-permute-start(f32[8,4,128]{2,1,0:T(4,128)S(1)} %get-tuple-element.64), channel_id=1, source_target_pairs={{0,4},{1,5},{2,6},{3,7},{4,0},{5,1},{6,2},{7,3},{8,12},{9,13},{10,... | collective-permute-start | bytes 49160 | tf_op jit(solution)/shard_map/ppermute | solution.py:23
  65.3 5.6 %collective-permute-start.21 = (f32[8,4,128]{2,1,0:T(4,128)S(1)}, f32[8,4,128]{2,1,0:T(4,128)S(1)}, u32[]{:S(2)}, u32[]{:S(2)}) collective-permute-start(f32[8,4,128]{2,1,0:T(4,128)S(1)} %get-tuple-element.65), channel_id=1, source_target_pairs={{0,12},{1,13},{2,14},{3,15},{4,8},{5,9},{6,10},{7,11},{8,4},{9,5},... | collective-permute-start | bytes 49160 | tf_op jit(solution)/shard_map/ppermute | solution.py:23
  65.9 5.0 %collective-permute-start.20 = (f32[8,4,128]{2,1,0:T(4,128)S(1)}, f32[8,4,128]{2,1,0:T(4,128)S(1)}, u32[]{:S(2)}, u32[]{:S(2)}) collective-permute-start(f32[8,4,128]{2,1,0:T(4,128)S(1)} %get-tuple-element.65), channel_id=1, source_target_pairs={{0,8},{1,9},{2,10},{3,11},{4,12},{5,13},{6,14},{7,15},{8,0},{9,1},... | collective-permute-start | bytes 49160 | tf_op jit(solution)/shard_map/ppermute | solution.py:23
  70.9 3.8 %collective-permute-start.22 = (f32[8,4,128]{2,1,0:T(4,128)S(1)}, f32[8,4,128]{2,1,0:T(4,128)S(1)}, u32[]{:S(2)}, u32[]{:S(2)}) collective-permute-start(f32[8,4,128]{2,1,0:T(4,128)S(1)} %add_add_fusion.refs_0_), channel_id=1, source_target_pairs={{0,16},{16,0},{1,17},{17,1},{2,18},{18,2},{3,19},{19,3},{4,20},{20... | collective-permute-start | bytes 49160 | tf_op jit(solution)/shard_map/ppermute | solution.py:23
  74.7 1.7 %copy-start = (f32[8,144,512]{2,1,0:T(8,128)S(1)}, f32[8,144,512]{2,1,0:T(8,128)}, u32[]{:S(2)}) copy-start(f32[8,144,512]{2,1,0:T(8,128)} %convert_element_type.23.refs_3_) | copy-start | bytes 7077892
  80.8 13.0 %collective-permute-start.23 = (f16[272,512]{1,0:T(8,128)(2,1)S(1)}, f16[272,512]{1,0:T(8,128)(2,1)S(1)}, u32[]{:S(2)}, u32[]{:S(2)}) collective-permute-start(f16[272,512]{1,0:T(8,128)(2,1)S(1)} %reduce-precision_convert_fusion.1), channel_id=1, source_target_pairs={{0,8},{1,9},{2,10},{3,11},{4,12},{5,13},{6,14},{7,15},{8,0},{9,1},... | collective-permute-start | bytes 835592 | tf_op jit(solution)/shard_map/ppermute | solution.py:23
  94.8 18.2 %all-to-all-start.1 = ((f32[32,24,128]{2,1,0:T(8,128)}), f32[32,24,128]{2,1,0:T(8,128)S(1)}, u32[]{:S(2)}, u32[]{:S(2)}) async-start(f32[32,24,128]{2,1,0:T(8,128)} %get-tuple-element.55), calls=%async_computation.1 | async-start | bytes 786432 | tf_op jit(solution)/shard_map/all_to_all | solution.py:546
  100.2 12.6 %collective-permute-start.24 = (f16[272,512]{1,0:T(8,128)(2,1)S(1)}, f16[272,512]{1,0:T(8,128)(2,1)S(1)}, u32[]{:S(2)}, u32[]{:S(2)}) collective-permute-start(f16[272,512]{1,0:T(8,128)(2,1)S(1)} %reduce-precision_convert_fusion), channel_id=1, source_target_pairs={{0,16},{16,0},{1,17},{17,1},{2,18},{18,2},{3,19},{19,3},{4,20},{20... | collective-permute-start | bytes 835592 | tf_op jit(solution)/shard_map/ppermute | solution.py:23

commit v7 on v6

--- a/solution.py
+++ b/solution.py
@@ -17,6 +17,7 @@
 PREPARE_VMEM_LIMIT = 60 * 1024 * 1024
 VMEM = pl.BlockSpec(memory_space=pltpu.VMEM)
 SMEM = pl.BlockSpec(memory_space=pltpu.SMEM)
+ANYWHERE = pl.BlockSpec(memory_space=pl.ANY)
 
 
 def swap(value, axis, mask):
@@ -305,7 +306,9 @@
 def gradient_kernel(slots, columns_ref, output_ref, hidden_ref, *refs):
     message_refs, fall_refs = refs[:2], refs[2:4]
     keep_ref, send_ref, mass_ref, small_ref = refs[4:8]
-    slope, wide, grad = refs[8:]
+    slope, wide, grad, columns, copied = refs[8:]
+    copy = pltpu.make_async_copy(columns_ref, columns, copied)
+    copy.start()
     me, part = lax.axis_index("seq"), lax.axis_index("dp") % 2
     rows = hidden_ref.shape[0]
     total = rows * slots
@@ -343,9 +346,14 @@
         first_bias = first_bias + jnp.sum(fall.reshape(rows // 8, 8, units), axis=0)
         at = slice(j * rows, (j + 1) * rows)
         slope[at, :] = fall.astype(jnp.bfloat16)
-        wide[:, at] = columns_ref[2 * ((me ^ mask) % side) + (part ^ d)]
     loss_sum = jnp.sum(squared) * (0.5 / total)
     grad_bias = jnp.sum(grad_bias, axis=1, keepdims=True)
+    copy.wait()
+    for j in range(slots):
+        d, mask = order[j // 2]
+        mask = mask + j % 2
+        at = slice(j * rows, (j + 1) * rows)
+        wide[:, at] = columns[2 * ((me ^ mask) % side) + (part ^ d)]
     grad[...] = jnp.dot(wide[...], slope[...], preferred_element_type=jnp.float32)
     share = keep_ref.shape[0]
     low = pl.multiple_of((me // side) * share, share)
@@ -383,12 +391,14 @@
             jax.ShapeDtypeStruct((KEY_VALUE_HEADS, rows), jnp.float32),
             jax.ShapeDtypeStruct((small_rows(units), 128), jnp.float32),
         ),
-        in_specs=[VMEM] * 7,
+        in_specs=[ANYWHERE] + [VMEM] * 6,
         out_specs=(VMEM,) * 4,
         scratch_shapes=[
             pltpu.VMEM((slots * rows, units), jnp.bfloat16),
             pltpu.VMEM((depth, slots * rows), jnp.bfloat16),
             pltpu.VMEM((depth, units), jnp.float32),
+            pltpu.VMEM(columns.shape, jnp.bfloat16),
+            pltpu.SemaphoreType.DMA,
         ],
         compiler_params=pltpu.CompilerParams(vmem_limit_bytes=VMEM_LIMIT),
         cost_estimate=pl.CostEstimate(

time: 115 us -> 114 us (level)
  no operation moved by 1% of the time
where the time goes in v7:
time: 114 us
  waiting for transfers between devices  44.3 us (39%)
  starting transfers between devices  34.7 us (30%)
  Pallas kernels  27.2 us (24%)
  other arithmetic  5.1 us (4%)
  local copies, waits for them, and re-layouts  1.89 us (2%)
    ppermute x22, waiting for transfers between devices, swap(): lax.ppermute(value, axis, [(i, i ^ mask) for i in range(lax.axis_size(axi...  40.4 us
    ppermute x22, starting transfers between devices, swap(): lax.ppermute(value, axis, [(i, i ^ mask) for i in range(lax.axis_size(axi...  21.6 us
    pallas_call x1, Pallas kernels, attention_mass(): pl.pallas_call(functools.partial(attention_kernel, slots), out_shape=jax....  13.6 us
    pallas_call x1, Pallas kernels, prepare(): pl.pallas_call(functools.partial(prepare_kernel, chunks), out_shape=(jax....  7.43 us
    all_to_all x1, starting transfers between devices, per_device(): message = lax.all_to_all(small, ('dp', 'seq'), 0, 0, tiled=True)  5.06 us
    all_to_all x1, starting transfers between devices, per_device(): lax.all_to_all(turned.reshape(seq, -1, rows), ('dp', 'seq'), 0, 0, tiled=...  4.44 us
    pallas_call x1, Pallas kernels, gradient(): pl.pallas_call(functools.partial(gradient_kernel, slots), out_shape=(jax....  3.93 us
    ppermute x3, waiting for transfers between devices, gather_near(): gathered.append(lax.ppermute(stacked, ('dp', 'seq'), pairs))  3.82 us
  transfers between devices with their start and end apart: 27, of which 14 were waited for; matrix products, arithmetic and copies ran while one was open for 4% of the time, Pallas kernels for 18%

profile of v7, /device:TPU:0, one launch (start us, length us, event | category | flops | bytes accessed | tf_op | source)
XLA Modules:
  0.0 114.0 jit_solution(17792166957095737802)
XLA Ops:
  0.6 5.1 %collective-permute-start.2 = (bf16[128,512]{1,0:T(8,128)(2,1)}, bf16[128,512]{1,0:T(8,128)(2,1)S(1)}, u32[]{:S(2)}, u32[]{:S(2)}) collective-permute-start(bf16[128,512]{1,0:T(8,128)(2,1)} %bitcast.21), channel_id=1, source_target_pairs={{0,12},{1,13},{2,14},{3,15},{4,8},{5,9},{6,10},{7,11},{8,4},{9,5},... | collective-permute-start | bytes 393224 | tf_op jit(solution)/shard_map/ppermute | solution.py:24
  5.8 0.6 collective-permute-start
  6.4 7.4 %shard_map.127 = (bf16[16,2,256,128]{3,2,1,0:T(8,128)(2,1)}, bf16[128,512]{1,0:T(8,128)(2,1)}, f32[144,512]{1,0:T(8,128)}) custom-call(bf16[128,8192]{1,0:T(8,128)(2,1)} %bitcast.28, bf16[8192,512]{1,0:T(8,128)(2,1)} %weight_ref.1, f32[1,512]{1,0:T(1,128)} %bitcast.32, bf16[4,512]{1,0:T(4,128)(2,1)} %output_ref.3, f32[4]{0:T(128)} %output_bias_ref.1), custom_call_target="tpu_custom_call" | custom-call | flops 1073741824 | bytes 12582912 | tf_op jit(solution)/shard_map/pallas_call | solution.py:178
  13.9 3.2 %collective-permute-done.1 = bf16[128,512]{1,0:T(8,128)(2,1)S(1)} collective-permute-done((bf16[128,512]{1,0:T(8,128)(2,1)}, bf16[128,512]{1,0:T(8,128)(2,1)S(1)}, u32[]{:S(2)}, u32[]{:S(2)}) %collective-permute-start.1) | collective-permute-done | bytes 131104 | tf_op jit(solution)/shard_map/ppermute | solution.py:24
  17.0 1.5 %collective-permute-start.3 = (bf16[1,128,512]{2,1,0:T(8,128)(2,1)S(1)}, bf16[1,128,512]{2,1,0:T(8,128)(2,1)S(1)}, u32[]{:S(2)}, u32[]{:S(2)}) collective-permute-start(bf16[1,128,512]{2,1,0:T(8,128)(2,1)S(1)} %bitcast.24), channel_id=1, source_target_pairs={{0,2},{1,3},{2,0},{3,1},{4,6},{5,7},{6,4},{7,5},{8,10},{9,11},{10,... | collective-permute-start | bytes 393224 | tf_op jit(solution)/shard_map/ppermute | solution.py:24
  18.6 1.0 convert_element_type.21
  19.5 0.6 collective-permute-start.4
  20.1 1.0 convert_bitcast_fusion
  21.1 4.1 %collective-permute-done.4 = f16[144,512]{1,0:T(8,128)(2,1)S(1)} collective-permute-done((f16[144,512]{1,0:T(8,128)(2,1)S(1)}, f16[144,512]{1,0:T(8,128)(2,1)S(1)}, u32[]{:S(2)}, u32[]{:S(2)}) %collective-permute-start.4) | collective-permute-done | bytes 147488 | tf_op jit(solution)/shard_map/ppermute | solution.py:24
  25.2 0.1 pad_maximum_fusion
  25.2 0.8 collective-permute-start.7
  26.1 0.8 collective-permute-start.6
  26.9 1.9 %collective-permute-start.5 = (f16[2,144,512]{2,1,0:T(8,128)(2,1)S(1)}, f16[2,144,512]{2,1,0:T(8,128)(2,1)S(1)}, u32[]{:S(2)}, u32[]{:S(2)}) collective-permute-start(f16[2,144,512]{2,1,0:T(8,128)(2,1)S(1)} %pad_maximum_fusion), channel_id=1, source_target_pairs={{0,4},{1,5},{2,6},{3,7},{4,0},{5,1},{6,2},{7,3},{8,12},{9,13},{10,... | collective-permute-start | bytes 884744 | tf_op jit(solution)/shard_map/ppermute | solution.py:76
  28.8 1.2 %collective-permute-start.14 = (bf16[2,128,512]{2,1,0:T(8,128)(2,1)S(1)}, bf16[2,128,512]{2,1,0:T(8,128)(2,1)S(1)}, u32[]{:S(2)}, u32[]{:S(2)}) collective-permute-start(bf16[2,128,512]{2,1,0:T(8,128)(2,1)S(1)} %pad_maximum_fusion.1.refs_4_), channel_id=1, source_target_pairs={{0,2},{1,3},{2,0},{3,1},{4,6},{5,7},{6,4},{7,5},{8,10},{9,11},{10,... | collective-permute-start | bytes 786440 | tf_op jit(solution)/shard_map/ppermute | solution.py:24
  30.0 0.9 collective-permute-start.11
  30.9 4.4 %all-to-all-start = ((bf16[16,512,128]{2,1,0:T(8,128)(2,1)}), bf16[16,512,128]{2,1,0:T(8,128)(2,1)}, u32[]{:S(2)}, u32[]{:S(2)}) async-start(bf16[16,512,128]{2,1,0:T(8,128)(2,1)} %bitcast.27), calls=%async_computation | async-start | bytes 4194304 | tf_op jit(solution)/shard_map/all_to_all | solution.py:527
  35.4 2.6 %collective-permute-done.11.refs_6_ = bf16[1,128,512]{2,1,0:T(8,128)(2,1)S(1)} collective-permute-done((bf16[1,128,512]{2,1,0:T(8,128)(2,1)S(1)}, bf16[1,128,512]{2,1,0:T(8,128)(2,1)S(1)}, u32[]{:S(2)}, u32[]{:S(2)}) %collective-permute-start.11) | collective-permute-done | bytes 131104 | tf_op jit(solution)/shard_map/ppermute | solution.py:24
  38.0 0.5 collective-permute-start.9
  38.5 1.9 %collective-permute-done.6 = f16[2,144,512]{2,1,0:T(8,128)(2,1)S(1)} collective-permute-done((f16[2,144,512]{2,1,0:T(8,128)(2,1)S(1)}, f16[2,144,512]{2,1,0:T(8,128)(2,1)S(1)}, u32[]{:S(2)}, u32[]{:S(2)}) %collective-permute-start.6) | collective-permute-done | bytes 294944 | tf_op jit(solution)/shard_map/ppermute | solution.py:76
  40.5 1.9 %collective-permute-done.5 = f16[2,144,512]{2,1,0:T(8,128)(2,1)S(1)} collective-permute-done((f16[2,144,512]{2,1,0:T(8,128)(2,1)S(1)}, f16[2,144,512]{2,1,0:T(8,128)(2,1)S(1)}, u32[]{:S(2)}, u32[]{:S(2)}) %collective-permute-start.5) | collective-permute-done | bytes 294944 | tf_op jit(solution)/shard_map/ppermute | solution.py:76
  42.5 0.6 collective-permute-start.13
  43.2 0.1 collective-permute-start.18
  43.3 0.8 collective-permute-done.13.refs_9_
  44.1 13.6 %shard_map.128 = f32[2,8,4,128]{3,2,1,0:T(4,128)S(1)} custom-call(s32[32]{0:T(128)S(1)} %copy-done.5, bf16[128,4096]{1,0:T(8,128)(2,1)S(1)} %bitcast.20, bf16[1,128,512]{2,1,0:T(8,128)(2,1)S(1)} %copy-done.4, bf16[1,128,512]{2,1,0:T(8,128)(2,1)S(1)} %collective-permute-done.8.refs_1_, bf16[1,128,512]{2,1,0:T(8,128)(2,1)S(1)} %bitcast.26, ...), custom_call_target="tpu_custom_call" | custom-call | flops 107374182400 | bytes 1048576 | tf_op jit(solution)/shard_map/pallas_call | solution.py:288
  57.7 0.4 collective-permute-start.16
  58.1 0.9 collective-permute-done.16
  59.1 0.3 convert_element_type.22.refs_2_
  59.5 1.7 %convert_element_type.23.refs_3_ = f32[8,144,512]{2,1,0:T(8,128)} convert(f16[8,144,512]{2,1,0:T(8,128)(2,1)S(1)} %collective-permute-done.18) | non-fusion elementwise | flops 589824 | bytes 3538944 | tf_op jit(solution)/shard_map/convert_element_type | solution.py:533
  61.2 3.9 %collective-permute-done.17 = f32[2,8,4,128]{3,2,1,0:T(4,128)S(1)} collective-permute-done((f32[2,8,4,128]{3,2,1,0:T(4,128)S(1)}, f32[2,8,4,128]{3,2,1,0:T(4,128)S(1)}, u32[]{:S(2)}, u32[]{:S(2)}) %collective-permute-start.17) | collective-permute-done | bytes 32800 | tf_op jit(solution)/shard_map/ppermute | solution.py:24
  65.3 0.6 collective-permute-start.21
  65.9 2.8 %collective-permute-start.20 = (f32[8,4,128]{2,1,0:T(4,128)S(1)}, f32[8,4,128]{2,1,0:T(4,128)S(1)}, u32[]{:S(2)}, u32[]{:S(2)}) collective-permute-start(f32[8,4,128]{2,1,0:T(4,128)S(1)} %get-tuple-element.65), channel_id=1, source_target_pairs={{0,8},{1,9},{2,10},{3,11},{4,12},{5,13},{6,14},{7,15},{8,0},{9,1},... | collective-permute-start | bytes 49160 | tf_op jit(solution)/shard_map/ppermute | solution.py:24
  68.7 0.2 collective-permute-done.19
  69.0 1.9 %collective-permute-done.21 = f32[8,4,128]{2,1,0:T(4,128)S(1)} collective-permute-done((f32[8,4,128]{2,1,0:T(4,128)S(1)}, f32[8,4,128]{2,1,0:T(4,128)S(1)}, u32[]{:S(2)}, u32[]{:S(2)}) %collective-permute-start.21) | collective-permute-done | bytes 16416 | tf_op jit(solution)/shard_map/ppermute | solution.py:24
  70.9 2.0 %collective-permute-start.22 = (f32[8,4,128]{2,1,0:T(4,128)S(1)}, f32[8,4,128]{2,1,0:T(4,128)S(1)}, u32[]{:S(2)}, u32[]{:S(2)}) collective-permute-start(f32[8,4,128]{2,1,0:T(4,128)S(1)} %add_add_fusion.refs_0_), channel_id=1, source_target_pairs={{0,16},{16,0},{1,17},{17,1},{2,18},{18,2},{3,19},{19,3},{4,20},{20... | collective-permute-start | bytes 49160 | tf_op jit(solution)/shard_map/ppermute | solution.py:24
  72.9 1.8 %collective-permute-done.22.refs_1_ = f32[8,4,128]{2,1,0:T(4,128)S(1)} collective-permute-done((f32[8,4,128]{2,1,0:T(4,128)S(1)}, f32[8,4,128]{2,1,0:T(4,128)S(1)}, u32[]{:S(2)}, u32[]{:S(2)}) %collective-permute-start.22) | collective-permute-done | bytes 16416 | tf_op jit(solution)/shard_map/ppermute | solution.py:24
  74.7 1.7 %copy-done = f32[8,144,512]{2,1,0:T(8,128)S(1)} copy-done((f32[8,144,512]{2,1,0:T(8,128)S(1)}, f32[8,144,512]{2,1,0:T(8,128)}, u32[]{:S(2)}) %copy-start) | copy-done | bytes 2359320
  76.4 3.9 %shard_map.129 = (f32[256,512]{1,0:T(8,128)S(1)}, f32[272,512]{1,0:T(8,128)S(1)}, f32[4,128]{1,0:T(4,128)}, f32[24,128]{1,0:T(8,128)S(1)}) custom-call(bf16[16,512,128]{2,1,0:T(8,128)(2,1)} %all-to-all-done.columns_ref, bf16[4,512]{1,0:T(4,128)(2,1)S(1)} %copy-done.2, bf16[128,512]{1,0:T(8,128)(2,1)S(1)} %copy-done.1, f32[8,4,128]{2,1,0:T(4,128)S(1)} %add_add_fusion.refs_0_, ...), custom_call_target="tpu_custom_call" | custom-call | flops 1073741824 | bytes 10485760 | tf_op jit(solution)/shard_map/pallas_call | solution.py:386
  80.3 0.3 reduce-precision_convert_fusion.1
  80.6 2.6 %collective-permute-start.23 = (f16[272,512]{1,0:T(8,128)(2,1)S(1)}, f16[272,512]{1,0:T(8,128)(2,1)S(1)}, u32[]{:S(2)}, u32[]{:S(2)}) collective-permute-start(f16[272,512]{1,0:T(8,128)(2,1)S(1)} %reduce-precision_convert_fusion.1), channel_id=1, source_target_pairs={{0,8},{1,9},{2,10},{3,11},{4,12},{5,13},{6,14},{7,15},{8,0},{9,1},... | collective-permute-start | bytes 835592 | tf_op jit(solution)/shard_map/ppermute | solution.py:24
  83.2 10.5 %collective-permute-done.23 = f16[272,512]{1,0:T(8,128)(2,1)S(1)} collective-permute-done((f16[272,512]{1,0:T(8,128)(2,1)S(1)}, f16[272,512]{1,0:T(8,128)(2,1)S(1)}, u32[]{:S(2)}, u32[]{:S(2)}) %collective-permute-start.23) | collective-permute-done | bytes 278560 | tf_op jit(solution)/shard_map/ppermute | solution.py:24
  93.7 1.0 shard_map.130
  94.6 5.1 %all-to-all-start.1 = ((f32[32,24,128]{2,1,0:T(8,128)}), f32[32,24,128]{2,1,0:T(8,128)S(1)}, u32[]{:S(2)}, u32[]{:S(2)}) async-start(f32[32,24,128]{2,1,0:T(8,128)} %get-tuple-element.55), calls=%async_computation.1 | async-start | bytes 786432 | tf_op jit(solution)/shard_map/all_to_all | solution.py:556
  99.7 0.3 reduce-precision_convert_fusion
  100.0 1.8 %collective-permute-start.24 = (f16[272,512]{1,0:T(8,128)(2,1)S(1)}, f16[272,512]{1,0:T(8,128)(2,1)S(1)}, u32[]{:S(2)}, u32[]{:S(2)}) collective-permute-start(f16[272,512]{1,0:T(8,128)(2,1)S(1)} %reduce-precision_convert_fusion), channel_id=1, source_target_pairs={{0,16},{16,0},{1,17},{17,1},{2,18},{18,2},{3,19},{19,3},{4,20},{20... | collective-permute-start | bytes 835592 | tf_op jit(solution)/shard_map/ppermute | solution.py:24
  101.8 0.3 reduce_precision.11.refs_0_
  102.1 10.5 %collective-permute-done.24 = f16[272,512]{1,0:T(8,128)(2,1)S(1)} collective-permute-done((f16[272,512]{1,0:T(8,128)(2,1)S(1)}, f16[272,512]{1,0:T(8,128)(2,1)S(1)}, u32[]{:S(2)}, u32[]{:S(2)}) %collective-permute-start.24) | collective-permute-done | bytes 278560 | tf_op jit(solution)/shard_map/ppermute | solution.py:24
  112.7 0.1 all-to-all-done.1.message_ref
  112.8 1.2 %shard_map.131 = (f32[512,512]{1,0:T(8,128)}, f32[4,512]{1,0:T(4,128)}, f32[1,512]{1,0:T(1,128)}, f32[4]{0:T(128)}, f32[1]{0:T(128)}) custom-call(f32[32,24,128]{2,1,0:T(8,128)S(1)} %all-to-all-done.1.message_ref, f32[272,512]{1,0:T(8,128)S(1)} %reduce_precision.11.refs_0_, f32[272,512]{1,0:T(8,128)S(1)} %convert_element_type.27.refs_1_), custom_call_target="tpu_custom_call" | custom-call | tf_op jit(solution)/shard_map/pallas_call | solution.py:481
  (42 shorter events, 0.7 us)
Async XLA Ops:
  0.6 13.2 %collective-permute-start.2 = (bf16[128,512]{1,0:T(8,128)(2,1)}, bf16[128,512]{1,0:T(8,128)(2,1)S(1)}, u32[]{:S(2)}, u32[]{:S(2)}) collective-permute-start(bf16[128,512]{1,0:T(8,128)(2,1)} %bitcast.21), channel_id=1, source_target_pairs={{0,12},{1,13},{2,14},{3,15},{4,8},{5,9},{6,10},{7,11},{8,4},{9,5},... | collective-permute-start | bytes 393224 | tf_op jit(solution)/shard_map/ppermute | solution.py:24
  5.7 11.3 %collective-permute-start.1 = (bf16[128,512]{1,0:T(8,128)(2,1)}, bf16[128,512]{1,0:T(8,128)(2,1)S(1)}, u32[]{:S(2)}, u32[]{:S(2)}) collective-permute-start(bf16[128,512]{1,0:T(8,128)(2,1)} %bitcast.22), channel_id=1, source_target_pairs={{0,8},{1,9},{2,10},{3,11},{4,12},{5,13},{6,14},{7,15},{8,0},{9,1},... | collective-permute-start | bytes 393224 | tf_op jit(solution)/shard_map/ppermute | solution.py:24
  5.8 11.3 %collective-permute-start = (bf16[128,512]{1,0:T(8,128)(2,1)}, bf16[128,512]{1,0:T(8,128)(2,1)S(1)}, u32[]{:S(2)}, u32[]{:S(2)}) collective-permute-start(bf16[128,512]{1,0:T(8,128)(2,1)} %bitcast.23), channel_id=1, source_target_pairs={{0,4},{1,5},{2,6},{3,7},{4,0},{5,1},{6,2},{7,3},{8,12},{9,13},{10,... | collective-permute-start | bytes 393224 | tf_op jit(solution)/shard_map/ppermute | solution.py:24
  13.8 16.2 %copy-start.4 = (bf16[1,128,512]{2,1,0:T(8,128)(2,1)S(1)}, bf16[1,128,512]{2,1,0:T(8,128)(2,1)}, u32[]{:S(2)}) copy-start(bf16[1,128,512]{2,1,0:T(8,128)(2,1)} %refs_0_.1) | copy-start | bytes 393220
  17.0 13.0 %collective-permute-start.3 = (bf16[1,128,512]{2,1,0:T(8,128)(2,1)S(1)}, bf16[1,128,512]{2,1,0:T(8,128)(2,1)S(1)}, u32[]{:S(2)}, u32[]{:S(2)}) collective-permute-start(bf16[1,128,512]{2,1,0:T(8,128)(2,1)S(1)} %bitcast.24), channel_id=1, source_target_pairs={{0,2},{1,3},{2,0},{3,1},{4,6},{5,7},{6,4},{7,5},{8,10},{9,11},{10,... | collective-permute-start | bytes 393224 | tf_op jit(solution)/shard_map/ppermute | solution.py:24
  19.5 5.6 %collective-permute-start.4 = (f16[144,512]{1,0:T(8,128)(2,1)S(1)}, f16[144,512]{1,0:T(8,128)(2,1)S(1)}, u32[]{:S(2)}, u32[]{:S(2)}) collective-permute-start(f16[144,512]{1,0:T(8,128)(2,1)S(1)} %convert_element_type.21), channel_id=1, source_target_pairs={{0,2},{1,3},{2,0},{3,1},{4,6},{5,7},{6,4},{7,5},{8,10},{9,11},{10,... | collective-permute-start | bytes 442376 | tf_op jit(solution)/shard_map/ppermute | solution.py:24
  25.2 13.2 %collective-permute-start.7 = (f16[2,144,512]{2,1,0:T(8,128)(2,1)S(1)}, f16[2,144,512]{2,1,0:T(8,128)(2,1)S(1)}, u32[]{:S(2)}, u32[]{:S(2)}) collective-permute-start(f16[2,144,512]{2,1,0:T(8,128)(2,1)S(1)} %pad_maximum_fusion), channel_id=1, source_target_pairs={{0,20},{1,21},{2,22},{3,23},{4,16},{5,17},{6,18},{7,19},{8,28},{9,... | collective-permute-start | bytes 884744 | tf_op jit(solution)/shard_map/ppermute | solution.py:76
  26.1 14.4 %collective-permute-start.6 = (f16[2,144,512]{2,1,0:T(8,128)(2,1)S(1)}, f16[2,144,512]{2,1,0:T(8,128)(2,1)S(1)}, u32[]{:S(2)}, u32[]{:S(2)}) collective-permute-start(f16[2,144,512]{2,1,0:T(8,128)(2,1)S(1)} %pad_maximum_fusion), channel_id=1, source_target_pairs={{0,16},{1,17},{2,18},{3,19},{4,20},{5,21},{6,22},{7,23},{8,24},{9,... | collective-permute-start | bytes 884744 | tf_op jit(solution)/shard_map/ppermute | solution.py:76
  26.9 15.5 %collective-permute-start.5 = (f16[2,144,512]{2,1,0:T(8,128)(2,1)S(1)}, f16[2,144,512]{2,1,0:T(8,128)(2,1)S(1)}, u32[]{:S(2)}, u32[]{:S(2)}) collective-permute-start(f16[2,144,512]{2,1,0:T(8,128)(2,1)S(1)} %pad_maximum_fusion), channel_id=1, source_target_pairs={{0,4},{1,5},{2,6},{3,7},{4,0},{5,1},{6,2},{7,3},{8,12},{9,13},{10,... | collective-permute-start | bytes 884744 | tf_op jit(solution)/shard_map/ppermute | solution.py:76
  28.8 9.1 %collective-permute-start.14 = (bf16[2,128,512]{2,1,0:T(8,128)(2,1)S(1)}, bf16[2,128,512]{2,1,0:T(8,128)(2,1)S(1)}, u32[]{:S(2)}, u32[]{:S(2)}) collective-permute-start(bf16[2,128,512]{2,1,0:T(8,128)(2,1)S(1)} %pad_maximum_fusion.1.refs_4_), channel_id=1, source_target_pairs={{0,2},{1,3},{2,0},{3,1},{4,6},{5,7},{6,4},{7,5},{8,10},{9,11},{10,... | collective-permute-start | bytes 786440 | tf_op jit(solution)/shard_map/ppermute | solution.py:24
  30.0 8.0 %collective-permute-start.11 = (bf16[1,128,512]{2,1,0:T(8,128)(2,1)S(1)}, bf16[1,128,512]{2,1,0:T(8,128)(2,1)S(1)}, u32[]{:S(2)}, u32[]{:S(2)}) collective-permute-start(bf16[1,128,512]{2,1,0:T(8,128)(2,1)S(1)} %copy-done.4), channel_id=1, source_target_pairs={{0,2},{1,3},{2,0},{3,1},{4,6},{5,7},{6,4},{7,5},{8,10},{9,11},{10,... | collective-permute-start | bytes 393224 | tf_op jit(solution)/shard_map/ppermute | solution.py:24
  30.9 43.8 %all-to-all-start = ((bf16[16,512,128]{2,1,0:T(8,128)(2,1)}), bf16[16,512,128]{2,1,0:T(8,128)(2,1)}, u32[]{:S(2)}, u32[]{:S(2)}) async-start(bf16[16,512,128]{2,1,0:T(8,128)(2,1)} %bitcast.27), calls=%async_computation | async-start | bytes 4194304 | tf_op jit(solution)/shard_map/all_to_all | solution.py:527
  38.0 4.5 %collective-permute-start.8 = (bf16[1,128,512]{2,1,0:T(8,128)(2,1)S(1)}, bf16[1,128,512]{2,1,0:T(8,128)(2,1)S(1)}, u32[]{:S(2)}, u32[]{:S(2)}) collective-permute-start(bf16[1,128,512]{2,1,0:T(8,128)(2,1)S(1)} %copy-done.4), channel_id=1, source_target_pairs={{0,1},{1,0},{2,3},{3,2},{4,5},{5,4},{6,7},{7,6},{8,9},{9,8},{10,11... | collective-permute-start | bytes 393224 | tf_op jit(solution)/shard_map/ppermute | solution.py:24
  38.0 5.3 %collective-permute-start.9 = (bf16[1,128,512]{2,1,0:T(8,128)(2,1)S(1)}, bf16[1,128,512]{2,1,0:T(8,128)(2,1)S(1)}, u32[]{:S(2)}, u32[]{:S(2)}) collective-permute-start(bf16[1,128,512]{2,1,0:T(8,128)(2,1)S(1)} %bitcast.25), channel_id=1, source_target_pairs={{0,1},{1,0},{2,3},{3,2},{4,5},{5,4},{6,7},{7,6},{8,9},{9,8},{10,11... | collective-permute-start | bytes 393224 | tf_op jit(solution)/shard_map/ppermute | solution.py:24
  38.5 5.6 %collective-permute-start.10 = (bf16[2,128,512]{2,1,0:T(8,128)(2,1)S(1)}, bf16[2,128,512]{2,1,0:T(8,128)(2,1)S(1)}, u32[]{:S(2)}, u32[]{:S(2)}) collective-permute-start(bf16[2,128,512]{2,1,0:T(8,128)(2,1)S(1)} %pad_maximum_fusion.1.refs_4_), channel_id=1, source_target_pairs={{0,1},{1,0},{2,3},{3,2},{4,5},{5,4},{6,7},{7,6},{8,9},{9,8},{10,11... | collective-permute-start | bytes 786440 | tf_op jit(solution)/shard_map/ppermute | solution.py:24
  40.5 2.7 %collective-permute-start.12 = (bf16[1,128,512]{2,1,0:T(8,128)(2,1)S(1)}, bf16[1,128,512]{2,1,0:T(8,128)(2,1)S(1)}, u32[]{:S(2)}, u32[]{:S(2)}) collective-permute-start(bf16[1,128,512]{2,1,0:T(8,128)(2,1)S(1)} %collective-permute-done.11.refs_6_), channel_id=1, source_target_pairs={{0,1},{1,0},{2,3},{3,2},{4,5},{5,4},{6,7},{7,6},{8,9},{9,8},{10,11... | collective-permute-start | bytes 393224 | tf_op jit(solution)/shard_map/ppermute | solution.py:24
  42.4 1.7 %collective-permute-start.15 = (bf16[2,128,512]{2,1,0:T(8,128)(2,1)S(1)}, bf16[2,128,512]{2,1,0:T(8,128)(2,1)S(1)}, u32[]{:S(2)}, u32[]{:S(2)}) collective-permute-start(bf16[2,128,512]{2,1,0:T(8,128)(2,1)S(1)} %collective-permute-done.14.refs_10_), channel_id=1, source_target_pairs={{0,1},{1,0},{2,3},{3,2},{4,5},{5,4},{6,7},{7,6},{8,9},{9,8},{10,11... | collective-permute-start | bytes 786440 | tf_op jit(solution)/shard_map/ppermute | solution.py:24
  42.4 1.7 %copy-start.3 = (bf16[1,128,4096]{2,1,0:T(8,128)(2,1)S(1)}, bf16[1,128,4096]{2,1,0:T(8,128)(2,1)}, u32[]{:S(2)}) copy-start(bf16[1,128,4096]{2,1,0:T(8,128)(2,1)} %param.8) | copy-start | bytes 3145732
  42.4 1.7 %copy-start.5 = (s32[32]{0:T(128)S(1)}, s32[32]{0:T(128)}, u32[]{:S(2)}) copy-start(s32[32]{0:T(128)} %order_ref.1) | copy-start | bytes 388
  42.5 1.6 %collective-permute-start.13 = (bf16[1,128,512]{2,1,0:T(8,128)(2,1)S(1)}, bf16[1,128,512]{2,1,0:T(8,128)(2,1)S(1)}, u32[]{:S(2)}, u32[]{:S(2)}) collective-permute-start(bf16[1,128,512]{2,1,0:T(8,128)(2,1)S(1)} %collective-permute-done.3.refs_8_), channel_id=1, source_target_pairs={{0,1},{1,0},{2,3},{3,2},{4,5},{5,4},{6,7},{7,6},{8,9},{9,8},{10,11... | collective-permute-start | bytes 393224 | tf_op jit(solution)/shard_map/ppermute | solution.py:24
  43.2 16.3 %collective-permute-start.18 = (f16[8,144,512]{2,1,0:T(8,128)(2,1)S(1)}, f16[8,144,512]{2,1,0:T(8,128)(2,1)S(1)}, u32[]{:S(2)}, u32[]{:S(2)}) collective-permute-start(f16[8,144,512]{2,1,0:T(8,128)(2,1)S(1)} %constant_dynamic-update-slice_fusion), channel_id=1, source_target_pairs={{0,1},{1,0},{2,3},{3,2},{4,5},{5,4},{6,7},{7,6},{8,9},{9,8},{10,11... | collective-permute-start | bytes 3538952 | tf_op jit(solution)/shard_map/ppermute | solution.py:24
  57.7 1.3 %collective-permute-start.16 = (f32[2,8,4,128]{3,2,1,0:T(4,128)S(1)}, f32[2,8,4,128]{3,2,1,0:T(4,128)S(1)}, u32[]{:S(2)}, u32[]{:S(2)}) collective-permute-start(f32[2,8,4,128]{3,2,1,0:T(4,128)S(1)} %shard_map.128), channel_id=1, source_target_pairs={{0,1},{1,0},{2,3},{3,2},{4,5},{5,4},{6,7},{7,6},{8,9},{9,8},{10,11... | collective-permute-start | bytes 98312 | tf_op jit(solution)/shard_map/ppermute | solution.py:24
  59.0 6.1 %collective-permute-start.17 = (f32[2,8,4,128]{3,2,1,0:T(4,128)S(1)}, f32[2,8,4,128]{3,2,1,0:T(4,128)S(1)}, u32[]{:S(2)}, u32[]{:S(2)}) collective-permute-start(f32[2,8,4,128]{3,2,1,0:T(4,128)S(1)} %add.15), channel_id=1, source_target_pairs={{0,2},{1,3},{2,0},{3,1},{4,6},{5,7},{6,4},{7,5},{8,10},{9,11},{10,... | collective-permute-start | bytes 98312 | tf_op jit(solution)/shard_map/ppermute | solution.py:24
  59.4 15.3 %copy-start.1 = (bf16[128,512]{1,0:T(8,128)(2,1)S(1)}, bf16[128,512]{1,0:T(8,128)(2,1)}, u32[]{:S(2)}) copy-start(bf16[128,512]{1,0:T(8,128)(2,1)} %get-tuple-element.39.hidden_ref) | copy-start | bytes 393220
  59.4 15.2 %copy-start.2 = (bf16[4,512]{1,0:T(4,128)(2,1)S(1)}, bf16[4,512]{1,0:T(4,128)(2,1)}, u32[]{:S(2)}) copy-start(bf16[4,512]{1,0:T(4,128)(2,1)} %output_ref.3) | copy-start | bytes 12292
  65.2 3.8 %collective-permute-start.19 = (f32[8,4,128]{2,1,0:T(4,128)S(1)}, f32[8,4,128]{2,1,0:T(4,128)S(1)}, u32[]{:S(2)}, u32[]{:S(2)}) collective-permute-start(f32[8,4,128]{2,1,0:T(4,128)S(1)} %get-tuple-element.64), channel_id=1, source_target_pairs={{0,4},{1,5},{2,6},{3,7},{4,0},{5,1},{6,2},{7,3},{8,12},{9,13},{10,... | collective-permute-start | bytes 49160 | tf_op jit(solution)/shard_map/ppermute | solution.py:24
  65.3 5.6 %collective-permute-start.21 = (f32[8,4,128]{2,1,0:T(4,128)S(1)}, f32[8,4,128]{2,1,0:T(4,128)S(1)}, u32[]{:S(2)}, u32[]{:S(2)}) collective-permute-start(f32[8,4,128]{2,1,0:T(4,128)S(1)} %get-tuple-element.65), channel_id=1, source_target_pairs={{0,12},{1,13},{2,14},{3,15},{4,8},{5,9},{6,10},{7,11},{8,4},{9,5},... | collective-permute-start | bytes 49160 | tf_op jit(solution)/shard_map/ppermute | solution.py:24
  65.9 5.0 %collective-permute-start.20 = (f32[8,4,128]{2,1,0:T(4,128)S(1)}, f32[8,4,128]{2,1,0:T(4,128)S(1)}, u32[]{:S(2)}, u32[]{:S(2)}) collective-permute-start(f32[8,4,128]{2,1,0:T(4,128)S(1)} %get-tuple-element.65), channel_id=1, source_target_pairs={{0,8},{1,9},{2,10},{3,11},{4,12},{5,13},{6,14},{7,15},{8,0},{9,1},... | collective-permute-start | bytes 49160 | tf_op jit(solution)/shard_map/ppermute | solution.py:24
  70.9 3.8 %collective-permute-start.22 = (f32[8,4,128]{2,1,0:T(4,128)S(1)}, f32[8,4,128]{2,1,0:T(4,128)S(1)}, u32[]{:S(2)}, u32[]{:S(2)}) collective-permute-start(f32[8,4,128]{2,1,0:T(4,128)S(1)} %add_add_fusion.refs_0_), channel_id=1, source_target_pairs={{0,16},{16,0},{1,17},{17,1},{2,18},{18,2},{3,19},{19,3},{4,20},{20... | collective-permute-start | bytes 49160 | tf_op jit(solution)/shard_map/ppermute | solution.py:24
  74.7 1.7 %copy-start = (f32[8,144,512]{2,1,0:T(8,128)S(1)}, f32[8,144,512]{2,1,0:T(8,128)}, u32[]{:S(2)}) copy-start(f32[8,144,512]{2,1,0:T(8,128)} %convert_element_type.23.refs_3_) | copy-start | bytes 7077892
  80.6 13.0 %collective-permute-start.23 = (f16[272,512]{1,0:T(8,128)(2,1)S(1)}, f16[272,512]{1,0:T(8,128)(2,1)S(1)}, u32[]{:S(2)}, u32[]{:S(2)}) collective-permute-start(f16[272,512]{1,0:T(8,128)(2,1)S(1)} %reduce-precision_convert_fusion.1), channel_id=1, source_target_pairs={{0,8},{1,9},{2,10},{3,11},{4,12},{5,13},{6,14},{7,15},{8,0},{9,1},... | collective-permute-start | bytes 835592 | tf_op jit(solution)/shard_map/ppermute | solution.py:24
  94.6 18.2 %all-to-all-start.1 = ((f32[32,24,128]{2,1,0:T(8,128)}), f32[32,24,128]{2,1,0:T(8,128)S(1)}, u32[]{:S(2)}, u32[]{:S(2)}) async-start(f32[32,24,128]{2,1,0:T(8,128)} %get-tuple-element.55), calls=%async_computation.1 | async-start | bytes 786432 | tf_op jit(solution)/shard_map/all_to_all | solution.py:556
  100.0 12.6 %collective-permute-start.24 = (f16[272,512]{1,0:T(8,128)(2,1)S(1)}, f16[272,512]{1,0:T(8,128)(2,1)S(1)}, u32[]{:S(2)}, u32[]{:S(2)}) collective-permute-start(f16[272,512]{1,0:T(8,128)(2,1)S(1)} %reduce-precision_convert_fusion), channel_id=1, source_target_pairs={{0,16},{16,0},{1,17},{17,1},{2,18},{18,2},{3,19},{19,3},{4,20},{20... | collective-permute-start | bytes 835592 | tf_op jit(solution)/shard_map/ppermute | solution.py:24
